TPU v7x, 256 devices: a whole 4x4x8 slice. The times are simulated.
256 devices in a mesh: dp: 32 (over y, x, core), mp: 8 (over z).
Axes of the slice: x: 4, y: 4, z: 8, core: 2. Of those that a mesh axis runs over, the one named last changes fastest.
Arguments:
- queries: bfloat16 [8192, 2048], P('dp', 'mp'), may hold values from -24 to 24
- context_grad: bfloat16 [8192, 2048], P('dp', 'mp'), may hold values from -6 to 6
- encoder_rows: bfloat16 [28672, 4096], P('dp'), may hold values from -60 to 60
- key_weight: bfloat16 [4096, 2048], P('dp', 'mp'), may hold values from -1 to 1
- value_weight: bfloat16 [4096, 2048], P('dp', 'mp'), may hold values from -0.09375 to 0.09375
- document_lengths: int32 [32, 4], P('dp'), may hold values from 1 to 128, 256 in all within a row
- block_bin: int32 [224], P('dp'), may hold values from 0 to 31, as said below
- block_document: int32 [224], P('dp'), may hold values from 0 to 3
Outputs:
- context: bfloat16 [8192, 2048], P('dp', 'mp')
- query_grad: bfloat16 [8192, 2048], P('dp', 'mp')
- encoder_grad: bfloat16 [28672, 4096], P('dp', 'mp')
- key_weight_grad: bfloat16 [4096, 2048], P('dp', 'mp')
- value_weight_grad: bfloat16 [4096, 2048], P('dp', 'mp')
Inputs may be any that keep to these rules, and one draw needn't show every extreme that they name: `block_bin`: each index of dp holds 7 encoder blocks and sends them to 7 different bins; one bin receives a block from every index of dp.
All inputs are finite; a program needn't handle non-finite values.
Results may differ from a plain program's by a relative error of at most 0.03.
The roundings to bfloat16 on the way count: a program that leaves them out, or rounds other values in their place, can miss the bound.
Values may be sent and summed in bfloat16 or wider, within the bound.
No kernel may reach another device: no remote copies, remote signals or barrier semaphores. Data moves between devices by JAX's collectives and lax.ppermute only.
A program may use at most 128 MiB of HBM per device.

v0:
```python
import jax
import jax.numpy as jnp
from jax import lax
from jax.sharding import PartitionSpec as P

HD = 256
BLK = 128


masked_value = -1e30


def attend_weights(scores, live_mask):
    present = jnp.any(live_mask, axis=1)[None, :, None]
    blocked = jnp.where(live_mask[None], scores, masked_value)
    highest = jnp.max(blocked, axis=2, keepdims=True)
    highest = jnp.where(present, highest, 0.0)
    raised = jnp.exp(jnp.where(live_mask[None], scores - highest, masked_value))
    totals = jnp.maximum(jnp.sum(raised, axis=2, keepdims=True), 1.0)
    return raised / totals


def token_documents(lengths, token_count):
    doc_ends = jnp.cumsum(lengths)
    positions = jnp.arange(token_count, dtype=jnp.int32)
    return jnp.sum((doc_ends[None, :] <= positions[:, None]).astype(jnp.int32), axis=1)


def per_device(
    queries,
    context_grad,
    encoder_rows,
    key_weight,
    value_weight,
    document_lengths,
    block_bin,
    block_document,
):
    bin_count = lax.axis_size("dp")
    full_key, full_value = (
        lax.all_gather(key_weight, "dp", axis=0, tiled=True),
        lax.all_gather(value_weight, "dp", axis=0, tiled=True),
    )
    head_width = full_key.shape[1]
    head_count = head_width // HD
    block_rows = BLK
    blocks_here = block_bin.shape[0]
    both_weights = jnp.concatenate([full_key, full_value], axis=1)
    projected = jnp.dot(encoder_rows, both_weights, preferred_element_type=jnp.float32).astype(
        jnp.bfloat16
    )
    route_table = (block_bin[:, None] == jnp.arange(bin_count, dtype=jnp.int32)[None, :]).astype(
        jnp.bfloat16
    )
    flat_blocks = projected.reshape(blocks_here, block_rows * 2 * head_width)
    outbound = lax.dot_general(
        route_table, flat_blocks, (((0,), (0,)), ((), ())), preferred_element_type=jnp.float32
    )
    outbound = outbound.astype(jnp.bfloat16).reshape(bin_count, block_rows, 2 * head_width)
    slot_docs = (
        lax.dot_general(
            route_table.astype(jnp.float32),
            (block_document + 1).astype(jnp.float32),
            (((0,), (0,)), ((), ())),
        )
        - 1.0
    )
    tag_rows = jnp.broadcast_to(slot_docs[:, None], (bin_count, block_rows)).astype(jnp.bfloat16)
    arrived, arrived_tags = (
        lax.all_to_all(outbound, "dp", split_axis=0, concat_axis=0, tiled=True),
        lax.all_to_all(tag_rows, "dp", split_axis=0, concat_axis=0, tiled=True),
    )
    key_slots = arrived[:, :, :head_width].reshape(bin_count * block_rows, head_count, HD)
    value_slots = arrived[:, :, head_width:].reshape(bin_count * block_rows, head_count, HD)
    token_count = queries.shape[0]
    token_docs = token_documents(document_lengths[0], token_count).astype(jnp.float32)
    live_mask = arrived_tags.reshape(-1).astype(jnp.float32)[None, :] == token_docs[:, None]
    query_heads = queries.reshape(token_count, head_count, HD)
    grad_heads = context_grad.reshape(token_count, head_count, HD)
    scaling = HD ** (-0.5)
    scores = (
        jnp.einsum("thd,shd->hts", query_heads, key_slots, preferred_element_type=jnp.float32)
        * scaling
    )
    attention = attend_weights(scores, live_mask)
    rounded = attention.astype(jnp.bfloat16)
    context = jnp.einsum(
        "hts,shd->thd", rounded, value_slots, preferred_element_type=jnp.float32
    ).astype(jnp.bfloat16)
    grad_raw = jnp.einsum(
        "thd,shd->hts", grad_heads, value_slots, preferred_element_type=jnp.float32
    )
    deltas = jnp.sum(attention * grad_raw, axis=2, keepdims=True)
    score_grad = (attention * (grad_raw - deltas) * scaling).astype(jnp.bfloat16)
    query_grad = jnp.einsum(
        "hts,shd->thd", score_grad, key_slots, preferred_element_type=jnp.float32
    ).astype(jnp.bfloat16)
    key_grad = jnp.einsum(
        "hts,thd->shd", score_grad, query_heads, preferred_element_type=jnp.float32
    ).astype(jnp.bfloat16)
    value_grad = jnp.einsum(
        "hts,thd->shd", rounded, grad_heads, preferred_element_type=jnp.float32
    ).astype(jnp.bfloat16)
    slot_grads = jnp.concatenate(
        [
            key_grad.reshape(bin_count, block_rows, head_width),
            value_grad.reshape(bin_count, block_rows, head_width),
        ],
        axis=2,
    )
    returned = lax.all_to_all(slot_grads, "dp", split_axis=0, concat_axis=0, tiled=True)
    own_grads = jnp.dot(
        route_table,
        returned.reshape(bin_count, block_rows * 2 * head_width),
        preferred_element_type=jnp.float32,
    )
    own_grads = own_grads.astype(jnp.bfloat16).reshape(encoder_rows.shape[0], 2 * head_width)
    weight_terms = lax.dot_general(
        encoder_rows, own_grads, (((0,), (0,)), ((), ())), preferred_element_type=jnp.float32
    )
    weight_sums = lax.psum_scatter(
        weight_terms.astype(jnp.bfloat16), "dp", scatter_dimension=0, tiled=True
    ).astype(jnp.float32)
    key_weight_grad = weight_sums[:, :head_width].astype(jnp.bfloat16)
    value_weight_grad = weight_sums[:, head_width:].astype(jnp.bfloat16)
    row_terms = lax.dot_general(
        own_grads, both_weights, (((1,), (1,)), ((), ())), preferred_element_type=jnp.float32
    )
    encoder_grad = lax.psum_scatter(
        row_terms.astype(jnp.bfloat16), "mp", scatter_dimension=1, tiled=True
    )
    return (
        context.reshape(token_count, head_width),
        query_grad.reshape(token_count, head_width),
        encoder_grad,
        key_weight_grad,
        value_weight_grad,
    )


def solution(mesh):
    in_specs = (
        P("dp", "mp"),
        P("dp", "mp"),
        P("dp", None),
        P("dp", "mp"),
        P("dp", "mp"),
        P("dp", None),
        P("dp"),
        P("dp"),
    )
    out_specs = (P("dp", "mp"), P("dp", "mp"), P("dp", "mp"), P("dp", "mp"), P("dp", "mp"))
    return jax.shard_map(
        per_device, mesh=mesh, in_specs=in_specs, out_specs=out_specs, check_vma=False
    )
```

profile of v0, /device:TPU:192, one launch (start us, length us, event | category | flops | bytes accessed | tf_op | source)
XLA Modules:
  0.0 455.3 jit_solution(6627151977607384738)
XLA Ops:
  10.2 7.3 %all-to-all-start.1 = ((bf16[32,1,128]{2,1,0:T(2,128)(2,1)}), bf16[32,1,128]{2,1,0:T(2,128)(2,1)S(1)}, u32[]{:S(2)}, u32[]{:S(2)}) async-start(bf16[32,1,128]{2,1,0:T(2,128)(2,1)} %broadcast_in_dim.9), calls=%async_computation.1 | async-start | bytes 32768 | tf_op jit(solution)/shard_map/all_to_all | solution.py:71
  17.6 42.7 %all-gather.3.cloned.1.call-done = bf16[4096,256]{1,0:T(8,128)(2,1)} async-done(((bf16[128,256]{1,0:T(8,128)(2,1)}), bf16[4096,256]{1,0:T(8,128)(2,1)}) %all-gather.3.cloned.1.call-update) | async-done | bytes 2097168 | tf_op jit(solution)/shard_map/all_gather | solution.py:41
  60.2 3.1 constant_dynamic-update-slice_fusion.1
  63.4 47.6 %all-gather.5.cloned.1.call-done = bf16[4096,256]{1,0:T(8,128)(2,1)} async-done(((bf16[128,256]{1,0:T(8,128)(2,1)}), bf16[4096,256]{1,0:T(8,128)(2,1)}) %all-gather.5.cloned.1.call-update) | async-done | bytes 2097168 | tf_op jit(solution)/shard_map/all_gather | solution.py:42
  111.0 3.1 constant_dynamic-update-slice_fusion
  114.0 8.9 %fusion.6 = bf16[896,512]{0,1:T(8,128)(2,1)S(1)} fusion(bf16[4096,512]{1,0:T(8,128)(2,1)} %constant_dynamic-update-slice_fusion, bf16[896,4096]{1,0:T(8,128)(2,1)} %param.10), kind=kOutput, calls=%fused_computation.21 | convolution fusion | flops 3758555136 | bytes 12451840 | tf_op jit(solution)/shard_map/dot_general | solution.py:49
  125.9 3.5 copy.36
  129.4 5.4 %all-to-all-start = ((bf16[32,128,512]{2,1,0:T(8,128)(2,1)}), bf16[32,128,512]{2,1,0:T(8,128)(2,1)}, u32[]{:S(2)}, u32[]{:S(2)}) async-start(bf16[32,128,512]{2,1,0:T(8,128)(2,1)} %bitcast.71), calls=%async_computation | async-start | bytes 8388608 | tf_op jit(solution)/shard_map/all_to_all | solution.py:70
  136.0 52.2 %all-to-all-done = bf16[32,128,512]{2,1,0:T(8,128)(2,1)} async-done(((bf16[32,128,512]{2,1,0:T(8,128)(2,1)}), bf16[32,128,512]{2,1,0:T(8,128)(2,1)}, u32[]{:S(2)}, u32[]{:S(2)}) %all-to-all-start) | async-done | bytes 4194336 | tf_op jit(solution)/shard_map/all_to_all | solution.py:70
  188.3 2.7 fusion.21
  193.3 1.4 convolution_convert_fusion.4
  194.7 1.5 multiply_reduce_fusion
  196.2 1.5 multiply_convert_fusion
  198.8 54.1 %all_to_all.16 = bf16[32,128,512]{2,1,0:T(8,128)(2,1)S(1)} all-to-all(bf16[32,128,512]{2,1,0:T(8,128)(2,1)S(1)} %pad_maximum_fusion), channel_id=1, replica_groups=mesh['dp'=32,'mp'=8] {'dp'}, dimensions={0} | all-to-all | bytes 8388608 | tf_op jit(solution)/shard_map/all_to_all | solution.py:111
  252.9 2.4 copy.37
  256.0 2.3 reshape.166
  258.3 9.9 %fusion = bf16[4096,512]{0,1:T(8,128)(2,1)} fusion(bf16[896,512]{1,0:T(8,128)(2,1)} %reshape.166, bf16[896,4096]{1,0:T(8,128)(2,1)} %param.10), kind=kOutput, calls=%fused_computation.7 | convolution fusion | flops 3760193536 | bytes 12451840 | tf_op jit(solution)/shard_map/dot_general | solution.py:118
  268.2 6.5 %copy.32 = bf16[4096,512]{1,0:T(8,128)(2,1)} copy(bf16[4096,512]{0,1:T(8,128)(2,1)} %fusion) | data formatting | bytes 8388608
  275.9 8.3 %convolution_convert_fusion.2 = bf16[896,4096]{1,0:T(8,128)(2,1)} fusion(bf16[896,512]{1,0:T(8,128)(2,1)S(1)} %copy-done.5, bf16[4096,512]{1,0:T(8,128)(2,1)} %constant_dynamic-update-slice_fusion), kind=kOutput, calls=%fused_computation.2 | convolution fusion | flops 3761766400 | bytes 12451840 | tf_op jit(solution)/shard_map/dot_general | solution.py:126
  284.2 4.5 fusion.7
  289.5 2.4 fusion.8
  292.7 70.4 %reduce-scatter.7.cloned.1.call-done = bf16[128,512]{1,0:T(8,128)(2,1)} async-done(((bf16[4096,512]{1,0:T(8,128)(2,1)}), bf16[128,512]{1,0:T(8,128)(2,1)}) %reduce-scatter.7.cloned.1.call-update) | async-done | bytes 131088
  363.1 1.5 fusion.22
  364.6 84.1 %reduce-scatter.5.cloned.1.call-done = bf16[896,512]{1,0:T(8,128)(2,1)} async-done(((bf16[896,4096]{1,0:T(8,128)(2,1)}), bf16[896,512]{1,0:T(8,128)(2,1)}) %reduce-scatter.5.cloned.1.call-update) | async-done | bytes 917520 | tf_op jit(solution)/shard_map/reduce_scatter | solution.py:129
  (46 shorter events, 14.0 us)
Async XLA Ops:
  7.2 186.2 %copy-start = (bf16[256,256]{1,0:T(8,128)(2,1)S(1)}, bf16[256,256]{1,0:T(8,128)(2,1)}, u32[]{:S(2)}) copy-start(bf16[256,256]{1,0:T(8,128)(2,1)} %param.9) | copy-start | bytes 393220
  7.2 53.1 %all-gather.3.cloned.1.call-start = ((), (), s32[]{:S(2)}) async-start(), calls=%async_computation.5 | async-start | bytes 2162688 | tf_op jit(solution)/shard_map/all_gather | solution.py:41
  7.9 103.0 %all-gather.5.cloned.1.call-start = ((), (), s32[]{:S(2)}) async-start(), calls=%async_computation.6 | async-start | bytes 2162688 | tf_op jit(solution)/shard_map/all_gather | solution.py:42
  10.2 119.2 %all-to-all-start.1 = ((bf16[32,1,128]{2,1,0:T(2,128)(2,1)}), bf16[32,1,128]{2,1,0:T(2,128)(2,1)S(1)}, u32[]{:S(2)}, u32[]{:S(2)}) async-start(bf16[32,1,128]{2,1,0:T(2,128)(2,1)} %broadcast_in_dim.9), calls=%async_computation.1 | async-start | bytes 32768 | tf_op jit(solution)/shard_map/all_to_all | solution.py:71
  114.0 10.5 %copy-start.7 = (s32[7]{0:T(128)S(1)}, s32[7]{0:T(128)}, u32[]{:S(2)}) copy-start(s32[7]{0:T(128)} %param.14) | copy-start | bytes 88
  129.4 5.6 %copy-start.8 = (s32[1,4]{1,0:T(1,128)S(1)}, s32[1,4]{1,0:T(1,128)}, u32[]{:S(2)}) copy-start(s32[1,4]{1,0:T(1,128)} %param.13) | copy-start | bytes 52
  129.4 58.8 %all-to-all-start = ((bf16[32,128,512]{2,1,0:T(8,128)(2,1)}), bf16[32,128,512]{2,1,0:T(8,128)(2,1)}, u32[]{:S(2)}, u32[]{:S(2)}) async-start(bf16[32,128,512]{2,1,0:T(8,128)(2,1)} %bitcast.71), calls=%async_computation | async-start | bytes 8388608 | tf_op jit(solution)/shard_map/all_to_all | solution.py:70
  134.8 228.3 %reduce-scatter.7.cloned.1.call-start = ((), (), s32[]{:S(2)}) async-start(), calls=%async_computation.8 | async-start | bytes 4325376
  136.0 55.0 %copy-start.6 = (bf16[256,256]{1,0:T(8,128)(2,1)S(1)}, bf16[256,256]{1,0:T(8,128)(2,1)}, u32[]{:S(2)}) copy-start(bf16[256,256]{1,0:T(8,128)(2,1)} %param.8) | copy-start | bytes 393220
  191.0 1.3 copy-start.3
  191.0 3.8 copy-start.4
  192.3 3.9 copy-start.2
  274.7 1.2 copy-start.5
  274.8 174.0 %reduce-scatter.5.cloned.1.call-start = ((), (), s32[]{:S(2)}) async-start(), calls=%async_computation.7 | async-start | bytes 8257536 | tf_op jit(solution)/shard_map/reduce_scatter | solution.py:129
  284.2 164.6 %copy-start.1 = (bf16[256,256]{1,0:T(8,128)(2,1)S(1)}, bf16[256,256]{1,0:T(8,128)(2,1)}, u32[]{:S(2)}) copy-start(bf16[256,256]{1,0:T(8,128)(2,1)} %param.9) | copy-start | bytes 393220
Sparse Core Ops, SparseCore 0:
  10.6 49.6 all-gather.2
  62.8 48.1 all-gather.4
  274.9 88.1 reduce-scatter.6
  366.2 82.4 reduce-scatter.4
where the time goes:
time: 461 us; the launch traced here: 455 us
  waiting for transfers between devices  298 us (65%)
  blocking collectives  54.1 us (12%)
  matrix products  41.5 us (9%)
  local copies, waits for them, and re-layouts  30.1 us (7%)
  between operations  14 us (3%)
  starting transfers between devices  13.3 us (3%)
    reduce_scatter x1, waiting for transfers between devices, per_device(): lax.psum_scatter(row_terms.astype(jnp.bfloat16), 'mp', scatter_dimension=...  84.1 us
    unnamed x5, waiting for transfers between devices  71.8 us
    all_to_all x1, blocking collectives, per_device(): lax.all_to_all(slot_grads, 'dp', split_axis=0, concat_axis=0, tiled=True)  54.1 us
    all_to_all x1, waiting for transfers between devices, per_device(): lax.all_to_all(outbound, 'dp', split_axis=0, concat_axis=0, tiled=True)  52.2 us
    all_gather x1, waiting for transfers between devices, per_device(): lax.all_gather(value_weight, 'dp', axis=0, tiled=True)  47.6 us
    all_gather x1, waiting for transfers between devices, per_device(): lax.all_gather(key_weight, 'dp', axis=0, tiled=True)  42.7 us
    unnamed x24, local copies, waits for them, and re-layouts  18.3 us
    dot_general x1, matrix products, per_device(): lax.dot_general(encoder_rows, own_grads, (((0,), (0,)), ((), ())), prefer...  9.88 us
  transfers between devices with their start and end apart: 6, of which 5 were waited for; matrix products, arithmetic and copies ran while one was open for 9% of the time, Pallas kernels for 0%

commit v1 on v0

--- a/solution.py
+++ b/solution.py
@@ -21,7 +21,8 @@
 
 
 def token_documents(lengths, token_count):
-    doc_ends = jnp.cumsum(lengths)
+    order = jnp.arange(lengths.shape[0], dtype=jnp.int32)
+    doc_ends = jnp.sum(jnp.where(order[None, :] <= order[:, None], lengths[None, :], 0), axis=1)
     positions = jnp.arange(token_count, dtype=jnp.int32)
     return jnp.sum((doc_ends[None, :] <= positions[:, None]).astype(jnp.int32), axis=1)
 

time: 461 us -> 461 us (level)
  no operation moved by 1% of the time
where the time goes in v1:
time: 461 us; the launch traced here: 455 us
  waiting for transfers between devices  298 us (65%)
  blocking collectives  54.1 us (12%)
  matrix products  41.5 us (9%)
  local copies, waits for them, and re-layouts  30.1 us (7%)
  between operations  14 us (3%)
  starting transfers between devices  13.3 us (3%)
    reduce_scatter x1, waiting for transfers between devices, per_device(): lax.psum_scatter(row_terms.astype(jnp.bfloat16), 'mp', scatter_dimension=...  84.1 us
    unnamed x5, waiting for transfers between devices  71.8 us
    all_to_all x1, blocking collectives, per_device(): lax.all_to_all(slot_grads, 'dp', split_axis=0, concat_axis=0, tiled=True)  54.1 us
    all_to_all x1, waiting for transfers between devices, per_device(): lax.all_to_all(outbound, 'dp', split_axis=0, concat_axis=0, tiled=True)  52.3 us
    all_gather x1, waiting for transfers between devices, per_device(): lax.all_gather(value_weight, 'dp', axis=0, tiled=True)  47.6 us
    all_gather x1, waiting for transfers between devices, per_device(): lax.all_gather(key_weight, 'dp', axis=0, tiled=True)  42.7 us
    unnamed x24, local copies, waits for them, and re-layouts  18.3 us
    dot_general x1, matrix products, per_device(): lax.dot_general(encoder_rows, own_grads, (((0,), (0,)), ((), ())), prefer...  9.88 us
  transfers between devices with their start and end apart: 6, of which 5 were waited for; matrix products, arithmetic and copies ran while one was open for 9% of the time, Pallas kernels for 0%

profile of v1, /device:TPU:192, one launch (start us, length us, event | category | flops | bytes accessed | tf_op | source)
XLA Modules:
  0.0 455.3 jit_solution(5259238090949687455)
XLA Ops:
  10.2 7.3 %all-to-all-start.1 = ((bf16[32,1,128]{2,1,0:T(2,128)(2,1)}), bf16[32,1,128]{2,1,0:T(2,128)(2,1)S(1)}, u32[]{:S(2)}, u32[]{:S(2)}) async-start(bf16[32,1,128]{2,1,0:T(2,128)(2,1)} %broadcast_in_dim.24), calls=%async_computation.1 | async-start | bytes 32768 | tf_op jit(solution)/shard_map/all_to_all | solution.py:72
  17.6 42.7 %all-gather.3.cloned.1.call-done = bf16[4096,256]{1,0:T(8,128)(2,1)} async-done(((bf16[128,256]{1,0:T(8,128)(2,1)}), bf16[4096,256]{1,0:T(8,128)(2,1)}) %all-gather.3.cloned.1.call-update) | async-done | bytes 2097168 | tf_op jit(solution)/shard_map/all_gather | solution.py:42
  60.2 3.1 constant_dynamic-update-slice_fusion.1
  63.4 47.6 %all-gather.5.cloned.1.call-done = bf16[4096,256]{1,0:T(8,128)(2,1)} async-done(((bf16[128,256]{1,0:T(8,128)(2,1)}), bf16[4096,256]{1,0:T(8,128)(2,1)}) %all-gather.5.cloned.1.call-update) | async-done | bytes 2097168 | tf_op jit(solution)/shard_map/all_gather | solution.py:43
  111.0 3.1 constant_dynamic-update-slice_fusion
  114.0 8.9 %fusion.6 = bf16[896,512]{0,1:T(8,128)(2,1)S(1)} fusion(bf16[4096,512]{1,0:T(8,128)(2,1)} %constant_dynamic-update-slice_fusion, bf16[896,4096]{1,0:T(8,128)(2,1)} %param.10), kind=kOutput, calls=%fused_computation.21 | convolution fusion | flops 3758555136 | bytes 12451840 | tf_op jit(solution)/shard_map/dot_general | solution.py:50
  125.9 3.5 copy.36
  129.4 5.4 %all-to-all-start = ((bf16[32,128,512]{2,1,0:T(8,128)(2,1)}), bf16[32,128,512]{2,1,0:T(8,128)(2,1)}, u32[]{:S(2)}, u32[]{:S(2)}) async-start(bf16[32,128,512]{2,1,0:T(8,128)(2,1)} %bitcast.70), calls=%async_computation | async-start | bytes 8388608 | tf_op jit(solution)/shard_map/all_to_all | solution.py:71
  136.0 52.3 %all-to-all-done = bf16[32,128,512]{2,1,0:T(8,128)(2,1)} async-done(((bf16[32,128,512]{2,1,0:T(8,128)(2,1)}), bf16[32,128,512]{2,1,0:T(8,128)(2,1)}, u32[]{:S(2)}, u32[]{:S(2)}) %all-to-all-start) | async-done | bytes 4194336 | tf_op jit(solution)/shard_map/all_to_all | solution.py:71
  188.3 2.7 fusion.21
  193.3 1.4 convolution_convert_fusion.4
  194.7 1.5 multiply_reduce_fusion
  196.2 1.5 multiply_convert_fusion
  198.8 54.1 %all_to_all.16 = bf16[32,128,512]{2,1,0:T(8,128)(2,1)S(1)} all-to-all(bf16[32,128,512]{2,1,0:T(8,128)(2,1)S(1)} %pad_maximum_fusion), channel_id=1, replica_groups=mesh['dp'=32,'mp'=8] {'dp'}, dimensions={0} | all-to-all | bytes 8388608 | tf_op jit(solution)/shard_map/all_to_all | solution.py:112
  252.9 2.4 copy.37
  256.0 2.3 reshape.141
  258.3 9.9 %fusion = bf16[4096,512]{0,1:T(8,128)(2,1)} fusion(bf16[896,512]{1,0:T(8,128)(2,1)} %reshape.141, bf16[896,4096]{1,0:T(8,128)(2,1)} %param.10), kind=kOutput, calls=%fused_computation.7 | convolution fusion | flops 3760193536 | bytes 12451840 | tf_op jit(solution)/shard_map/dot_general | solution.py:119
  268.2 6.5 %copy.32 = bf16[4096,512]{1,0:T(8,128)(2,1)} copy(bf16[4096,512]{0,1:T(8,128)(2,1)} %fusion) | data formatting | bytes 8388608
  275.9 8.3 %convolution_convert_fusion.2 = bf16[896,4096]{1,0:T(8,128)(2,1)} fusion(bf16[896,512]{1,0:T(8,128)(2,1)S(1)} %copy-done.5, bf16[4096,512]{1,0:T(8,128)(2,1)} %constant_dynamic-update-slice_fusion), kind=kOutput, calls=%fused_computation.2 | convolution fusion | flops 3761766400 | bytes 12451840 | tf_op jit(solution)/shard_map/dot_general | solution.py:127
  284.2 4.5 fusion.7
  289.5 2.4 fusion.8
  292.7 70.4 %reduce-scatter.7.cloned.1.call-done = bf16[128,512]{1,0:T(8,128)(2,1)} async-done(((bf16[4096,512]{1,0:T(8,128)(2,1)}), bf16[128,512]{1,0:T(8,128)(2,1)}) %reduce-scatter.7.cloned.1.call-update) | async-done | bytes 131088
  363.1 1.5 fusion.22
  364.6 84.1 %reduce-scatter.5.cloned.1.call-done = bf16[896,512]{1,0:T(8,128)(2,1)} async-done(((bf16[896,4096]{1,0:T(8,128)(2,1)}), bf16[896,512]{1,0:T(8,128)(2,1)}) %reduce-scatter.5.cloned.1.call-update) | async-done | bytes 917520 | tf_op jit(solution)/shard_map/reduce_scatter | solution.py:130
  (46 shorter events, 14.0 us)
Async XLA Ops:
  7.2 186.2 %copy-start = (bf16[256,256]{1,0:T(8,128)(2,1)S(1)}, bf16[256,256]{1,0:T(8,128)(2,1)}, u32[]{:S(2)}) copy-start(bf16[256,256]{1,0:T(8,128)(2,1)} %param.9) | copy-start | bytes 393220
  7.2 53.1 %all-gather.3.cloned.1.call-start = ((), (), s32[]{:S(2)}) async-start(), calls=%async_computation.5 | async-start | bytes 2162688 | tf_op jit(solution)/shard_map/all_gather | solution.py:42
  7.9 103.0 %all-gather.5.cloned.1.call-start = ((), (), s32[]{:S(2)}) async-start(), calls=%async_computation.6 | async-start | bytes 2162688 | tf_op jit(solution)/shard_map/all_gather | solution.py:43
  10.2 119.2 %all-to-all-start.1 = ((bf16[32,1,128]{2,1,0:T(2,128)(2,1)}), bf16[32,1,128]{2,1,0:T(2,128)(2,1)S(1)}, u32[]{:S(2)}, u32[]{:S(2)}) async-start(bf16[32,1,128]{2,1,0:T(2,128)(2,1)} %broadcast_in_dim.24), calls=%async_computation.1 | async-start | bytes 32768 | tf_op jit(solution)/shard_map/all_to_all | solution.py:72
  114.0 10.5 %copy-start.7 = (s32[7]{0:T(128)S(1)}, s32[7]{0:T(128)}, u32[]{:S(2)}) copy-start(s32[7]{0:T(128)} %param.14) | copy-start | bytes 88
  129.4 5.6 %copy-start.8 = (s32[1,4]{1,0:T(1,128)S(1)}, s32[1,4]{1,0:T(1,128)}, u32[]{:S(2)}) copy-start(s32[1,4]{1,0:T(1,128)} %param.13) | copy-start | bytes 52
  129.4 58.8 %all-to-all-start = ((bf16[32,128,512]{2,1,0:T(8,128)(2,1)}), bf16[32,128,512]{2,1,0:T(8,128)(2,1)}, u32[]{:S(2)}, u32[]{:S(2)}) async-start(bf16[32,128,512]{2,1,0:T(8,128)(2,1)} %bitcast.70), calls=%async_computation | async-start | bytes 8388608 | tf_op jit(solution)/shard_map/all_to_all | solution.py:71
  134.8 228.3 %reduce-scatter.7.cloned.1.call-start = ((), (), s32[]{:S(2)}) async-start(), calls=%async_computation.8 | async-start | bytes 4325376
  136.0 55.0 %copy-start.6 = (bf16[256,256]{1,0:T(8,128)(2,1)S(1)}, bf16[256,256]{1,0:T(8,128)(2,1)}, u32[]{:S(2)}) copy-start(bf16[256,256]{1,0:T(8,128)(2,1)} %param.8) | copy-start | bytes 393220
  191.0 1.3 copy-start.3
  191.0 3.8 copy-start.4
  192.3 3.9 copy-start.2
  274.7 1.2 copy-start.5
  274.8 174.0 %reduce-scatter.5.cloned.1.call-start = ((), (), s32[]{:S(2)}) async-start(), calls=%async_computation.7 | async-start | bytes 8257536 | tf_op jit(solution)/shard_map/reduce_scatter | solution.py:130
  284.2 164.6 %copy-start.1 = (bf16[256,256]{1,0:T(8,128)(2,1)S(1)}, bf16[256,256]{1,0:T(8,128)(2,1)}, u32[]{:S(2)}) copy-start(bf16[256,256]{1,0:T(8,128)(2,1)} %param.9) | copy-start | bytes 393220
Sparse Core Ops, SparseCore 0:
  10.6 49.6 all-gather.2
  62.8 48.1 all-gather.4
  274.9 88.1 reduce-scatter.6
  366.2 82.4 reduce-scatter.4

commit v2 on v0

v2 whole, which is shorter than its diff:
```python
import functools

import jax
import jax.numpy as jnp
from jax import lax
from jax.experimental import pallas as pl
from jax.experimental.pallas import tpu as pltpu
from jax.sharding import Mesh
from jax.sharding import PartitionSpec as P

HD = 256
BLK = 128
EBLK = 7
NDOC = 4
MASKED = -1e30
SCALE = HD ** (-0.5)
PLANE = ("y", "x")
DP = ("y", "x", "c")
bf16, f32 = jnp.bfloat16, jnp.float32
VMEM = pl.BlockSpec(memory_space=pltpu.VMEM)
SMEM = pl.BlockSpec(memory_space=pltpu.SMEM)
ANY = pl.BlockSpec(memory_space=pl.ANY)


def mul(a, b, da, db):
    return lax.dot_general(a, b, (((da,), (db,)), ((), ())), preferred_element_type=f32)


def params(**more):
    return pltpu.CompilerParams(vmem_limit_bytes=56 * 2**20, **more)


def token_range(b, bins, docs, lengths):
    j, k = bins[b], docs[b]
    first = jnp.int32(0)
    for i in range(NDOC - 1):
        first = first + jnp.where(i < k, lengths[j, i], 0)
    return first, first + lengths[j, k]


def block_scores(b, bins, docs, lengths, kv, qc):
    first, last = token_range(b, bins, docs, lengths)
    key, value = kv[b * BLK : (b + 1) * BLK, :HD], kv[b * BLK : (b + 1) * BLK, HD:]
    scores = mul(key, qc[b, :, :HD], 1, 1) * SCALE
    raw = mul(value, qc[b, :, HD:], 1, 1)
    token = lax.broadcasted_iota(jnp.int32, scores.shape, 1)
    return scores, raw, (token >= first) & (token < last)


def project_kernel(bins, docs, lengths, e, w, tokens, kv, qc, stats, acc, sems):
    step = pl.program_id(0)

    def fetch(b):
        return pltpu.make_async_copy(tokens.at[bins[b], 128:384, :], qc.at[b], sems.at[b])

    @pl.when(step == 0)
    def _():
        for b in range(EBLK):
            fetch(b).start()

    part = jnp.dot(e[...], w[...].reshape(-1, 2 * HD), preferred_element_type=f32)

    @pl.when(step == 0)
    def _():
        acc[...] = part

    @pl.when(step > 0)
    def _():
        acc[...] += part

    @pl.when(step == pl.num_programs(0) - 1)
    def _():
        kv[...] = acc[...].astype(bf16)
        stats[...] = jnp.zeros_like(stats)
        stats[7:8, :] = jnp.full((1, HD), MASKED, f32)
        stats[31:32, :] = jnp.full((1, HD), -1.0, f32)
        for b in range(EBLK):
            fetch(b).wait()
        for b in range(EBLK):
            scores, raw, live = block_scores(b, bins, docs, lengths, kv, qc)
            scores = jnp.where(live, scores, MASKED)
            top = jnp.max(scores, axis=0, keepdims=True)
            raised = jnp.where(live, jnp.exp(scores - top), 0.0)
            stats[b : b + 1, :] = top
            stats[8 + b : 9 + b, :] = jnp.sum(raised, axis=0, keepdims=True)
            stats[16 + b : 17 + b, :] = jnp.sum(raised * raw, axis=0, keepdims=True)
            stats[24 + b : 25 + b, :] = jnp.full((1, HD), bins[b].astype(f32))


def attend_kernel(bins, docs, lengths, kv, qc, stats, grads, grads_t, mine, other):
    core = lax.axis_index("c")
    mine[...] = jnp.zeros_like(mine)
    other[...] = jnp.zeros_like(other)
    tops = stats[:, 0:8, :].reshape(-1, HD)
    sums = stats[:, 8:16, :].reshape(-1, HD)
    dots = stats[:, 16:24, :].reshape(-1, HD)
    owners = stats[:, 24:32, :].reshape(-1, HD)
    for b in range(EBLK):
        scores, raw, live = block_scores(b, bins, docs, lengths, kv, qc)
        same = owners == bins[b].astype(f32)
        masked = jnp.where(same, tops, MASKED)
        top = jnp.max(masked, axis=0, keepdims=True)
        level = jnp.where(same, jnp.exp(masked - top), 0.0)
        total = jnp.maximum(jnp.sum(level * sums, axis=0, keepdims=True), 1.0)
        delta = jnp.sum(level * dots, axis=0, keepdims=True) / total
        attention = jnp.exp(jnp.where(live, scores - top, MASKED)) / total
        rounded = attention.astype(bf16)
        score_grad = (attention * (raw - delta) * SCALE).astype(bf16)
        rows = slice(b * BLK, (b + 1) * BLK)
        query, cotangent = qc[b, :, :HD], qc[b, :, HD:]
        grads[rows, :HD] = mul(score_grad, query, 1, 0).astype(bf16)
        grads[rows, HD:] = mul(rounded, cotangent, 1, 0).astype(bf16)
        grads_t[:HD, rows] = mul(query, score_grad, 0, 1).astype(bf16)
        grads_t[HD:, rows] = mul(cotangent, rounded, 0, 1).astype(bf16)
        context = mul(rounded, kv[rows, HD:], 0, 0).astype(bf16)
        query_grad = mul(score_grad, kv[rows, :HD], 0, 0).astype(bf16)
        slot = bins[b] // 2
        here = bins[b] % 2 == core

        @pl.when(here)
        def _():
            mine[slot, :, :HD] = context
            mine[slot, :, HD:] = query_grad

        @pl.when(jnp.logical_not(here))
        def _():
            other[slot, :, :HD] = context
            other[slot, :, HD:] = query_grad


def rows_kernel(grads, w, out):
    out[0] = mul(grads[...], w[...].reshape(-1, 2 * HD), 1, 1).astype(bf16)


def weights_kernel(grads_t, e, mine, other):
    core = lax.axis_index("c")
    term = jnp.dot(grads_t[...], e[...], preferred_element_type=f32).astype(bf16)
    for i in range(term.shape[1] // 256):
        even, odd = term[:, i * 256 : i * 256 + 128], term[:, i * 256 + 128 : i * 256 + 256]
        mine[i] = jnp.where(core == 0, even, odd)
        other[i] = jnp.where(core == 0, odd, even)


def shape(*dims, dtype=bf16):
    return jax.ShapeDtypeStruct(dims, dtype)


def per_device(queries, context_grad, encoder_rows, key_weight, value_weight, document_lengths, block_bin, block_document):
    rows, width = encoder_rows.shape
    tokens = queries.shape[0]
    bin_count = 32
    packed = jnp.concatenate(
        [
            jnp.concatenate([key_weight, value_weight], axis=1),
            jnp.concatenate([queries, context_grad], axis=1),
            jnp.pad(document_lengths.astype(bf16), ((0, 15), (0, 2 * HD - NDOC))),
        ],
        axis=0,
    )
    gathered = lax.all_gather(packed, DP, axis=0, tiled=False)
    lengths = gathered[:, 384, :NDOC].astype(jnp.int32)

    kv, qc, stats = pl.pallas_call(
        project_kernel,
        grid=(8,),
        in_specs=[
            SMEM,
            SMEM,
            SMEM,
            pl.BlockSpec((rows, 512), lambda k: (0, k)),
            pl.BlockSpec((4, 128, 2 * HD), lambda k: (k, 0, 0)),
            ANY,
        ],
        out_specs=[
            pl.BlockSpec((rows, 2 * HD), lambda k: (0, 0)),
            pl.BlockSpec((EBLK, tokens, 2 * HD), lambda k: (0, 0, 0)),
            pl.BlockSpec((32, HD), lambda k: (0, 0)),
        ],
        out_shape=[shape(rows, 2 * HD), shape(EBLK, tokens, 2 * HD), shape(32, HD, dtype=f32)],
        scratch_shapes=[pltpu.VMEM((rows, 2 * HD), f32), pltpu.SemaphoreType.DMA((EBLK,))],
        compiler_params=params(),
        name="project",
    )(block_bin, block_document, lengths, encoder_rows, gathered, gathered)

    all_stats = lax.all_to_all(
        jnp.broadcast_to(stats[None], (bin_count, 32, HD)), DP, split_axis=0, concat_axis=0, tiled=True
    )

    grads, grads_t, mine, other = pl.pallas_call(
        attend_kernel,
        in_specs=[SMEM, SMEM, SMEM, VMEM, VMEM, VMEM],
        out_specs=[VMEM] * 4,
        out_shape=[
            shape(rows, 2 * HD),
            shape(2 * HD, rows),
            shape(16, tokens, 2 * HD),
            shape(16, tokens, 2 * HD),
        ],
        compiler_params=params(),
        name="attend",
    )(block_bin, block_document, lengths, kv, qc, all_stats)

    def swap(v):
        return lax.ppermute(v, "c", [(0, 1), (1, 0)])

    def spread(own, arrived):
        both = (own.astype(f32) + arrived.astype(f32)).astype(bf16)
        return lax.all_to_all(both, PLANE, split_axis=0, concat_axis=0, tiled=True)

    row_terms = pl.pallas_call(
        rows_kernel,
        grid=(8,),
        in_specs=[
            pl.BlockSpec((rows, 2 * HD), lambda k: (0, 0)),
            pl.BlockSpec((4, 128, 2 * HD), lambda k: (k, 0, 0)),
        ],
        out_specs=pl.BlockSpec((1, rows, 512), lambda k: (k, 0, 0)),
        out_shape=shape(8, rows, 512),
        compiler_params=params(),
        name="row_terms",
    )(grads, gathered)
    encoder_grad = lax.psum_scatter(row_terms, "mp", scatter_dimension=0, tiled=False)

    token_sums = spread(mine, swap(other))

    mine_w, other_w = pl.pallas_call(
        weights_kernel,
        grid=(8,),
        in_specs=[
            pl.BlockSpec((2 * HD, rows), lambda k: (0, 0)),
            pl.BlockSpec((rows, 512), lambda k: (0, k)),
        ],
        out_specs=[pl.BlockSpec((2, 2 * HD, 128), lambda k: (k, 0, 0))] * 2,
        out_shape=[shape(16, 2 * HD, 128)] * 2,
        compiler_params=params(),
        name="weight_terms",
    )(grads_t, encoder_rows)
    weight_sums = spread(mine_w, swap(other_w))

    outs = jnp.sum(token_sums.astype(f32), axis=0).astype(bf16)
    weights = jnp.sum(weight_sums.astype(f32), axis=0).astype(bf16).T
    return outs[:, :HD], outs[:, HD:], encoder_grad, weights[:, :HD], weights[:, HD:]


def solution(mesh):
    fine = Mesh(mesh.devices.reshape(4, 4, 2, 8), ("y", "x", "c", "mp"))
    both, first = P(DP, "mp"), P(DP)
    return jax.shard_map(
        per_device,
        mesh=fine,
        in_specs=(both, both, P(DP, None), both, both, P(DP, None), first, first),
        out_specs=(both,) * 5,
        check_vma=False,
    )
```

time: 461 us -> 276 us (0.60)
  waiting for transfers between devices: 298 us -> 164 us
  Pallas kernels: 0 us -> 42.9 us
  matrix products: 41.5 us -> 0 us
  blocking collectives: 54.1 us -> 22.6 us
  local copies, waits for them, and re-layouts: 30.1 us -> 3.08 us
  other arithmetic: 3.83 us -> 17.5 us
    reduce_scatter x1, waiting for transfers between devices: 84.1 us -> 0.01 us  [per_device(): lax.psum_scatter(row_terms, 'mp', scatter_dimension=0, tiled=False)]
    unnamed x5 -> x2, waiting for transfers between devices: 71.8 us -> 0.03 us
    pallas_call x0 -> x4, Pallas kernels: none -> 42.9 us  [the longest x1 12.5 us: per_device(): pl.pallas_call(project_kernel, grid=(8,), in_specs=[SMEM, SMEM, SMEM, pl....]
    dot_general x12 -> x0, matrix products: 41.5 us -> none  [the longest x1 9.88 us: per_device(): lax.dot_general(encoder_rows, own_grads, (((0,), (0,)), ((), ())), prefer...]
    all_to_all x2, waiting for transfers between devices: 52.2 us -> 88.8 us  [spread(): return lax.all_to_all(both, PLANE, split_axis=0, concat_axis=0, tiled=True)]
    all_to_all x1, blocking collectives: 54.1 us -> 22.6 us  [per_device(): lax.all_to_all(jnp.broadcast_to(stats[None], (bin_count, 32, HD)), DP, sp...]
    all_gather x2 -> x1, waiting for transfers between devices: 90.3 us -> 71.2 us  [per_device(): gathered = lax.all_gather(packed, DP, axis=0, tiled=False)]
    unnamed x24 -> x2, local copies, waits for them, and re-layouts: 18.3 us -> 1.48 us
  transfers between devices with their start and end apart: 6 -> 6, of which waited for: 5 -> 4; matrix products, arithmetic and copies ran while one was open for 9% -> 6% of each run, Pallas kernels for 0% -> 4%
where the time goes in v2:
time: 276 us; the launch traced here: 273 us
  waiting for transfers between devices  164 us (59%)
  Pallas kernels  42.9 us (16%)
  blocking collectives  22.6 us (8%)
  other arithmetic  17.5 us (6%)
  between operations  14.1 us (5%)
  starting transfers between devices  8.93 us (3%)
  local copies, waits for them, and re-layouts  3.08 us (1%)
    all_to_all x2, waiting for transfers between devices, spread(): return lax.all_to_all(both, PLANE, split_axis=0, concat_axis=0, tiled=True)  88.8 us
    all_gather x1, waiting for transfers between devices, per_device(): gathered = lax.all_gather(packed, DP, axis=0, tiled=False)  71.2 us
    all_to_all x1, blocking collectives, per_device(): lax.all_to_all(jnp.broadcast_to(stats[None], (bin_count, 32, HD)), DP, sp...  22.6 us
    pallas_call x1, Pallas kernels, per_device(): pl.pallas_call(project_kernel, grid=(8,), in_specs=[SMEM, SMEM, SMEM, pl....  12.5 us
    convert_element_type x2, other arithmetic, spread(): both = (own.astype(f32) + arrived.astype(f32)).astype(bf16)  10.4 us
    pallas_call x1, Pallas kernels, per_device(): pl.pallas_call(attend_kernel, in_specs=[SMEM, SMEM, SMEM, VMEM, VMEM, VME...  10.3 us
    pallas_call x1, Pallas kernels, per_device(): pl.pallas_call(weights_kernel, grid=(8,), in_specs=[pl.BlockSpec((2 * HD,...  10.2 us
    pallas_call x1, Pallas kernels, per_device(): pl.pallas_call(rows_kernel, grid=(8,), in_specs=[pl.BlockSpec((rows, 2 *...  9.9 us
  transfers between devices with their start and end apart: 6, of which 4 were waited for; matrix products, arithmetic and copies ran while one was open for 6% of the time, Pallas kernels for 4%

profile of v2, /device:TPU:192, one launch (start us, length us, event | category | flops | bytes accessed | tf_op | source)
XLA Modules:
  0.0 273.2 jit_solution(5017753420692728218)
XLA Ops:
  7.2 0.7 convert_element_type.32
  7.9 1.8 fusion.1
  9.7 71.2 %all-gather.3.cloned.1.call-done = bf16[12800,512]{1,0:T(8,128)(2,1)} async-done(((bf16[400,512]{1,0:T(8,128)(2,1)}), bf16[12800,512]{1,0:T(8,128)(2,1)}) %all-gather.3.cloned.1.call-update) | async-done | bytes 13107216 | tf_op jit(solution)/shard_map/all_gather | solution.py:160
  81.0 1.5 slice_convert_fusion
  82.4 12.5 %project.1 = (bf16[896,512]{1,0:T(8,128)(2,1)}, bf16[7,256,512]{2,1,0:T(8,128)(2,1)}, f32[32,256]{1,0:T(8,128)}) custom-call(s32[7]{0:T(128)} %bins.3, s32[7]{0:T(128)} %docs.3, s32[32,4]{1,0:T(8,128)} %bitcast.9, bf16[896,4096]{1,0:T(8,128)(2,1)} %e.3, bf16[32,400,512]{2,1,0:T(8,128)(2,1)} %bitcast.5, bf16[32,400,512]{2,1,0:T(8,128)(2,1)} %bitcast.6), custom_call_target="tpu_custom_call" | custom-call | tf_op jit(solution)/shard_map/project/pallas_call | solution.py:163
  95.0 0.9 broadcast_in_dim.2
  95.8 22.6 %all_to_all.15.stats = f32[32,32,256]{2,1,0:T(8,128)} all-to-all(f32[32,32,256]{2,1,0:T(8,128)S(1)} %broadcast_in_dim.2), channel_id=1, replica_groups=mesh['y'=4,'x'=4,'c'=2,'mp'=8] {'y','x','c'}, dimensions={0} | all-to-all | bytes 2097152 | tf_op jit(solution)/shard_map/all_to_all | solution.py:185
  118.5 10.3 %attend.1 = (bf16[896,512]{1,0:T(8,128)(2,1)}, bf16[512,896]{1,0:T(8,128)(2,1)}, bf16[16,256,512]{2,1,0:T(8,128)(2,1)}, bf16[16,256,512]{2,1,0:T(8,128)(2,1)}) custom-call(s32[7]{0:T(128)} %bins.3, s32[7]{0:T(128)} %docs.3, s32[32,4]{1,0:T(8,128)} %bitcast.10, bf16[896,512]{1,0:T(8,128)(2,1)} %get-tuple-element.14.kv, ...), custom_call_target="tpu_custom_call" | custom-call | tf_op jit(solution)/shard_map/attend/pallas_call | solution.py:189
  128.8 9.9 %row_terms.1 = bf16[8,896,512]{2,1,0:T(8,128)(2,1)} custom-call(bf16[896,512]{1,0:T(8,128)(2,1)} %get-tuple-element.19.grads, bf16[32,400,512]{2,1,0:T(8,128)(2,1)} %bitcast.7), custom_call_target="tpu_custom_call" | custom-call | tf_op jit(solution)/shard_map/row_terms/pallas_call | solution.py:210
  138.7 0.2 collective-permute-start
  138.9 10.2 %weight_terms.1 = (bf16[16,512,128]{2,1,0:T(8,128)(2,1)}, bf16[16,512,128]{2,1,0:T(8,128)(2,1)}) custom-call(bf16[512,896]{1,0:T(8,128)(2,1)} %get-tuple-element.20.grads_t, bf16[896,4096]{1,0:T(8,128)(2,1)} %e.3), custom_call_target="tpu_custom_call" | custom-call | tf_op jit(solution)/shard_map/weight_terms/pallas_call | solution.py:226
  149.1 0.4 collective-permute-start.1
  149.5 4.0 %collective-permute-done.1 = bf16[16,512,128]{2,1,0:T(8,128)(2,1)S(1)} collective-permute-done((bf16[16,512,128]{2,1,0:T(8,128)(2,1)}, bf16[16,512,128]{2,1,0:T(8,128)(2,1)S(1)}, u32[]{:S(2)}, u32[]{:S(2)}) %collective-permute-start.1) | collective-permute-done | bytes 2097184 | tf_op jit(solution)/shard_map/ppermute | solution.py:204
  153.5 3.5 %add_convert_fusion.1 = bf16[16,512,128]{2,1,0:T(8,128)(2,1)} fusion(bf16[16,512,128]{2,1,0:T(8,128)(2,1)S(1)} %collective-permute-done.1, bf16[16,512,128]{2,1,0:T(8,128)(2,1)} %get-tuple-element.21), kind=kLoop, calls=%fused_computation.1 | loop fusion | flops 4194304 | bytes 6291456 | tf_op jit(solution)/shard_map/convert_element_type | solution.py:207
  157.0 3.7 %all-to-all-start.2 = ((bf16[16,512,128]{2,1,0:T(8,128)(2,1)}), bf16[16,512,128]{2,1,0:T(8,128)(2,1)S(1)}, u32[]{:S(2)}, u32[]{:S(2)}) async-start(bf16[16,512,128]{2,1,0:T(8,128)(2,1)} %add_convert_fusion.1), calls=%async_computation.3 | async-start | bytes 4194304 | tf_op jit(solution)/shard_map/all_to_all | solution.py:208
  160.7 6.9 %add_convert_fusion = bf16[16,256,512]{2,1,0:T(8,128)(2,1)} fusion(bf16[16,256,512]{2,1,0:T(8,128)(2,1)} %collective-permute-done, bf16[16,256,512]{2,1,0:T(8,128)(2,1)} %get-tuple-element.17), kind=kLoop, calls=%fused_computation | loop fusion | flops 8388608 | bytes 12582912 | tf_op jit(solution)/shard_map/convert_element_type | solution.py:207
  167.7 27.4 %all-to-all-done.2 = bf16[16,512,128]{2,1,0:T(8,128)(2,1)S(1)} async-done(((bf16[16,512,128]{2,1,0:T(8,128)(2,1)}), bf16[16,512,128]{2,1,0:T(8,128)(2,1)S(1)}, u32[]{:S(2)}, u32[]{:S(2)}) %all-to-all-start.2) | async-done | bytes 2097184 | tf_op jit(solution)/shard_map/all_to_all | solution.py:208
  195.1 4.5 %all-to-all-start.1 = ((bf16[16,256,512]{2,1,0:T(8,128)(2,1)}), bf16[16,256,512]{2,1,0:T(8,128)(2,1)}, u32[]{:S(2)}, u32[]{:S(2)}) async-start(bf16[16,256,512]{2,1,0:T(8,128)(2,1)} %add_convert_fusion), calls=%async_computation.1 | async-start | bytes 8388608 | tf_op jit(solution)/shard_map/all_to_all | solution.py:208
  199.6 0.3 reduce_sum.25
  199.9 0.7 copy.24
  200.7 0.7 copy.25
  201.4 61.3 %all-to-all-done.1 = bf16[16,256,512]{2,1,0:T(8,128)(2,1)} async-done(((bf16[16,256,512]{2,1,0:T(8,128)(2,1)}), bf16[16,256,512]{2,1,0:T(8,128)(2,1)}, u32[]{:S(2)}, u32[]{:S(2)}) %all-to-all-start.1) | async-done | bytes 4194336 | tf_op jit(solution)/shard_map/all_to_all | solution.py:208
  262.8 2.8 %reduce_sum.24 = bf16[256,512]{1,0:T(8,128)(2,1)S(1)} reduce(bf16[16,256,512]{2,1,0:T(8,128)(2,1)} %all-to-all-done.1, bf16[]{:T(256)} %constant.5.clone.1), dimensions={0}, to_apply=%region_0.1 | reduce | flops 1966080 | bytes 4456450 | tf_op jit(solution)/shard_map/reduce_sum | solution.py:240
  265.6 0.7 fusion.2
  (7 shorter events, 0.1 us)
Async XLA Ops:
  7.2 73.8 %all-gather.3.cloned.1.call-start = ((), (), s32[]{:S(2)}) async-start(), calls=%async_computation.5 | async-start | bytes 13516800 | tf_op jit(solution)/shard_map/all_gather | solution.py:160
  9.7 256.7 %reduce-scatter.2.cloned.1.call-start = ((), (), s32[]{:S(2)}) async-start(), calls=%async_computation.4 | async-start | bytes 8257536 | tf_op jit(solution)/shard_map/reduce_scatter | solution.py:222
  138.7 22.0 %collective-permute-start = (bf16[16,256,512]{2,1,0:T(8,128)(2,1)}, bf16[16,256,512]{2,1,0:T(8,128)(2,1)}, u32[]{:S(2)}, u32[]{:S(2)}) collective-permute-start(bf16[16,256,512]{2,1,0:T(8,128)(2,1)} %get-tuple-element.18), channel_id=1, source_target_pairs={{0,8},{8,0},{1,9},{9,1},{2,10},{10,2},{3,11},{11,3},{4,12},{12,4},... | collective-permute-start | bytes 12582920 | tf_op jit(solution)/shard_map/ppermute | solution.py:204
  149.1 4.4 %collective-permute-start.1 = (bf16[16,512,128]{2,1,0:T(8,128)(2,1)}, bf16[16,512,128]{2,1,0:T(8,128)(2,1)S(1)}, u32[]{:S(2)}, u32[]{:S(2)}) collective-permute-start(bf16[16,512,128]{2,1,0:T(8,128)(2,1)} %get-tuple-element.22), channel_id=1, source_target_pairs={{0,8},{8,0},{1,9},{9,1},{2,10},{10,2},{3,11},{11,3},{4,12},{12,4},... | collective-permute-start | bytes 6291464 | tf_op jit(solution)/shard_map/ppermute | solution.py:204
  157.0 38.1 %all-to-all-start.2 = ((bf16[16,512,128]{2,1,0:T(8,128)(2,1)}), bf16[16,512,128]{2,1,0:T(8,128)(2,1)S(1)}, u32[]{:S(2)}, u32[]{:S(2)}) async-start(bf16[16,512,128]{2,1,0:T(8,128)(2,1)} %add_convert_fusion.1), calls=%async_computation.3 | async-start | bytes 4194304 | tf_op jit(solution)/shard_map/all_to_all | solution.py:208
  195.1 67.7 %all-to-all-start.1 = ((bf16[16,256,512]{2,1,0:T(8,128)(2,1)}), bf16[16,256,512]{2,1,0:T(8,128)(2,1)}, u32[]{:S(2)}, u32[]{:S(2)}) async-start(bf16[16,256,512]{2,1,0:T(8,128)(2,1)} %add_convert_fusion), calls=%async_computation.1 | async-start | bytes 8388608 | tf_op jit(solution)/shard_map/all_to_all | solution.py:208
Sparse Core Ops, SparseCore 0:
  11.1 69.7 all-gather.2
  138.8 80.8 reduce-scatter.1

commit v3 on v2

v3 whole, which is shorter than its diff:
```python
import jax
import jax.numpy as jnp
from jax import lax
from jax.experimental import pallas as pl
from jax.experimental.pallas import tpu as pltpu
from jax.sharding import Mesh
from jax.sharding import PartitionSpec as P

HD = 256
BLK = 128
EBLK = 7
NDOC = 4
WIN = 128
BINS = 32
MASKED = -1e30
SCALE = HD ** (-0.5)
PLANE = ("y", "x")
DP = ("y", "x", "c")
bf16, f32 = jnp.bfloat16, jnp.float32
VMEM = pl.BlockSpec(memory_space=pltpu.VMEM)
SMEM = pl.BlockSpec(memory_space=pltpu.SMEM)
COST = pl.CostEstimate(flops=3758096384, bytes_accessed=16 * 2**20, transcendentals=0)
ANY = pl.BlockSpec(memory_space=pl.ANY)


def mul(a, b, da, db):
    return lax.dot_general(a, b, (((da,), (db,)), ((), ())), preferred_element_type=f32)


def params(**more):
    return pltpu.CompilerParams(vmem_limit_bytes=56 * 2**20, **more)


def token_range(b, bins, docs, lengths):
    j, k = bins[b], docs[b]
    first = jnp.int32(0)
    for i in range(NDOC - 1):
        first = first + jnp.where(i < k, lengths[j, i], 0)
    return first, first + lengths[j, k]


def to_window(row, first):
    return pltpu.roll(row, 2 * WIN - first, 1)[:, :WIN]


def from_window(row, first):
    return pltpu.roll(jnp.concatenate([row, jnp.zeros_like(row)], axis=1), first, 1)


def block_scores(b, bins, docs, lengths, kv, qc):
    first, last = token_range(b, bins, docs, lengths)
    key, value = kv[b * BLK : (b + 1) * BLK, :HD], kv[b * BLK : (b + 1) * BLK, HD:]
    scores = mul(key, qc[b, :, :HD], 1, 1) * SCALE
    raw = mul(value, qc[b, :, HD:], 1, 1)
    token = lax.broadcasted_iota(jnp.int32, scores.shape, 1)
    return scores, raw, (token >= first) & (token < last), first


def project_kernel(bins, docs, lengths, e, w, tokens, kv, qc, stats, acc, sems):
    step = pl.program_id(0)

    def fetch(b):
        return pltpu.make_async_copy(tokens.at[bins[b], 128:384, :], qc.at[b], sems.at[b])

    @pl.when(step == 0)
    def _():
        for b in range(EBLK):
            fetch(b).start()

    part = jnp.dot(e[...], w[...].reshape(-1, 2 * HD), preferred_element_type=f32)

    @pl.when(step == 0)
    def _():
        acc[...] = part

    @pl.when(step > 0)
    def _():
        acc[...] += part

    @pl.when(step == pl.num_programs(0) - 1)
    def _():
        kv[...] = acc[...].astype(bf16)
        stats[...] = jnp.zeros_like(stats)
        for b in range(EBLK):
            fetch(b).wait()
        for b in range(EBLK):
            scores, raw, live, first = block_scores(b, bins, docs, lengths, kv, qc)
            scores = jnp.where(live, scores, MASKED)
            top = jnp.max(scores, axis=0, keepdims=True)
            raised = jnp.where(live, jnp.exp(scores - top), 0.0)
            stats[b : b + 1, :] = to_window(top, first)
            stats[8 + b : 9 + b, :] = to_window(jnp.sum(raised, axis=0, keepdims=True), first)
            stats[16 + b : 17 + b, :] = to_window(jnp.sum(raised * raw, axis=0, keepdims=True), first)


def attend_kernel(bins, docs, lengths, kv, qc, stats, ids, grads, grads_t, mine, other, zero, made, sems):
    core = lax.axis_index("c")

    def send(source, j, do):
        here = lax.rem(j, 2) == core

        @pl.when(here)
        def _():
            do(pltpu.make_async_copy(source, mine.at[lax.div(j, 2)], sems.at[j]))

        @pl.when(jnp.logical_not(here))
        def _():
            do(pltpu.make_async_copy(source, other.at[lax.div(j, 2)], sems.at[j]))

    zero[...] = jnp.zeros_like(zero)

    def clear(j, carry):
        used = bins[0] == j
        for b in range(1, EBLK):
            used = used | (bins[b] == j)

        @pl.when(jnp.logical_not(used))
        def _():
            send(zero, j, lambda copy: copy.start())

        return carry

    lax.fori_loop(0, BINS, clear, 0)

    tops = stats[:, 0:8, :].reshape(-1, WIN)
    sums = stats[:, 8:16, :].reshape(-1, WIN)
    dots = stats[:, 16:24, :].reshape(-1, WIN)
    owners = ids[...].reshape(-1, WIN)
    for b in range(EBLK):
        scores, raw, live, first = block_scores(b, bins, docs, lengths, kv, qc)
        same = owners == (bins[b] * NDOC + docs[b]).astype(f32)
        masked = jnp.where(same, tops, MASKED)
        top = jnp.max(masked, axis=0, keepdims=True)
        level = jnp.where(same, jnp.exp(masked - top), 0.0)
        total = jnp.maximum(jnp.sum(level * sums, axis=0, keepdims=True), 1.0)
        delta = jnp.sum(level * dots, axis=0, keepdims=True) / total
        top, delta = from_window(top, first), from_window(delta, first)
        total = jnp.maximum(from_window(total, first), 1.0)
        attention = jnp.exp(jnp.where(live, scores - top, MASKED)) / total
        rounded = attention.astype(bf16)
        score_grad = (attention * (raw - delta) * SCALE).astype(bf16)
        rows = slice(b * BLK, (b + 1) * BLK)
        query, cotangent = qc[b, :, :HD], qc[b, :, HD:]
        made[b, :, :HD] = mul(rounded, kv[rows, HD:], 0, 0).astype(bf16)
        made[b, :, HD:] = mul(score_grad, kv[rows, :HD], 0, 0).astype(bf16)
        send(made.at[b], bins[b], lambda copy: copy.start())
        grads[rows, :HD] = mul(score_grad, query, 1, 0).astype(bf16)
        grads[rows, HD:] = mul(rounded, cotangent, 1, 0).astype(bf16)
        grads_t[:HD, rows] = mul(query, score_grad, 0, 1).astype(bf16)
        grads_t[HD:, rows] = mul(cotangent, rounded, 0, 1).astype(bf16)

    def finish(j, carry):
        send(zero, j, lambda copy: copy.wait())
        return carry

    lax.fori_loop(0, BINS, finish, 0)


def rows_kernel(grads, w, out):
    terms = mul(grads[...], w[...].reshape(-1, 2 * HD), 1, 1).astype(bf16)
    for i in range(out.shape[0]):
        out[i] = terms[:, i * 512 : (i + 1) * 512]


def weights_kernel(grads_t, e, mine, other):
    core = lax.axis_index("c")
    term = jnp.dot(grads_t[...], e[...], preferred_element_type=f32).astype(bf16)
    for i in range(term.shape[1] // 256):
        even, odd = term[:, i * 256 : i * 256 + 128], term[:, i * 256 + 128 : i * 256 + 256]
        mine[i] = jnp.where(core == 0, even, odd)
        other[i] = jnp.where(core == 0, odd, even)


def shape(*dims, dtype=bf16):
    return jax.ShapeDtypeStruct(dims, dtype)


def per_device(queries, context_grad, encoder_rows, key_weight, value_weight, document_lengths, block_bin, block_document):
    rows, width = encoder_rows.shape
    tokens = queries.shape[0]
    packed = jnp.concatenate(
        [
            jnp.concatenate([key_weight, value_weight], axis=1),
            jnp.concatenate([queries, context_grad], axis=1),
        ],
        axis=0,
    )
    gathered = lax.all_gather(packed, DP, axis=0, tiled=False)

    def share(v):
        spread_out = jnp.broadcast_to(v[None], (BINS, *v.shape))
        return lax.all_to_all(spread_out, DP, split_axis=0, concat_axis=0, tiled=True)

    facts = jnp.concatenate([document_lengths[0], block_bin * NDOC + block_document, jnp.full((1,), -1, jnp.int32)])
    facts = share(facts[None, :])[:, 0, :]
    lengths = facts[:, :NDOC]
    ids = jnp.broadcast_to(facts[:, NDOC:, None].astype(f32), (BINS, 8, WIN))

    kv, qc, stats = pl.pallas_call(
        project_kernel,
        grid=(4,),
        in_specs=[
            SMEM,
            SMEM,
            SMEM,
            pl.BlockSpec((rows, 1024), lambda k: (0, k)),
            pl.BlockSpec((8, 128, 2 * HD), lambda k: (k, 0, 0)),
            ANY,
        ],
        out_specs=[
            pl.BlockSpec((rows, 2 * HD), lambda k: (0, 0)),
            pl.BlockSpec((EBLK, tokens, 2 * HD), lambda k: (0, 0, 0)),
            pl.BlockSpec((24, WIN), lambda k: (0, 0)),
        ],
        out_shape=[shape(rows, 2 * HD), shape(EBLK, tokens, 2 * HD), shape(24, WIN, dtype=f32)],
        scratch_shapes=[pltpu.VMEM((rows, 2 * HD), f32), pltpu.SemaphoreType.DMA((EBLK,))],
        compiler_params=params(),
        name="project",
    )(block_bin, block_document, lengths, encoder_rows, gathered, gathered)

    all_stats = share(stats)

    grads, grads_t, mine, other = pl.pallas_call(
        attend_kernel,
        in_specs=[SMEM, SMEM, SMEM, VMEM, VMEM, VMEM, VMEM],
        out_specs=[VMEM, VMEM, ANY, ANY],
        out_shape=[
            shape(rows, 2 * HD),
            shape(2 * HD, rows),
            shape(16, tokens, 2 * HD),
            shape(16, tokens, 2 * HD),
        ],
        scratch_shapes=[
            pltpu.VMEM((tokens, 2 * HD), bf16),
            pltpu.VMEM((EBLK, tokens, 2 * HD), bf16),
            pltpu.SemaphoreType.DMA((BINS,)),
        ],
        compiler_params=params(),
        name="attend",
    )(block_bin, block_document, lengths, kv, qc, all_stats, ids)

    def swap(v):
        return lax.ppermute(v, "c", [(0, 1), (1, 0)])

    def spread(v):
        return lax.all_to_all(v, PLANE, split_axis=0, concat_axis=0, tiled=True)

    def add(a, b):
        return (a.astype(f32) + b.astype(f32)).astype(bf16)

    arrived = swap(other)

    row_terms = pl.pallas_call(
        rows_kernel,
        grid=(4,),
        in_specs=[
            pl.BlockSpec((rows, 2 * HD), lambda k: (0, 0)),
            pl.BlockSpec((8, 128, 2 * HD), lambda k: (k, 0, 0)),
        ],
        out_specs=pl.BlockSpec((2, rows, 512), lambda k: (k, 0, 0)),
        out_shape=shape(8, rows, 512),
        compiler_params=params(),
        cost_estimate=COST,
        name="row_terms",
    )(grads, gathered)
    encoder_grad = lax.psum_scatter(row_terms, "mp", scatter_dimension=0, tiled=False)

    pair_sums = add(mine, arrived)
    pair_sums, grads_t = lax.optimization_barrier((pair_sums, grads_t))
    token_sums = spread(pair_sums)

    mine_w, other_w = pl.pallas_call(
        weights_kernel,
        grid=(4,),
        in_specs=[
            pl.BlockSpec((2 * HD, rows), lambda k: (0, 0)),
            pl.BlockSpec((rows, 1024), lambda k: (0, k)),
        ],
        out_specs=[pl.BlockSpec((4, 2 * HD, 128), lambda k: (k, 0, 0))] * 2,
        out_shape=[shape(16, 2 * HD, 128)] * 2,
        compiler_params=params(),
        cost_estimate=COST,
        name="weight_terms",
    )(grads_t, encoder_rows)
    weight_sums = spread(add(mine_w, swap(other_w)))

    outs = jnp.sum(token_sums.astype(f32), axis=0).astype(bf16)
    weights = jnp.sum(weight_sums.astype(f32), axis=0).astype(bf16).T
    return outs[:, :HD], outs[:, HD:], encoder_grad, weights[:, :HD], weights[:, HD:]


def solution(mesh):
    fine = Mesh(mesh.devices.reshape(4, 4, 2, 8), ("y", "x", "c", "mp"))
    both, first = P(DP, "mp"), P(DP)
    return jax.shard_map(
        per_device,
        mesh=fine,
        in_specs=(both, both, P(DP, None), both, both, P(DP, None), first, first),
        out_specs=(both,) * 5,
        check_vma=False,
    )
```

time: 276 us -> 254 us (0.920)
  waiting for transfers between devices: 164 us -> 151 us
  blocking collectives: 22.6 us -> 14.4 us
  Pallas kernels: 42.9 us -> 34.7 us
  starting transfers between devices: 8.93 us -> 15.3 us
    all_gather x1, waiting for transfers between devices: 71.2 us -> 55 us  [per_device(): gathered = lax.all_gather(packed, DP, axis=0, tiled=False)]
    all_to_all x1, blocking collectives: 22.6 us -> 14.4 us  [share(): lax.all_to_all(spread_out, DP, split_axis=0, concat_axis=0, tiled=True)]
    ppermute x2, waiting for transfers between devices: 4 us -> 11.6 us  [swap(): return lax.ppermute(v, 'c', [(0, 1), (1, 0)])]
    all_to_all x2 -> x3, starting transfers between devices: 8.25 us -> 15 us  [the longest x2 9.57 us: spread(): return lax.all_to_all(v, PLANE, split_axis=0, concat_axis=0, tiled=True)]
    pallas_call x3, Pallas kernels: 32.6 us -> 27.2 us  [the longest x1 10.4 us: per_device(): pl.pallas_call(project_kernel, grid=(4,), in_specs=[SMEM, SMEM, SMEM, pl....]
    all_to_all x2 -> x3, waiting for transfers between devices: 88.8 us -> 84.3 us  [the longest x2 74.1 us: spread(): return lax.all_to_all(v, PLANE, split_axis=0, concat_axis=0, tiled=True)]
    convert_element_type x4 -> x3, other arithmetic: 12.6 us -> 9.34 us  [the longest x2 9.26 us: add(): return (a.astype(f32) + b.astype(f32)).astype(bf16)]
  transfers between devices with their start and end apart: 6 -> 7, of which waited for: 4 -> 6; matrix products, arithmetic and copies ran while one was open for 6% -> 6% of each run, Pallas kernels for 4% -> 3%
where the time goes in v3:
time: 254 us; the launch traced here: 250 us
  waiting for transfers between devices  151 us (59%)
  Pallas kernels  34.7 us (14%)
  other arithmetic  15.7 us (6%)
  starting transfers between devices  15.3 us (6%)
  blocking collectives  14.4 us (6%)
  between operations  14.1 us (6%)
  local copies, waits for them, and re-layouts  4.52 us (2%)
    all_to_all x2, waiting for transfers between devices, spread(): return lax.all_to_all(v, PLANE, split_axis=0, concat_axis=0, tiled=True)  74.1 us
    all_gather x1, waiting for transfers between devices, per_device(): gathered = lax.all_gather(packed, DP, axis=0, tiled=False)  55 us
    all_to_all x1, blocking collectives, share(): lax.all_to_all(spread_out, DP, split_axis=0, concat_axis=0, tiled=True)  14.4 us
    ppermute x2, waiting for transfers between devices, swap(): return lax.ppermute(v, 'c', [(0, 1), (1, 0)])  11.6 us
    pallas_call x1, Pallas kernels, per_device(): pl.pallas_call(project_kernel, grid=(4,), in_specs=[SMEM, SMEM, SMEM, pl....  10.4 us
    all_to_all x1, waiting for transfers between devices, share(): lax.all_to_all(spread_out, DP, split_axis=0, concat_axis=0, tiled=True)  10.2 us
    all_to_all x2, starting transfers between devices, spread(): return lax.all_to_all(v, PLANE, split_axis=0, concat_axis=0, tiled=True)  9.57 us
    convert_element_type x2, other arithmetic, add(): return (a.astype(f32) + b.astype(f32)).astype(bf16)  9.26 us
  transfers between devices with their start and end apart: 7, of which 6 were waited for; matrix products, arithmetic and copies ran while one was open for 6% of the time, Pallas kernels for 3%

profile of v3, /device:TPU:192, one launch (start us, length us, event | category | flops | bytes accessed | tf_op | source)
XLA Modules:
  0.0 249.7 jit_solution(10081915277814470939)
XLA Ops:
  7.2 1.8 maximum_maximum_fusion
  9.7 0.7 pad_add_fusion
  10.4 14.4 %all_to_all.20 = s32[32,1,12]{2,1,0:T(1,128)} all-to-all(s32[32,1,12]{2,1,0:T(1,128)S(1)} %broadcast_in_dim.6), channel_id=1, replica_groups=mesh['y'=4,'x'=4,'c'=2,'mp'=8] {'y','x','c'}, dimensions={0} | all-to-all | bytes 3072 | tf_op jit(solution)/shard_map/all_to_all | solution.py:192
  24.9 55.0 %all-gather.3.cloned.1.call-done = bf16[12288,512]{1,0:T(8,128)(2,1)} async-done(((bf16[384,512]{1,0:T(8,128)(2,1)}), bf16[12288,512]{1,0:T(8,128)(2,1)}) %all-gather.3.cloned.1.call-update) | async-done | bytes 12582928 | tf_op jit(solution)/shard_map/all_gather | solution.py:188
  79.9 10.4 %project.1 = (bf16[896,512]{1,0:T(8,128)(2,1)}, bf16[7,256,512]{2,1,0:T(8,128)(2,1)}, f32[24,128]{1,0:T(8,128)}) custom-call(s32[7]{0:T(128)} %bins.3, s32[7]{0:T(128)} %docs.3, s32[32,4]{1,0:T(8,128)} %bitcast.10, bf16[896,4096]{1,0:T(8,128)(2,1)} %e.3, bf16[32,384,512]{2,1,0:T(8,128)(2,1)} %bitcast.6, bf16[32,384,512]{2,1,0:T(8,128)(2,1)} %bitcast.7), custom_call_target="tpu_custom_call" | custom-call | tf_op jit(solution)/shard_map/project/pallas_call | solution.py:199
  90.3 1.5 broadcast_in_dim.7
  91.8 5.4 %all-to-all-start.1 = ((f32[32,24,128]{2,1,0:T(8,128)}), f32[32,24,128]{2,1,0:T(8,128)S(1)}, u32[]{:S(2)}, u32[]{:S(2)}) async-start(f32[32,24,128]{2,1,0:T(8,128)} %broadcast_in_dim.7), calls=%async_computation.1 | async-start | bytes 786432 | tf_op jit(solution)/shard_map/all_to_all | solution.py:192
  97.3 10.2 %all-to-all-done.1.stats = f32[32,24,128]{2,1,0:T(8,128)S(1)} async-done(((f32[32,24,128]{2,1,0:T(8,128)}), f32[32,24,128]{2,1,0:T(8,128)S(1)}, u32[]{:S(2)}, u32[]{:S(2)}) %all-to-all-start.1) | async-done | bytes 393248 | tf_op jit(solution)/shard_map/all_to_all | solution.py:192
  107.5 0.8 broadcast_in_dim.8.ids
  108.3 7.6 %attend.1 = (bf16[896,512]{1,0:T(8,128)(2,1)}, bf16[512,896]{1,0:T(8,128)(2,1)}, bf16[16,256,512]{2,1,0:T(8,128)(2,1)}, bf16[16,256,512]{2,1,0:T(8,128)(2,1)}) custom-call(s32[7]{0:T(128)} %bins.3, s32[7]{0:T(128)} %docs.3, s32[32,4]{1,0:T(8,128)} %bitcast.11, bf16[896,512]{1,0:T(8,128)(2,1)} %get-tuple-element.16.kv, ...), custom_call_target="tpu_custom_call" | custom-call | tf_op jit(solution)/shard_map/attend/pallas_call | solution.py:223
  115.9 8.2 %row_terms.1 = bf16[8,896,512]{2,1,0:T(8,128)(2,1)} custom-call(bf16[896,512]{1,0:T(8,128)(2,1)} %get-tuple-element.23.grads, bf16[32,384,512]{2,1,0:T(8,128)(2,1)} %bitcast.8), custom_call_target="tpu_custom_call" | custom-call | flops 3758096384 | bytes 16777216 | tf_op jit(solution)/shard_map/row_terms/pallas_call | solution.py:253
  124.2 7.3 %collective-permute-done = bf16[16,256,512]{2,1,0:T(8,128)(2,1)S(1)} collective-permute-done((bf16[16,256,512]{2,1,0:T(8,128)(2,1)}, bf16[16,256,512]{2,1,0:T(8,128)(2,1)S(1)}, u32[]{:S(2)}, u32[]{:S(2)}) %collective-permute-start) | collective-permute-done | bytes 4194336 | tf_op jit(solution)/shard_map/ppermute | solution.py:243
  131.5 5.8 %add_convert_fusion = bf16[16,256,512]{2,1,0:T(8,128)(2,1)} fusion(bf16[16,256,512]{2,1,0:T(8,128)(2,1)S(1)} %collective-permute-done, bf16[16,256,512]{2,1,0:T(8,128)(2,1)} %get-tuple-element.19), kind=kLoop, calls=%fused_computation | loop fusion | flops 8388608 | bytes 12582912 | tf_op jit(solution)/shard_map/convert_element_type | solution.py:249
  137.3 4.5 %all-to-all-start.2 = ((bf16[16,256,512]{2,1,0:T(8,128)(2,1)}), bf16[16,256,512]{2,1,0:T(8,128)(2,1)}, u32[]{:S(2)}, u32[]{:S(2)}) async-start(bf16[16,256,512]{2,1,0:T(8,128)(2,1)} %add_convert_fusion), calls=%async_computation.2 | async-start | bytes 8388608 | tf_op jit(solution)/shard_map/all_to_all | solution.py:246
  141.9 8.6 %weight_terms.1 = (bf16[16,512,128]{2,1,0:T(8,128)(2,1)}, bf16[16,512,128]{2,1,0:T(8,128)(2,1)}) custom-call(bf16[512,896]{1,0:T(8,128)(2,1)} %get-tuple-element.24.grads_t, bf16[896,4096]{1,0:T(8,128)(2,1)} %e.3), custom_call_target="tpu_custom_call" | custom-call | flops 3758096384 | bytes 16777216 | tf_op jit(solution)/shard_map/weight_terms/pallas_call | solution.py:272
  150.5 4.3 %collective-permute-done.1 = bf16[16,512,128]{2,1,0:T(8,128)(2,1)S(1)} collective-permute-done((bf16[16,512,128]{2,1,0:T(8,128)(2,1)}, bf16[16,512,128]{2,1,0:T(8,128)(2,1)S(1)}, u32[]{:S(2)}, u32[]{:S(2)}) %collective-permute-start.1) | collective-permute-done | bytes 2097184 | tf_op jit(solution)/shard_map/ppermute | solution.py:243
  154.8 3.5 %add_convert_fusion.1 = bf16[16,512,128]{2,1,0:T(8,128)(2,1)} fusion(bf16[16,512,128]{2,1,0:T(8,128)(2,1)S(1)} %collective-permute-done.1, bf16[16,512,128]{2,1,0:T(8,128)(2,1)} %get-tuple-element.25), kind=kLoop, calls=%fused_computation.1 | loop fusion | flops 4194304 | bytes 6291456 | tf_op jit(solution)/shard_map/convert_element_type | solution.py:249
  158.3 47.5 %all-to-all-done.2 = bf16[16,256,512]{2,1,0:T(8,128)(2,1)} async-done(((bf16[16,256,512]{2,1,0:T(8,128)(2,1)}), bf16[16,256,512]{2,1,0:T(8,128)(2,1)}, u32[]{:S(2)}, u32[]{:S(2)}) %all-to-all-start.2) | async-done | bytes 4194336 | tf_op jit(solution)/shard_map/all_to_all | solution.py:246
  205.8 5.0 %all-to-all-start.3 = ((bf16[16,512,128]{2,1,0:T(8,128)(2,1)}), bf16[16,512,128]{2,1,0:T(8,128)(2,1)S(1)}, u32[]{:S(2)}, u32[]{:S(2)}) async-start(bf16[16,512,128]{2,1,0:T(8,128)(2,1)} %add_convert_fusion.1), calls=%async_computation.4 | async-start | bytes 4194304 | tf_op jit(solution)/shard_map/all_to_all | solution.py:246
  210.8 2.8 %reduce_sum.24 = bf16[256,512]{1,0:T(8,128)(2,1)S(1)} reduce(bf16[16,256,512]{2,1,0:T(8,128)(2,1)} %all-to-all-done.2, bf16[]{:T(256)} %constant.7.clone.1), dimensions={0}, to_apply=%region_0.0 | reduce | flops 1966080 | bytes 4456450 | tf_op jit(solution)/shard_map/reduce_sum | solution.py:287
  213.6 0.7 fusion
  214.4 26.7 %all-to-all-done.3 = bf16[16,512,128]{2,1,0:T(8,128)(2,1)S(1)} async-done(((bf16[16,512,128]{2,1,0:T(8,128)(2,1)}), bf16[16,512,128]{2,1,0:T(8,128)(2,1)S(1)}, u32[]{:S(2)}, u32[]{:S(2)}) %all-to-all-start.3) | async-done | bytes 2097184 | tf_op jit(solution)/shard_map/all_to_all | solution.py:246
  241.3 0.7 copy.13
  242.1 0.7 copy.14
  (16 shorter events, 1.4 us)
Async XLA Ops:
  7.2 72.7 %all-gather.3.cloned.1.call-start = ((), (), s32[]{:S(2)}) async-start(), calls=%async_computation.6 | async-start | bytes 12976128 | tf_op jit(solution)/shard_map/all_gather | solution.py:188
  79.9 17.4 %copy-start.1 = (s32[32,1,12]{2,1,0:T(1,128)S(1)}, s32[32,1,12]{2,1,0:T(1,128)}, u32[]{:S(2)}) copy-start(s32[32,1,12]{2,1,0:T(1,128)} %all_to_all.20) | copy-start | bytes 4612
  91.8 15.7 %all-to-all-start.1 = ((f32[32,24,128]{2,1,0:T(8,128)}), f32[32,24,128]{2,1,0:T(8,128)S(1)}, u32[]{:S(2)}, u32[]{:S(2)}) async-start(f32[32,24,128]{2,1,0:T(8,128)} %broadcast_in_dim.7), calls=%async_computation.1 | async-start | bytes 786432 | tf_op jit(solution)/shard_map/all_to_all | solution.py:192
  97.2 145.6 %reduce-scatter.2.cloned.1.call-start = ((), (), s32[]{:S(2)}) async-start(), calls=%async_computation.5 | async-start | bytes 8257536 | tf_op jit(solution)/shard_map/reduce_scatter | solution.py:266
  107.5 0.8 copy-start
  124.1 7.5 %collective-permute-start = (bf16[16,256,512]{2,1,0:T(8,128)(2,1)}, bf16[16,256,512]{2,1,0:T(8,128)(2,1)S(1)}, u32[]{:S(2)}, u32[]{:S(2)}) collective-permute-start(bf16[16,256,512]{2,1,0:T(8,128)(2,1)} %get-tuple-element.20), channel_id=1, source_target_pairs={{0,8},{8,0},{1,9},{9,1},{2,10},{10,2},{3,11},{11,3},{4,12},{12,4},... | collective-permute-start | bytes 12582920 | tf_op jit(solution)/shard_map/ppermute | solution.py:243
  137.3 68.4 %all-to-all-start.2 = ((bf16[16,256,512]{2,1,0:T(8,128)(2,1)}), bf16[16,256,512]{2,1,0:T(8,128)(2,1)}, u32[]{:S(2)}, u32[]{:S(2)}) async-start(bf16[16,256,512]{2,1,0:T(8,128)(2,1)} %add_convert_fusion), calls=%async_computation.2 | async-start | bytes 8388608 | tf_op jit(solution)/shard_map/all_to_all | solution.py:246
  150.5 4.4 %collective-permute-start.1 = (bf16[16,512,128]{2,1,0:T(8,128)(2,1)}, bf16[16,512,128]{2,1,0:T(8,128)(2,1)S(1)}, u32[]{:S(2)}, u32[]{:S(2)}) collective-permute-start(bf16[16,512,128]{2,1,0:T(8,128)(2,1)} %get-tuple-element.26), channel_id=1, source_target_pairs={{0,8},{8,0},{1,9},{9,1},{2,10},{10,2},{3,11},{11,3},{4,12},{12,4},... | collective-permute-start | bytes 6291464 | tf_op jit(solution)/shard_map/ppermute | solution.py:243
  205.8 35.3 %all-to-all-start.3 = ((bf16[16,512,128]{2,1,0:T(8,128)(2,1)}), bf16[16,512,128]{2,1,0:T(8,128)(2,1)S(1)}, u32[]{:S(2)}, u32[]{:S(2)}) async-start(bf16[16,512,128]{2,1,0:T(8,128)(2,1)} %add_convert_fusion.1), calls=%async_computation.4 | async-start | bytes 4194304 | tf_op jit(solution)/shard_map/all_to_all | solution.py:246
Sparse Core Ops, SparseCore 0:
  11.1 68.6 all-gather.2
  124.2 80.8 reduce-scatter.1

commit v4 on v3

--- a/solution.py
+++ b/solution.py
@@ -39,28 +39,19 @@
     return first, first + lengths[j, k]
 
 
-def to_window(row, first):
-    return pltpu.roll(row, 2 * WIN - first, 1)[:, :WIN]
-
-
-def from_window(row, first):
-    return pltpu.roll(jnp.concatenate([row, jnp.zeros_like(row)], axis=1), first, 1)
-
-
 def block_scores(b, bins, docs, lengths, kv, qc):
     first, last = token_range(b, bins, docs, lengths)
     key, value = kv[b * BLK : (b + 1) * BLK, :HD], kv[b * BLK : (b + 1) * BLK, HD:]
     scores = mul(key, qc[b, :, :HD], 1, 1) * SCALE
     raw = mul(value, qc[b, :, HD:], 1, 1)
-    token = lax.broadcasted_iota(jnp.int32, scores.shape, 1)
-    return scores, raw, (token >= first) & (token < last), first
-
-
-def project_kernel(bins, docs, lengths, e, w, tokens, kv, qc, stats, acc, sems):
+    return scores, raw, lax.broadcasted_iota(jnp.int32, scores.shape, 1) < last - first
+
+
+def project_kernel(bins, docs, lengths, e, w, tokens, kv, qc, shared, acc, fetched, stats, sems):
     step = pl.program_id(0)
 
     def fetch(b):
-        return pltpu.make_async_copy(tokens.at[bins[b], 128:384, :], qc.at[b], sems.at[b])
+        return pltpu.make_async_copy(tokens.at[bins[b], 128:384, :], fetched.at[b], sems.at[b])
 
     @pl.when(step == 0)
     def _():
@@ -83,29 +74,23 @@
         stats[...] = jnp.zeros_like(stats)
         for b in range(EBLK):
             fetch(b).wait()
+            first, _ = token_range(b, bins, docs, lengths)
+            turned = pltpu.roll(fetched[b].astype(f32), lax.rem(2 * WIN - first, 2 * WIN), 0)
+            qc[b] = turned[:WIN].astype(bf16)
         for b in range(EBLK):
-            scores, raw, live, first = block_scores(b, bins, docs, lengths, kv, qc)
+            scores, raw, live = block_scores(b, bins, docs, lengths, kv, qc)
             scores = jnp.where(live, scores, MASKED)
             top = jnp.max(scores, axis=0, keepdims=True)
             raised = jnp.where(live, jnp.exp(scores - top), 0.0)
-            stats[b : b + 1, :] = to_window(top, first)
-            stats[8 + b : 9 + b, :] = to_window(jnp.sum(raised, axis=0, keepdims=True), first)
-            stats[16 + b : 17 + b, :] = to_window(jnp.sum(raised * raw, axis=0, keepdims=True), first)
-
-
-def attend_kernel(bins, docs, lengths, kv, qc, stats, ids, grads, grads_t, mine, other, zero, made, sems):
-    core = lax.axis_index("c")
-
-    def send(source, j, do):
-        here = lax.rem(j, 2) == core
-
-        @pl.when(here)
-        def _():
-            do(pltpu.make_async_copy(source, mine.at[lax.div(j, 2)], sems.at[j]))
-
-        @pl.when(jnp.logical_not(here))
-        def _():
-            do(pltpu.make_async_copy(source, other.at[lax.div(j, 2)], sems.at[j]))
+            stats[b : b + 1, :] = top
+            stats[8 + b : 9 + b, :] = jnp.sum(raised, axis=0, keepdims=True)
+            stats[16 + b : 17 + b, :] = jnp.sum(raised * raw, axis=0, keepdims=True)
+        shared[...] = jnp.broadcast_to(stats[...][None], shared.shape)
+
+
+def attend_kernel(bins, docs, lengths, kv, qc, stats, ids, grads, grads_t, slots, zero, made, sems):
+    def copy(source, j):
+        return pltpu.make_async_copy(source, slots.at[j], sems.at[j])
 
     zero[...] = jnp.zeros_like(zero)
 
@@ -116,7 +101,7 @@
 
         @pl.when(jnp.logical_not(used))
         def _():
-            send(zero, j, lambda copy: copy.start())
+            copy(zero, j).start()
 
         return carry
 
@@ -127,15 +112,13 @@
     dots = stats[:, 16:24, :].reshape(-1, WIN)
     owners = ids[...].reshape(-1, WIN)
     for b in range(EBLK):
-        scores, raw, live, first = block_scores(b, bins, docs, lengths, kv, qc)
+        scores, raw, live = block_scores(b, bins, docs, lengths, kv, qc)
         same = owners == (bins[b] * NDOC + docs[b]).astype(f32)
         masked = jnp.where(same, tops, MASKED)
         top = jnp.max(masked, axis=0, keepdims=True)
         level = jnp.where(same, jnp.exp(masked - top), 0.0)
         total = jnp.maximum(jnp.sum(level * sums, axis=0, keepdims=True), 1.0)
         delta = jnp.sum(level * dots, axis=0, keepdims=True) / total
-        top, delta = from_window(top, first), from_window(delta, first)
-        total = jnp.maximum(from_window(total, first), 1.0)
         attention = jnp.exp(jnp.where(live, scores - top, MASKED)) / total
         rounded = attention.astype(bf16)
         score_grad = (attention * (raw - delta) * SCALE).astype(bf16)
@@ -143,17 +126,38 @@
         query, cotangent = qc[b, :, :HD], qc[b, :, HD:]
         made[b, :, :HD] = mul(rounded, kv[rows, HD:], 0, 0).astype(bf16)
         made[b, :, HD:] = mul(score_grad, kv[rows, :HD], 0, 0).astype(bf16)
-        send(made.at[b], bins[b], lambda copy: copy.start())
+        copy(made.at[b], bins[b]).start()
         grads[rows, :HD] = mul(score_grad, query, 1, 0).astype(bf16)
         grads[rows, HD:] = mul(rounded, cotangent, 1, 0).astype(bf16)
         grads_t[:HD, rows] = mul(query, score_grad, 0, 1).astype(bf16)
         grads_t[HD:, rows] = mul(cotangent, rounded, 0, 1).astype(bf16)
 
     def finish(j, carry):
-        send(zero, j, lambda copy: copy.wait())
+        copy(zero, j).wait()
         return carry
 
     lax.fori_loop(0, BINS, finish, 0)
+
+
+def collect_kernel(docs, lengths, windows, context, query_grad, acc):
+    step = pl.program_id(0)
+
+    @pl.when(step == 0)
+    def _():
+        acc[...] = jnp.zeros_like(acc)
+
+    for i in range(windows.shape[0]):
+        acc[docs[step * windows.shape[0] + i]] += windows[i].astype(f32)
+
+    @pl.when(step == pl.num_programs(0) - 1)
+    def _():
+        total = jnp.concatenate([acc[0], jnp.zeros_like(acc[0])], axis=0)
+        first = lengths[0, 0]
+        for k in range(1, NDOC):
+            total += pltpu.roll(jnp.concatenate([acc[k], jnp.zeros_like(acc[k])], axis=0), first, 0)
+            first = first + lengths[0, k]
+        context[...] = total[:, :HD].astype(bf16)
+        query_grad[...] = total[:, HD:].astype(bf16)
 
 
 def rows_kernel(grads, w, out):
@@ -195,6 +199,10 @@
     facts = share(facts[None, :])[:, 0, :]
     lengths = facts[:, :NDOC]
     ids = jnp.broadcast_to(facts[:, NDOC:, None].astype(f32), (BINS, 8, WIN))
+    sent = facts[:, NDOC : NDOC + EBLK]
+    me = lax.axis_index(DP)
+    sent_docs = jnp.sum(jnp.where(sent // NDOC == me, sent % NDOC, 0), axis=1)
+    ids, sent_docs, lengths, gathered = lax.optimization_barrier((ids, sent_docs, lengths, gathered))
 
     kv, qc, stats = pl.pallas_call(
         project_kernel,
@@ -209,46 +217,41 @@
         ],
         out_specs=[
             pl.BlockSpec((rows, 2 * HD), lambda k: (0, 0)),
-            pl.BlockSpec((EBLK, tokens, 2 * HD), lambda k: (0, 0, 0)),
-            pl.BlockSpec((24, WIN), lambda k: (0, 0)),
-        ],
-        out_shape=[shape(rows, 2 * HD), shape(EBLK, tokens, 2 * HD), shape(24, WIN, dtype=f32)],
-        scratch_shapes=[pltpu.VMEM((rows, 2 * HD), f32), pltpu.SemaphoreType.DMA((EBLK,))],
+            pl.BlockSpec((EBLK, WIN, 2 * HD), lambda k: (0, 0, 0)),
+            pl.BlockSpec((BINS, 24, WIN), lambda k: (0, 0, 0)),
+        ],
+        out_shape=[shape(rows, 2 * HD), shape(EBLK, WIN, 2 * HD), shape(BINS, 24, WIN, dtype=f32)],
+        scratch_shapes=[
+            pltpu.VMEM((rows, 2 * HD), f32),
+            pltpu.VMEM((EBLK, tokens, 2 * HD), bf16),
+            pltpu.VMEM((24, WIN), f32),
+            pltpu.SemaphoreType.DMA((EBLK,)),
+        ],
         compiler_params=params(),
         name="project",
     )(block_bin, block_document, lengths, encoder_rows, gathered, gathered)
 
-    all_stats = share(stats)
-
-    grads, grads_t, mine, other = pl.pallas_call(
+    all_stats = lax.all_to_all(stats, DP, split_axis=0, concat_axis=0, tiled=True)
+
+    grads, grads_t, slots = pl.pallas_call(
         attend_kernel,
         in_specs=[SMEM, SMEM, SMEM, VMEM, VMEM, VMEM, VMEM],
-        out_specs=[VMEM, VMEM, ANY, ANY],
+        out_specs=[VMEM, VMEM, ANY],
         out_shape=[
             shape(rows, 2 * HD),
             shape(2 * HD, rows),
-            shape(16, tokens, 2 * HD),
-            shape(16, tokens, 2 * HD),
+            shape(BINS, WIN, 2 * HD),
         ],
         scratch_shapes=[
-            pltpu.VMEM((tokens, 2 * HD), bf16),
-            pltpu.VMEM((EBLK, tokens, 2 * HD), bf16),
+            pltpu.VMEM((WIN, 2 * HD), bf16),
+            pltpu.VMEM((EBLK, WIN, 2 * HD), bf16),
             pltpu.SemaphoreType.DMA((BINS,)),
         ],
         compiler_params=params(),
         name="attend",
     )(block_bin, block_document, lengths, kv, qc, all_stats, ids)
 
-    def swap(v):
-        return lax.ppermute(v, "c", [(0, 1), (1, 0)])
-
-    def spread(v):
-        return lax.all_to_all(v, PLANE, split_axis=0, concat_axis=0, tiled=True)
-
-    def add(a, b):
-        return (a.astype(f32) + b.astype(f32)).astype(bf16)
-
-    arrived = swap(other)
+    windows = lax.all_to_all(slots, DP, split_axis=0, concat_axis=0, tiled=True)
 
     row_terms = pl.pallas_call(
         rows_kernel,
@@ -265,9 +268,6 @@
     )(grads, gathered)
     encoder_grad = lax.psum_scatter(row_terms, "mp", scatter_dimension=0, tiled=False)
 
-    pair_sums = add(mine, arrived)
-    pair_sums, grads_t = lax.optimization_barrier((pair_sums, grads_t))
-    token_sums = spread(pair_sums)
 
     mine_w, other_w = pl.pallas_call(
         weights_kernel,
@@ -282,11 +282,24 @@
         cost_estimate=COST,
         name="weight_terms",
     )(grads_t, encoder_rows)
-    weight_sums = spread(add(mine_w, swap(other_w)))
-
-    outs = jnp.sum(token_sums.astype(f32), axis=0).astype(bf16)
+    arrived = lax.ppermute(other_w, "c", [(0, 1), (1, 0)])
+    pair_sums = (mine_w.astype(f32) + arrived.astype(f32)).astype(bf16)
+    windows, pair_sums = lax.optimization_barrier((windows, pair_sums))
+    weight_sums = lax.all_to_all(pair_sums, PLANE, split_axis=0, concat_axis=0, tiled=True)
+
+    context, query_grad = pl.pallas_call(
+        collect_kernel,
+        grid=(8,),
+        in_specs=[SMEM, SMEM, pl.BlockSpec((4, WIN, 2 * HD), lambda k: (k, 0, 0))],
+        out_specs=[pl.BlockSpec((tokens, HD), lambda k: (0, 0))] * 2,
+        out_shape=[shape(tokens, HD)] * 2,
+        scratch_shapes=[pltpu.VMEM((NDOC, WIN, 2 * HD), f32)],
+        compiler_params=params(),
+        name="collect",
+    )(sent_docs, document_lengths, windows)
+
     weights = jnp.sum(weight_sums.astype(f32), axis=0).astype(bf16).T
-    return outs[:, :HD], outs[:, HD:], encoder_grad, weights[:, :HD], weights[:, HD:]
+    return context, query_grad, encoder_grad, weights[:, :HD], weights[:, HD:]
 
 
 def solution(mesh):

time: 254 us -> 226 us (0.89)
  waiting for transfers between devices: 151 us -> 126 us
  other arithmetic: 15.7 us -> 7.73 us
  Pallas kernels: 34.7 us -> 40.9 us
    all_to_all x2, waiting for transfers between devices: 74.1 us -> 60.7 us  [the longest x1 36.8 us: per_device(): windows = lax.all_to_all(slots, DP, split_axis=0, concat_axis=0, tiled=True)]
    ppermute x2 -> x1, waiting for transfers between devices: 11.6 us -> 4.3 us  [per_device(): arrived = lax.ppermute(other_w, 'c', [(0, 1), (1, 0)])]
    pallas_call x0 -> x1, Pallas kernels: none -> 6.23 us  [per_device(): pl.pallas_call(collect_kernel, grid=(8,), in_specs=[SMEM, SMEM, pl.BlockS...]
    convert_element_type x2 -> x1, other arithmetic: 9.26 us -> 3.49 us  [per_device(): pair_sums = (mine_w.astype(f32) + arrived.astype(f32)).astype(bf16)]
    all_to_all x1, waiting for transfers between devices: 10.2 us -> 7.22 us  [share(): lax.all_to_all(spread_out, DP, split_axis=0, concat_axis=0, tiled=True)]
  transfers between devices with their start and end apart: 7 -> 6, of which waited for: 6 -> 5; matrix products, arithmetic and copies ran while one was open for 6% -> 4% of each run, Pallas kernels for 3% -> 7%
where the time goes in v4:
time: 226 us; the launch traced here: 223 us
  waiting for transfers between devices  126 us (56%)
  Pallas kernels  40.9 us (18%)
  starting transfers between devices  16.1 us (7%)
  blocking collectives  15.8 us (7%)
  between operations  14.1 us (6%)
  other arithmetic  7.73 us (3%)
  local copies, waits for them, and re-layouts  2.87 us (1%)
    all_gather x1, waiting for transfers between devices, per_device(): gathered = lax.all_gather(packed, DP, axis=0, tiled=False)  53.4 us
    all_to_all x1, waiting for transfers between devices, per_device(): windows = lax.all_to_all(slots, DP, split_axis=0, concat_axis=0, tiled=True)  36.8 us
    all_to_all x1, waiting for transfers between devices, per_device(): lax.all_to_all(pair_sums, PLANE, split_axis=0, concat_axis=0, tiled=True)  23.9 us
    all_to_all x1, blocking collectives, per_device(): lax.all_to_all(stats, DP, split_axis=0, concat_axis=0, tiled=True)  15.8 us
    pallas_call x1, Pallas kernels, per_device(): pl.pallas_call(project_kernel, grid=(4,), in_specs=[SMEM, SMEM, SMEM, pl....  11.1 us
    pallas_call x1, Pallas kernels, per_device(): pl.pallas_call(weights_kernel, grid=(4,), in_specs=[pl.BlockSpec((2 * HD,...  8.78 us
    pallas_call x1, Pallas kernels, per_device(): pl.pallas_call(rows_kernel, grid=(4,), in_specs=[pl.BlockSpec((rows, 2 *...  8.21 us
    all_to_all x1, starting transfers between devices, share(): lax.all_to_all(spread_out, DP, split_axis=0, concat_axis=0, tiled=True)  7.32 us
  transfers between devices with their start and end apart: 6, of which 5 were waited for; matrix products, arithmetic and copies ran while one was open for 4% of the time, Pallas kernels for 7%

profile of v4, /device:TPU:192, one launch (start us, length us, event | category | flops | bytes accessed | tf_op | source)
XLA Modules:
  0.0 223.2 jit_solution(191670939044316312)
XLA Ops:
  7.2 1.8 maximum_maximum_fusion
  9.0 0.7 multiply_add_fusion
  9.7 0.7 pad_add_fusion
  10.4 0.6 broadcast_in_dim.5
  11.0 7.3 %all-to-all-start = ((s32[32,1,12]{2,1,0:T(1,128)}), s32[32,1,12]{2,1,0:T(1,128)S(1)}, u32[]{:S(2)}, u32[]{:S(2)}) async-start(s32[32,1,12]{2,1,0:T(1,128)} %broadcast_in_dim.5), calls=%async_computation | async-start | bytes 32768 | tf_op jit(solution)/shard_map/all_to_all | solution.py:196
  18.4 7.2 %all-to-all-done = s32[32,1,12]{2,1,0:T(1,128)S(1)} async-done(((s32[32,1,12]{2,1,0:T(1,128)}), s32[32,1,12]{2,1,0:T(1,128)S(1)}, u32[]{:S(2)}, u32[]{:S(2)}) %all-to-all-start) | async-done | bytes 1568 | tf_op jit(solution)/shard_map/all_to_all | solution.py:196
  25.6 0.7 fusion.2.docs
  26.4 53.4 %all-gather.3.cloned.1.call-done = bf16[12288,512]{1,0:T(8,128)(2,1)} async-done(((bf16[384,512]{1,0:T(8,128)(2,1)}), bf16[12288,512]{1,0:T(8,128)(2,1)}) %all-gather.3.cloned.1.call-update) | async-done | bytes 12582928 | tf_op jit(solution)/shard_map/all_gather | solution.py:192
  79.9 0.8 broadcast_in_dim.6.ids
  80.6 11.1 %project.1 = (bf16[896,512]{1,0:T(8,128)(2,1)}, bf16[7,128,512]{2,1,0:T(8,128)(2,1)}, f32[32,24,128]{2,1,0:T(8,128)}) custom-call(s32[7]{0:T(128)} %bins.3, s32[7]{0:T(128)} %docs.3, s32[32,4]{1,0:T(8,128)} %bitcast.12, bf16[896,4096]{1,0:T(8,128)(2,1)} %e.3, bf16[32,384,512]{2,1,0:T(8,128)(2,1)} %bitcast.6, bf16[32,384,512]{2,1,0:T(8,128)(2,1)} %bitcast.7), custom_call_target="tpu_custom_call" | custom-call | tf_op jit(solution)/shard_map/project/pallas_call | solution.py:207
  91.8 15.8 %all_to_all.20.stats = f32[32,24,128]{2,1,0:T(8,128)} all-to-all(f32[32,24,128]{2,1,0:T(8,128)} %get-tuple-element.26), channel_id=1, replica_groups=mesh['y'=4,'x'=4,'c'=2,'mp'=8] {'y','x','c'}, dimensions={0} | all-to-all | bytes 786432 | tf_op jit(solution)/shard_map/all_to_all | solution.py:234
  107.6 6.5 %attend.1 = (bf16[896,512]{1,0:T(8,128)(2,1)}, bf16[512,896]{1,0:T(8,128)(2,1)}, bf16[32,128,512]{2,1,0:T(8,128)(2,1)}) custom-call(s32[7]{0:T(128)} %bins.3, s32[7]{0:T(128)} %docs.3, s32[32,4]{1,0:T(8,128)} %bitcast.13, bf16[896,512]{1,0:T(8,128)(2,1)} %get-tuple-element.24.kv, bf16[7,128,512]{2,1,0:T(8,128)(2,1)} %get-tuple-element.25.qc, ...), custom_call_target="tpu_custom_call" | custom-call | tf_op jit(solution)/shard_map/attend/pallas_call | solution.py:236
  114.2 8.2 %row_terms.1 = bf16[8,896,512]{2,1,0:T(8,128)(2,1)} custom-call(bf16[896,512]{1,0:T(8,128)(2,1)} %get-tuple-element.35.grads, bf16[32,384,512]{2,1,0:T(8,128)(2,1)} %bitcast.8), custom_call_target="tpu_custom_call" | custom-call | flops 3758096384 | bytes 16777216 | tf_op jit(solution)/shard_map/row_terms/pallas_call | solution.py:256
  122.4 4.9 %all-to-all-start.2 = ((bf16[32,128,512]{2,1,0:T(8,128)(2,1)}), bf16[32,128,512]{2,1,0:T(8,128)(2,1)}, u32[]{:S(2)}, u32[]{:S(2)}) async-start(bf16[32,128,512]{2,1,0:T(8,128)(2,1)} %get-tuple-element.28), calls=%async_computation.2 | async-start | bytes 8388608 | tf_op jit(solution)/shard_map/all_to_all | solution.py:254
  127.3 8.8 %weight_terms.1 = (bf16[16,512,128]{2,1,0:T(8,128)(2,1)}, bf16[16,512,128]{2,1,0:T(8,128)(2,1)}) custom-call(bf16[512,896]{1,0:T(8,128)(2,1)} %get-tuple-element.29.grads_t, bf16[896,4096]{1,0:T(8,128)(2,1)} %e.3), custom_call_target="tpu_custom_call" | custom-call | flops 3758096384 | bytes 16777216 | tf_op jit(solution)/shard_map/weight_terms/pallas_call | solution.py:272
  136.1 4.3 %collective-permute-done = bf16[16,512,128]{2,1,0:T(8,128)(2,1)S(1)} collective-permute-done((bf16[16,512,128]{2,1,0:T(8,128)(2,1)}, bf16[16,512,128]{2,1,0:T(8,128)(2,1)S(1)}, u32[]{:S(2)}, u32[]{:S(2)}) %collective-permute-start) | collective-permute-done | bytes 2097184 | tf_op jit(solution)/shard_map/ppermute | solution.py:285
  140.4 3.5 %add_convert_fusion = bf16[16,512,128]{2,1,0:T(8,128)(2,1)} fusion(bf16[16,512,128]{2,1,0:T(8,128)(2,1)S(1)} %collective-permute-done, bf16[16,512,128]{2,1,0:T(8,128)(2,1)} %get-tuple-element.30), kind=kLoop, calls=%fused_computation | loop fusion | flops 4194304 | bytes 6291456 | tf_op jit(solution)/shard_map/convert_element_type | solution.py:286
  143.9 36.8 %all-to-all-done.2.windows = bf16[32,128,512]{2,1,0:T(8,128)(2,1)} async-done(((bf16[32,128,512]{2,1,0:T(8,128)(2,1)}), bf16[32,128,512]{2,1,0:T(8,128)(2,1)}, u32[]{:S(2)}, u32[]{:S(2)}) %all-to-all-start.2) | async-done | bytes 4194336 | tf_op jit(solution)/shard_map/all_to_all | solution.py:254
  180.7 3.7 %all-to-all-start.3 = ((bf16[16,512,128]{2,1,0:T(8,128)(2,1)}), bf16[16,512,128]{2,1,0:T(8,128)(2,1)S(1)}, u32[]{:S(2)}, u32[]{:S(2)}) async-start(bf16[16,512,128]{2,1,0:T(8,128)(2,1)} %add_convert_fusion), calls=%async_computation.4 | async-start | bytes 4194304 | tf_op jit(solution)/shard_map/all_to_all | solution.py:288
  184.5 6.2 %collect.1 = (bf16[256,256]{1,0:T(8,128)(2,1)}, bf16[256,256]{1,0:T(8,128)(2,1)}) custom-call(s32[32]{0:T(128)} %fusion.2.docs, s32[1,4]{1,0:T(1,128)} %lengths.1, bf16[32,128,512]{2,1,0:T(8,128)(2,1)} %all-to-all-done.2.windows), custom_call_target="tpu_custom_call" | custom-call | tf_op jit(solution)/shard_map/collect/pallas_call | solution.py:290
  190.7 23.9 %all-to-all-done.3 = bf16[16,512,128]{2,1,0:T(8,128)(2,1)S(1)} async-done(((bf16[16,512,128]{2,1,0:T(8,128)(2,1)}), bf16[16,512,128]{2,1,0:T(8,128)(2,1)S(1)}, u32[]{:S(2)}, u32[]{:S(2)}) %all-to-all-start.3) | async-done | bytes 2097184 | tf_op jit(solution)/shard_map/all_to_all | solution.py:288
  214.6 0.3 reduce_sum.22
  214.9 0.7 copy.13
  215.6 0.7 copy.14
  (10 shorter events, 0.3 us)
Async XLA Ops:
  7.2 72.7 %all-gather.3.cloned.1.call-start = ((), (), s32[]{:S(2)}) async-start(), calls=%async_computation.6 | async-start | bytes 12976128 | tf_op jit(solution)/shard_map/all_gather | solution.py:192
  11.0 14.6 %all-to-all-start = ((s32[32,1,12]{2,1,0:T(1,128)}), s32[32,1,12]{2,1,0:T(1,128)S(1)}, u32[]{:S(2)}, u32[]{:S(2)}) async-start(s32[32,1,12]{2,1,0:T(1,128)} %broadcast_in_dim.5), calls=%async_computation | async-start | bytes 32768 | tf_op jit(solution)/shard_map/all_to_all | solution.py:196
  18.4 198.0 %reduce-scatter.2.cloned.1.call-start = ((), (), s32[]{:S(2)}) async-start(), calls=%async_computation.5 | async-start | bytes 8257536 | tf_op jit(solution)/shard_map/reduce_scatter | solution.py:269
  25.6 55.0 %copy-start = (s32[32,1,12]{2,1,0:T(1,128)}, s32[32,1,12]{2,1,0:T(1,128)S(1)}, u32[]{:S(2)}) copy-start(s32[32,1,12]{2,1,0:T(1,128)S(1)} %all-to-all-done) | copy-start | bytes 4612
  122.4 58.4 %all-to-all-start.2 = ((bf16[32,128,512]{2,1,0:T(8,128)(2,1)}), bf16[32,128,512]{2,1,0:T(8,128)(2,1)}, u32[]{:S(2)}, u32[]{:S(2)}) async-start(bf16[32,128,512]{2,1,0:T(8,128)(2,1)} %get-tuple-element.28), calls=%async_computation.2 | async-start | bytes 8388608 | tf_op jit(solution)/shard_map/all_to_all | solution.py:254
  136.0 4.4 %collective-permute-start = (bf16[16,512,128]{2,1,0:T(8,128)(2,1)}, bf16[16,512,128]{2,1,0:T(8,128)(2,1)S(1)}, u32[]{:S(2)}, u32[]{:S(2)}) collective-permute-start(bf16[16,512,128]{2,1,0:T(8,128)(2,1)} %get-tuple-element.31), channel_id=1, source_target_pairs={{0,8},{8,0},{1,9},{9,1},{2,10},{10,2},{3,11},{11,3},{4,12},{12,4},... | collective-permute-start | bytes 6291464 | tf_op jit(solution)/shard_map/ppermute | solution.py:285
  180.7 33.8 %all-to-all-start.3 = ((bf16[16,512,128]{2,1,0:T(8,128)(2,1)}), bf16[16,512,128]{2,1,0:T(8,128)(2,1)S(1)}, u32[]{:S(2)}, u32[]{:S(2)}) async-start(bf16[16,512,128]{2,1,0:T(8,128)(2,1)} %add_convert_fusion), calls=%async_computation.4 | async-start | bytes 4194304 | tf_op jit(solution)/shard_map/all_to_all | solution.py:288
Sparse Core Ops, SparseCore 0:
  11.1 68.6 all-gather.2
  122.5 80.9 reduce-scatter.1

commit v5 on v4

--- a/solution.py
+++ b/solution.py
@@ -14,7 +14,6 @@
 BINS = 32
 MASKED = -1e30
 SCALE = HD ** (-0.5)
-PLANE = ("y", "x")
 DP = ("y", "x", "c")
 bf16, f32 = jnp.bfloat16, jnp.float32
 VMEM = pl.BlockSpec(memory_space=pltpu.VMEM)
@@ -175,8 +174,31 @@
         other[i] = jnp.where(core == 0, odd, even)
 
 
+def turn_kernel(weights, key, value):
+    key[...] = weights[:HD].astype(f32).T.astype(bf16)
+    value[...] = weights[HD:].astype(f32).T.astype(bf16)
+
+
 def shape(*dims, dtype=bf16):
     return jax.ShapeDtypeStruct(dims, dtype)
+
+
+def send(v, axis, distance):
+    return lax.ppermute(v, axis, [(i, (i + distance) % 4) for i in range(4)])
+
+
+def quarter_sum(terms, axis, dim):
+    me = lax.axis_index(axis)
+
+    def part(distance):
+        return lax.dynamic_index_in_dim(terms, lax.rem(me + distance + 4, 4), dim, keepdims=False)
+
+    far = part(2)
+    half = far.shape[-2] // 2
+    near = send(part(1), axis, 1), send(part(-1), axis, -1)
+    top, low = send(far[..., :half, :], axis, 2), send(far[..., half:, :], axis, -2)
+    total = part(0).astype(f32) + near[0].astype(f32) + near[1].astype(f32)
+    return (total + jnp.concatenate([top, low], axis=-2).astype(f32)).astype(bf16)
 
 
 def per_device(queries, context_grad, encoder_rows, key_weight, value_weight, document_lengths, block_bin, block_document):
@@ -284,8 +306,15 @@
     )(grads_t, encoder_rows)
     arrived = lax.ppermute(other_w, "c", [(0, 1), (1, 0)])
     pair_sums = (mine_w.astype(f32) + arrived.astype(f32)).astype(bf16)
-    windows, pair_sums = lax.optimization_barrier((windows, pair_sums))
-    weight_sums = lax.all_to_all(pair_sums, PLANE, split_axis=0, concat_axis=0, tiled=True)
+    weights = quarter_sum(pair_sums.reshape(4, 4, 2 * HD, 128), "x", 1)
+    weights = quarter_sum(weights, "y", 0)
+    key_weight_grad, value_weight_grad = pl.pallas_call(
+        turn_kernel,
+        in_specs=[VMEM],
+        out_specs=[VMEM] * 2,
+        out_shape=[shape(128, HD)] * 2,
+        name="turn",
+    )(weights)
 
     context, query_grad = pl.pallas_call(
         collect_kernel,
@@ -298,8 +327,7 @@
         name="collect",
     )(sent_docs, document_lengths, windows)
 
-    weights = jnp.sum(weight_sums.astype(f32), axis=0).astype(bf16).T
-    return context, query_grad, encoder_grad, weights[:, :HD], weights[:, HD:]
+    return context, query_grad, encoder_grad, key_weight_grad, value_weight_grad
 
 
 def solution(mesh):

time: 226 us -> 233 us (1.031)
  starting transfers between devices: 16.1 us -> 25.7 us
  waiting for transfers between devices: 126 us -> 119 us
    ppermute x0 -> x8, waiting for transfers between devices: none -> 54.1 us  [send(): return lax.ppermute(v, axis, [(i, (i + distance) % 4) for i in range(4)])]
    all_to_all x1, waiting for transfers between devices: 36.8 us -> 0.01 us  [per_device(): windows = lax.all_to_all(slots, DP, split_axis=0, concat_axis=0, tiled=True)]
    all_to_all x1 -> x0, waiting for transfers between devices: 23.9 us -> none  [per_device(): lax.all_to_all(pair_sums, PLANE, split_axis=0, concat_axis=0, tiled=True)]
    ppermute x0 -> x8, starting transfers between devices: none -> 13.4 us  [send(): return lax.ppermute(v, axis, [(i, (i + distance) % 4) for i in range(4)])]
    all_to_all x1 -> x0, starting transfers between devices: 3.72 us -> none  [per_device(): lax.all_to_all(pair_sums, PLANE, split_axis=0, concat_axis=0, tiled=True)]
    convert_element_type x0 -> x2, other arithmetic: none -> 2.35 us  [quarter_sum(): (total + jnp.concatenate([top, low], axis=-2).astype(f32)).astype(bf16)]
  transfers between devices with their start and end apart: 6 -> 13, of which waited for: 5 -> 8; matrix products, arithmetic and copies ran while one was open for 4% -> 4% of each run, Pallas kernels for 7% -> 7%
where the time goes in v5:
time: 233 us; the launch traced here: 230 us
  waiting for transfers between devices  119 us (51%)
  Pallas kernels  42.7 us (18%)
  starting transfers between devices  25.7 us (11%)
  blocking collectives  15.8 us (7%)
  between operations  14.1 us (6%)
  other arithmetic  9.19 us (4%)
  local copies, waits for them, and re-layouts  3.63 us (2%)
    ppermute x8, waiting for transfers between devices, send(): return lax.ppermute(v, axis, [(i, (i + distance) % 4) for i in range(4)])  54.1 us
    all_gather x1, waiting for transfers between devices, per_device(): gathered = lax.all_gather(packed, DP, axis=0, tiled=False)  53.4 us
    all_to_all x1, blocking collectives, per_device(): lax.all_to_all(stats, DP, split_axis=0, concat_axis=0, tiled=True)  15.8 us
    ppermute x8, starting transfers between devices, send(): return lax.ppermute(v, axis, [(i, (i + distance) % 4) for i in range(4)])  13.4 us
    pallas_call x1, Pallas kernels, per_device(): pl.pallas_call(project_kernel, grid=(4,), in_specs=[SMEM, SMEM, SMEM, pl....  11.1 us
    pallas_call x1, Pallas kernels, per_device(): pl.pallas_call(weights_kernel, grid=(4,), in_specs=[pl.BlockSpec((2 * HD,...  8.89 us
    pallas_call x1, Pallas kernels, per_device(): pl.pallas_call(rows_kernel, grid=(4,), in_specs=[pl.BlockSpec((rows, 2 *...  8.21 us
    all_to_all x1, starting transfers between devices, share(): lax.all_to_all(spread_out, DP, split_axis=0, concat_axis=0, tiled=True)  7.32 us
  transfers between devices with their start and end apart: 13, of which 8 were waited for; matrix products, arithmetic and copies ran while one was open for 4% of the time, Pallas kernels for 7%

profile of v5, /device:TPU:192, one launch (start us, length us, event | category | flops | bytes accessed | tf_op | source)
XLA Modules:
  0.0 230.2 jit_solution(10205277976258384893)
XLA Ops:
  7.2 1.8 maximum_maximum_fusion
  11.0 7.3 %all-to-all-start = ((s32[32,1,12]{2,1,0:T(1,128)}), s32[32,1,12]{2,1,0:T(1,128)S(1)}, u32[]{:S(2)}, u32[]{:S(2)}) async-start(s32[32,1,12]{2,1,0:T(1,128)} %broadcast_in_dim.5), calls=%async_computation | async-start | bytes 32768 | tf_op jit(solution)/shard_map/all_to_all | solution.py:218
  18.4 7.2 %all-to-all-done = s32[32,1,12]{2,1,0:T(1,128)S(1)} async-done(((s32[32,1,12]{2,1,0:T(1,128)}), s32[32,1,12]{2,1,0:T(1,128)S(1)}, u32[]{:S(2)}, u32[]{:S(2)}) %all-to-all-start) | async-done | bytes 1568 | tf_op jit(solution)/shard_map/all_to_all | solution.py:218
  26.5 53.4 %all-gather.3.cloned.1.call-done = bf16[12288,512]{1,0:T(8,128)(2,1)} async-done(((bf16[384,512]{1,0:T(8,128)(2,1)}), bf16[12288,512]{1,0:T(8,128)(2,1)}) %all-gather.3.cloned.1.call-update) | async-done | bytes 12582928 | tf_op jit(solution)/shard_map/all_gather | solution.py:214
  80.6 11.1 %project.1 = (bf16[896,512]{1,0:T(8,128)(2,1)}, bf16[7,128,512]{2,1,0:T(8,128)(2,1)}, f32[32,24,128]{2,1,0:T(8,128)}) custom-call(s32[7]{0:T(128)} %bins.3, s32[7]{0:T(128)} %docs.3, s32[32,4]{1,0:T(8,128)} %bitcast.35, bf16[896,4096]{1,0:T(8,128)(2,1)} %e.3, bf16[32,384,512]{2,1,0:T(8,128)(2,1)} %bitcast.28, bf16[32,384,512]{2,1,0:T(8,128)(2,1)} %bitcast.29), custom_call_target="tpu_custom_call" | custom-call | tf_op jit(solution)/shard_map/project/pallas_call | solution.py:229
  91.8 15.8 %all_to_all.15.stats = f32[32,24,128]{2,1,0:T(8,128)} all-to-all(f32[32,24,128]{2,1,0:T(8,128)} %get-tuple-element.26), channel_id=1, replica_groups=mesh['y'=4,'x'=4,'c'=2,'mp'=8] {'y','x','c'}, dimensions={0} | all-to-all | bytes 786432 | tf_op jit(solution)/shard_map/all_to_all | solution.py:256
  107.6 6.7 %attend.1 = (bf16[896,512]{1,0:T(8,128)(2,1)}, bf16[512,896]{1,0:T(8,128)(2,1)}, bf16[32,128,512]{2,1,0:T(8,128)(2,1)}) custom-call(s32[7]{0:T(128)} %bins.3, s32[7]{0:T(128)} %docs.3, s32[32,4]{1,0:T(8,128)} %bitcast.36, bf16[896,512]{1,0:T(8,128)(2,1)} %get-tuple-element.24.kv, bf16[7,128,512]{2,1,0:T(8,128)(2,1)} %get-tuple-element.25.qc, ...), custom_call_target="tpu_custom_call" | custom-call | tf_op jit(solution)/shard_map/attend/pallas_call | solution.py:258
  114.2 8.2 %row_terms.1 = bf16[8,896,512]{2,1,0:T(8,128)(2,1)} custom-call(bf16[896,512]{1,0:T(8,128)(2,1)} %get-tuple-element.31.grads, bf16[32,384,512]{2,1,0:T(8,128)(2,1)} %bitcast.30), custom_call_target="tpu_custom_call" | custom-call | flops 3758096384 | bytes 16777216 | tf_op jit(solution)/shard_map/row_terms/pallas_call | solution.py:278
  122.5 4.9 %all-to-all-start.2 = ((bf16[32,128,512]{2,1,0:T(8,128)(2,1)}), bf16[32,128,512]{2,1,0:T(8,128)(2,1)}, u32[]{:S(2)}, u32[]{:S(2)}) async-start(bf16[32,128,512]{2,1,0:T(8,128)(2,1)} %get-tuple-element.28), calls=%async_computation.2 | async-start | bytes 8388608 | tf_op jit(solution)/shard_map/all_to_all | solution.py:276
  127.3 8.9 %weight_terms.1 = (bf16[16,512,128]{2,1,0:T(8,128)(2,1)}, bf16[16,512,128]{2,1,0:T(8,128)(2,1)}) custom-call(bf16[512,896]{1,0:T(8,128)(2,1)} %get-tuple-element.32.grads_t, bf16[896,4096]{1,0:T(8,128)(2,1)} %e.3), custom_call_target="tpu_custom_call" | custom-call | flops 3758096384 | bytes 16777216 | tf_op jit(solution)/shard_map/weight_terms/pallas_call | solution.py:294
  136.2 4.4 %collective-permute-done = bf16[16,512,128]{2,1,0:T(8,128)(2,1)S(1)} collective-permute-done((bf16[16,512,128]{2,1,0:T(8,128)(2,1)}, bf16[16,512,128]{2,1,0:T(8,128)(2,1)S(1)}, u32[]{:S(2)}, u32[]{:S(2)}) %collective-permute-start) | collective-permute-done | bytes 2097184 | tf_op jit(solution)/shard_map/ppermute | solution.py:307
  140.6 1.4 copy-done
  142.0 2.8 %add_convert_fusion = bf16[16,512,128]{2,1,0:T(8,128)(2,1)S(1)} fusion(bf16[16,512,128]{2,1,0:T(8,128)(2,1)} %copy-done, bf16[16,512,128]{2,1,0:T(8,128)(2,1)} %get-tuple-element.33), kind=kLoop, calls=%fused_computation | loop fusion | flops 4194304 | bytes 6291456 | tf_op jit(solution)/shard_map/convert_element_type | solution.py:308
  144.9 3.0 %collective-permute-start.2 = (bf16[4,512,128]{2,1,0:T(8,128)(2,1)S(1)}, bf16[4,512,128]{2,1,0:T(8,128)(2,1)}, u32[]{:S(2)}, u32[]{:S(2)}) collective-permute-start(bf16[4,512,128]{2,1,0:T(8,128)(2,1)S(1)} %get-tuple-element.38), channel_id=1, source_target_pairs={{0,48},{16,0},{32,16},{48,32},{1,49},{17,1},{33,17},{49,33},{2,50}... | collective-permute-start | bytes 1572872 | tf_op jit(solution)/shard_map/ppermute | solution.py:187
  148.6 2.3 collective-permute-start.4
  152.2 43.8 %collective-permute-done.4 = bf16[4,256,128]{2,1,0:T(8,128)(2,1)} collective-permute-done((bf16[4,256,128]{2,1,0:T(8,128)(2,1)}, bf16[4,256,128]{2,1,0:T(8,128)(2,1)}, u32[]{:S(2)}, u32[]{:S(2)}) %collective-permute-start.4) | collective-permute-done | bytes 262176 | tf_op jit(solution)/shard_map/ppermute | solution.py:187
  196.0 5.1 %collective-permute-done.3 = bf16[4,256,128]{2,1,0:T(8,128)(2,1)} collective-permute-done((bf16[4,256,128]{2,1,0:T(8,128)(2,1)S(1)}, bf16[4,256,128]{2,1,0:T(8,128)(2,1)}, u32[]{:S(2)}, u32[]{:S(2)}) %collective-permute-start.3) | collective-permute-done | bytes 262176 | tf_op jit(solution)/shard_map/ppermute | solution.py:187
  201.1 1.6 fusion.2
  202.8 3.2 %collective-permute-start.6 = (bf16[512,128]{1,0:T(8,128)(2,1)S(1)}, bf16[512,128]{1,0:T(8,128)(2,1)S(1)}, u32[]{:S(2)}, u32[]{:S(2)}) collective-permute-start(bf16[512,128]{1,0:T(8,128)(2,1)S(1)} %get-tuple-element.43), channel_id=1, source_target_pairs={{0,192},{64,0},{128,64},{192,128},{1,193},{65,1},{129,65},{193,129... | collective-permute-start | bytes 393224 | tf_op jit(solution)/shard_map/ppermute | solution.py:187
  206.0 1.6 collective-permute-start.8
  207.7 2.0 collective-permute-start.7
  209.6 3.1 %collective-permute-done.8 = bf16[256,128]{1,0:T(8,128)(2,1)S(1)} collective-permute-done((bf16[256,128]{1,0:T(8,128)(2,1)S(1)}, bf16[256,128]{1,0:T(8,128)(2,1)S(1)}, u32[]{:S(2)}, u32[]{:S(2)}) %collective-permute-start.8) | collective-permute-done | bytes 65568 | tf_op jit(solution)/shard_map/ppermute | solution.py:187
  215.5 1.7 turn.1
  217.2 6.2 %collect.1 = (bf16[256,256]{1,0:T(8,128)(2,1)}, bf16[256,256]{1,0:T(8,128)(2,1)}) custom-call(s32[32]{0:T(128)} %fusion.8.docs, s32[1,4]{1,0:T(1,128)} %lengths.1, bf16[32,128,512]{2,1,0:T(8,128)(2,1)} %all-to-all-done.2.windows), custom_call_target="tpu_custom_call" | custom-call | tf_op jit(solution)/shard_map/collect/pallas_call | solution.py:319
  (29 shorter events, 8.7 us)
Async XLA Ops:
  7.2 72.7 %all-gather.3.cloned.1.call-start = ((), (), s32[]{:S(2)}) async-start(), calls=%async_computation.5 | async-start | bytes 12976128 | tf_op jit(solution)/shard_map/all_gather | solution.py:214
  11.0 14.6 %all-to-all-start = ((s32[32,1,12]{2,1,0:T(1,128)}), s32[32,1,12]{2,1,0:T(1,128)S(1)}, u32[]{:S(2)}, u32[]{:S(2)}) async-start(s32[32,1,12]{2,1,0:T(1,128)} %broadcast_in_dim.5), calls=%async_computation | async-start | bytes 32768 | tf_op jit(solution)/shard_map/all_to_all | solution.py:218
  18.4 205.0 %reduce-scatter.2.cloned.1.call-start = ((), (), s32[]{:S(2)}) async-start(), calls=%async_computation.4 | async-start | bytes 8257536 | tf_op jit(solution)/shard_map/reduce_scatter | solution.py:291
  25.6 55.0 %copy-start.1 = (s32[32,1,12]{2,1,0:T(1,128)}, s32[32,1,12]{2,1,0:T(1,128)S(1)}, u32[]{:S(2)}) copy-start(s32[32,1,12]{2,1,0:T(1,128)S(1)} %all-to-all-done) | copy-start | bytes 4612
  122.5 94.7 %all-to-all-start.2 = ((bf16[32,128,512]{2,1,0:T(8,128)(2,1)}), bf16[32,128,512]{2,1,0:T(8,128)(2,1)}, u32[]{:S(2)}, u32[]{:S(2)}) async-start(bf16[32,128,512]{2,1,0:T(8,128)(2,1)} %get-tuple-element.28), calls=%async_computation.2 | async-start | bytes 8388608 | tf_op jit(solution)/shard_map/all_to_all | solution.py:276
  136.2 4.4 %collective-permute-start = (bf16[16,512,128]{2,1,0:T(8,128)(2,1)}, bf16[16,512,128]{2,1,0:T(8,128)(2,1)S(1)}, u32[]{:S(2)}, u32[]{:S(2)}) collective-permute-start(bf16[16,512,128]{2,1,0:T(8,128)(2,1)} %get-tuple-element.34), channel_id=1, source_target_pairs={{0,8},{8,0},{1,9},{9,1},{2,10},{10,2},{3,11},{11,3},{4,12},{12,4},... | collective-permute-start | bytes 6291464 | tf_op jit(solution)/shard_map/ppermute | solution.py:307
  140.6 1.4 copy-start
  144.9 56.2 %collective-permute-start.2 = (bf16[4,512,128]{2,1,0:T(8,128)(2,1)S(1)}, bf16[4,512,128]{2,1,0:T(8,128)(2,1)}, u32[]{:S(2)}, u32[]{:S(2)}) collective-permute-start(bf16[4,512,128]{2,1,0:T(8,128)(2,1)S(1)} %get-tuple-element.38), channel_id=1, source_target_pairs={{0,48},{16,0},{32,16},{48,32},{1,49},{17,1},{33,17},{49,33},{2,50}... | collective-permute-start | bytes 1572872 | tf_op jit(solution)/shard_map/ppermute | solution.py:187
  147.9 53.2 %collective-permute-start.1 = (bf16[4,512,128]{2,1,0:T(8,128)(2,1)S(1)}, bf16[4,512,128]{2,1,0:T(8,128)(2,1)}, u32[]{:S(2)}, u32[]{:S(2)}) collective-permute-start(bf16[4,512,128]{2,1,0:T(8,128)(2,1)S(1)} %get-tuple-element.39), channel_id=1, source_target_pairs={{0,16},{16,32},{32,48},{48,0},{1,17},{17,33},{33,49},{49,1},{2,18}... | collective-permute-start | bytes 1572872 | tf_op jit(solution)/shard_map/ppermute | solution.py:187
  148.6 47.3 %collective-permute-start.4 = (bf16[4,256,128]{2,1,0:T(8,128)(2,1)}, bf16[4,256,128]{2,1,0:T(8,128)(2,1)}, u32[]{:S(2)}, u32[]{:S(2)}) collective-permute-start(bf16[4,256,128]{2,1,0:T(8,128)(2,1)} %get-tuple-element.45), channel_id=1, source_target_pairs={{0,32},{16,48},{32,0},{48,16},{1,33},{17,49},{33,1},{49,17},{2,34}... | collective-permute-start | bytes 786440 | tf_op jit(solution)/shard_map/ppermute | solution.py:187
  150.9 50.2 %collective-permute-start.3 = (bf16[4,256,128]{2,1,0:T(8,128)(2,1)S(1)}, bf16[4,256,128]{2,1,0:T(8,128)(2,1)}, u32[]{:S(2)}, u32[]{:S(2)}) collective-permute-start(bf16[4,256,128]{2,1,0:T(8,128)(2,1)S(1)} %get-tuple-element.44), channel_id=1, source_target_pairs={{0,32},{16,48},{32,0},{48,16},{1,33},{17,49},{33,1},{49,17},{2,34}... | collective-permute-start | bytes 786440 | tf_op jit(solution)/shard_map/ppermute | solution.py:187
  202.8 10.7 %collective-permute-start.6 = (bf16[512,128]{1,0:T(8,128)(2,1)S(1)}, bf16[512,128]{1,0:T(8,128)(2,1)S(1)}, u32[]{:S(2)}, u32[]{:S(2)}) collective-permute-start(bf16[512,128]{1,0:T(8,128)(2,1)S(1)} %get-tuple-element.43), channel_id=1, source_target_pairs={{0,192},{64,0},{128,64},{192,128},{1,193},{65,1},{129,65},{193,129... | collective-permute-start | bytes 393224 | tf_op jit(solution)/shard_map/ppermute | solution.py:187
  206.0 8.8 %collective-permute-start.5 = (bf16[512,128]{1,0:T(8,128)(2,1)S(1)}, bf16[512,128]{1,0:T(8,128)(2,1)S(1)}, u32[]{:S(2)}, u32[]{:S(2)}) collective-permute-start(bf16[512,128]{1,0:T(8,128)(2,1)S(1)} %get-tuple-element.42), channel_id=1, source_target_pairs={{0,64},{64,128},{128,192},{192,0},{1,65},{65,129},{129,193},{193,1... | collective-permute-start | bytes 393224 | tf_op jit(solution)/shard_map/ppermute | solution.py:187
  206.0 6.7 %collective-permute-start.8 = (bf16[256,128]{1,0:T(8,128)(2,1)S(1)}, bf16[256,128]{1,0:T(8,128)(2,1)S(1)}, u32[]{:S(2)}, u32[]{:S(2)}) collective-permute-start(bf16[256,128]{1,0:T(8,128)(2,1)S(1)} %get-tuple-element.41), channel_id=1, source_target_pairs={{0,128},{64,192},{128,0},{192,64},{1,129},{65,193},{129,1},{193,65... | collective-permute-start | bytes 196616 | tf_op jit(solution)/shard_map/ppermute | solution.py:187
  207.7 5.8 %collective-permute-start.7 = (bf16[256,128]{1,0:T(8,128)(2,1)S(1)}, bf16[256,128]{1,0:T(8,128)(2,1)S(1)}, u32[]{:S(2)}, u32[]{:S(2)}) collective-permute-start(bf16[256,128]{1,0:T(8,128)(2,1)S(1)} %get-tuple-element.40), channel_id=1, source_target_pairs={{0,128},{64,192},{128,0},{192,64},{1,129},{65,193},{129,1},{193,65... | collective-permute-start | bytes 196616 | tf_op jit(solution)/shard_map/ppermute | solution.py:187
Sparse Core Ops, SparseCore 0:
  11.1 68.6 all-gather.2
  122.6 80.8 reduce-scatter.1

commit v6 on v4

--- a/solution.py
+++ b/solution.py
@@ -47,16 +47,29 @@
     return scores, raw, lax.broadcasted_iota(jnp.int32, scores.shape, 1) < last - first
 
 
-def project_kernel(bins, docs, lengths, e, w, tokens, kv, qc, shared, acc, fetched, stats, sems):
+def project_kernel(bins, docs, lengths, e, w, near, far, kv, qc, shared, acc, fetched, stats, sems):
     step = pl.program_id(0)
 
-    def fetch(b):
-        return pltpu.make_async_copy(tokens.at[bins[b], 128:384, :], fetched.at[b], sems.at[b])
+    core = lax.axis_index("c")
+
+    def fetch(b, held, do):
+        j = bins[b]
+        back_x = lax.rem(lax.axis_index("x") + 4 - lax.rem(lax.div(j, 2), 4), 4)
+        back_y = lax.rem(lax.axis_index("y") + 4 - lax.div(j, 8), 4)
+        do(pltpu.make_async_copy(held.at[0, back_x, back_y], fetched.at[b, :WIN, :], sems.at[b, 0]))
+        do(pltpu.make_async_copy(held.at[1, back_y, back_x], fetched.at[b, WIN:, :], sems.at[b, 1]))
 
     @pl.when(step == 0)
     def _():
         for b in range(EBLK):
-            fetch(b).start()
+
+            @pl.when(lax.rem(bins[b], 2) == core)
+            def _():
+                fetch(b, near, lambda copy: copy.start())
+
+            @pl.when(lax.rem(bins[b], 2) != core)
+            def _():
+                fetch(b, far, lambda copy: copy.start())
 
     part = jnp.dot(e[...], w[...].reshape(-1, 2 * HD), preferred_element_type=f32)
 
@@ -73,7 +86,7 @@
         kv[...] = acc[...].astype(bf16)
         stats[...] = jnp.zeros_like(stats)
         for b in range(EBLK):
-            fetch(b).wait()
+            fetch(b, near, lambda copy: copy.wait())
             first, _ = token_range(b, bins, docs, lengths)
             turned = pltpu.roll(fetched[b].astype(f32), lax.rem(2 * WIN - first, 2 * WIN), 0)
             qc[b] = turned[:WIN].astype(bf16)
@@ -179,17 +192,27 @@
     return jax.ShapeDtypeStruct(dims, dtype)
 
 
+def gather_ring(v, axis):
+    def send(part, distance):
+        return lax.ppermute(part, axis, [(i, (i + distance) % 4) for i in range(4)])
+
+    half = v.shape[-2] // 2
+    across = jnp.concatenate([send(v[..., :half, :], 2), send(v[..., half:, :], -2)], axis=-2)
+    return jnp.stack([v, send(v, 1), across, send(v, -1)])
+
+
 def per_device(queries, context_grad, encoder_rows, key_weight, value_weight, document_lengths, block_bin, block_document):
     rows, width = encoder_rows.shape
     tokens = queries.shape[0]
-    packed = jnp.concatenate(
+    gathered = lax.all_gather(jnp.concatenate([key_weight, value_weight], axis=1), DP, axis=0, tiled=False)
+    own_tokens = jnp.concatenate([queries, context_grad], axis=1)
+    near_tokens = jnp.stack(
         [
-            jnp.concatenate([key_weight, value_weight], axis=1),
-            jnp.concatenate([queries, context_grad], axis=1),
-        ],
-        axis=0,
+            gather_ring(gather_ring(own_tokens[:WIN], "y"), "x"),
+            gather_ring(gather_ring(own_tokens[WIN:], "x"), "y"),
+        ]
     )
-    gathered = lax.all_gather(packed, DP, axis=0, tiled=False)
+    far_tokens = lax.ppermute(near_tokens, "c", [(0, 1), (1, 0)])
 
     def share(v):
         spread_out = jnp.broadcast_to(v[None], (BINS, *v.shape))
@@ -214,6 +237,7 @@
             pl.BlockSpec((rows, 1024), lambda k: (0, k)),
             pl.BlockSpec((8, 128, 2 * HD), lambda k: (k, 0, 0)),
             ANY,
+            ANY,
         ],
         out_specs=[
             pl.BlockSpec((rows, 2 * HD), lambda k: (0, 0)),
@@ -225,11 +249,11 @@
             pltpu.VMEM((rows, 2 * HD), f32),
             pltpu.VMEM((EBLK, tokens, 2 * HD), bf16),
             pltpu.VMEM((24, WIN), f32),
-            pltpu.SemaphoreType.DMA((EBLK,)),
+            pltpu.SemaphoreType.DMA((EBLK, 2)),
         ],
         compiler_params=params(),
         name="project",
-    )(block_bin, block_document, lengths, encoder_rows, gathered, gathered)
+    )(block_bin, block_document, lengths, encoder_rows, gathered, near_tokens, far_tokens)
 
     all_stats = lax.all_to_all(stats, DP, split_axis=0, concat_axis=0, tiled=True)
 

time: 226 us -> 231 us (1.022)
  starting transfers between devices: 16.1 us -> 37.9 us
  waiting for transfers between devices: 126 us -> 108 us
    all_gather x1, waiting for transfers between devices: 53.4 us -> 0.01 us  [per_device(): lax.all_gather(jnp.concatenate([key_weight, value_weight], axis=1), DP, a...]
    ppermute x0 -> x17, waiting for transfers between devices: none -> 35.6 us  [the longest x16 35.6 us: send(): return lax.ppermute(part, axis, [(i, (i + distance) % 4) for i in range(4)])]
    ppermute x0 -> x17, starting transfers between devices: none -> 25.3 us  [the longest x16 25.3 us: send(): return lax.ppermute(part, axis, [(i, (i + distance) % 4) for i in range(4)])]
    all_to_all x1, starting transfers between devices: 7.32 us -> 3.83 us  [share(): lax.all_to_all(spread_out, DP, split_axis=0, concat_axis=0, tiled=True)]
    another operation x0 -> x9, other arithmetic: none -> 3.12 us  [the longest x3 2.85 us: per_device(): jnp.stack([gather_ring(gather_ring(own_tokens[:WIN], 'y'), 'x'), gather_r...]
  transfers between devices with their start and end apart: 6 -> 23, of which waited for: 5 -> 11; matrix products, arithmetic and copies ran while one was open for 4% -> 5% of each run, Pallas kernels for 7% -> 6%
where the time goes in v6:
time: 231 us; the launch traced here: 230 us
  waiting for transfers between devices  108 us (47%)
  Pallas kernels  40.6 us (18%)
  starting transfers between devices  37.9 us (16%)
  blocking collectives  14.9 us (6%)
  between operations  14.3 us (6%)
  other arithmetic  9.3 us (4%)
  local copies, waits for them, and re-layouts  4.86 us (2%)
    all_to_all x1, waiting for transfers between devices, per_device(): windows = lax.all_to_all(slots, DP, split_axis=0, concat_axis=0, tiled=True)  37 us
    ppermute x16, waiting for transfers between devices, send(): return lax.ppermute(part, axis, [(i, (i + distance) % 4) for i in range(4)])  35.6 us
    ppermute x16, starting transfers between devices, send(): return lax.ppermute(part, axis, [(i, (i + distance) % 4) for i in range(4)])  25.3 us
    all_to_all x1, waiting for transfers between devices, per_device(): lax.all_to_all(pair_sums, PLANE, split_axis=0, concat_axis=0, tiled=True)  23.9 us
    all_to_all x1, blocking collectives, per_device(): lax.all_to_all(stats, DP, split_axis=0, concat_axis=0, tiled=True)  14.9 us
    pallas_call x1, Pallas kernels, per_device(): pl.pallas_call(project_kernel, grid=(4,), in_specs=[SMEM, SMEM, SMEM, pl....  11.1 us
    pallas_call x1, Pallas kernels, per_device(): pl.pallas_call(weights_kernel, grid=(4,), in_specs=[pl.BlockSpec((2 * HD,...  8.56 us
    pallas_call x1, Pallas kernels, per_device(): pl.pallas_call(rows_kernel, grid=(4,), in_specs=[pl.BlockSpec((rows, 2 *...  8.2 us
  transfers between devices with their start and end apart: 23, of which 11 were waited for; matrix products, arithmetic and copies ran while one was open for 5% of the time, Pallas kernels for 6%

profile of v6, /device:TPU:192, one launch (start us, length us, event | category | flops | bytes accessed | tf_op | source)
XLA Modules:
  0.0 229.8 jit_solution(2069391165864572757)
XLA Ops:
  10.6 3.1 %collective-permute-start.10 = (bf16[64,512]{1,0:T(8,128)(2,1)S(1)}, bf16[64,512]{1,0:T(8,128)(2,1)S(1)}, u32[]{:S(2)}, u32[]{:S(2)}) collective-permute-start(bf16[64,512]{1,0:T(8,128)(2,1)S(1)} %get-tuple-element.55), channel_id=1, source_target_pairs={{0,32},{16,48},{32,0},{48,16},{1,33},{17,49},{33,1},{49,17},{2,34}... | collective-permute-start | bytes 196616 | tf_op jit(solution)/shard_map/ppermute | solution.py:197
  14.3 2.8 %collective-permute-start.11 = (bf16[128,512]{1,0:T(8,128)(2,1)S(1)}, bf16[128,512]{1,0:T(8,128)(2,1)S(1)}, u32[]{:S(2)}, u32[]{:S(2)}) collective-permute-start(bf16[128,512]{1,0:T(8,128)(2,1)S(1)} %get-tuple-element.52), channel_id=1, source_target_pairs={{0,48},{16,0},{32,16},{48,32},{1,49},{17,1},{33,17},{49,33},{2,50}... | collective-permute-start | bytes 393224 | tf_op jit(solution)/shard_map/ppermute | solution.py:197
  17.1 3.0 %collective-permute-start.3 = (bf16[128,512]{1,0:T(8,128)(2,1)S(1)}, bf16[128,512]{1,0:T(8,128)(2,1)S(1)}, u32[]{:S(2)}, u32[]{:S(2)}) collective-permute-start(bf16[128,512]{1,0:T(8,128)(2,1)S(1)} %get-tuple-element.53), channel_id=1, source_target_pairs={{0,192},{64,0},{128,64},{192,128},{1,193},{65,1},{129,65},{193,129... | collective-permute-start | bytes 393224 | tf_op jit(solution)/shard_map/ppermute | solution.py:197
  20.8 2.9 %collective-permute-start.1 = (bf16[64,512]{1,0:T(8,128)(2,1)S(1)}, bf16[64,512]{1,0:T(8,128)(2,1)S(1)}, u32[]{:S(2)}, u32[]{:S(2)}) collective-permute-start(bf16[64,512]{1,0:T(8,128)(2,1)S(1)} %get-tuple-element.54), channel_id=1, source_target_pairs={{0,128},{64,192},{128,0},{192,64},{1,129},{65,193},{129,1},{193,65... | collective-permute-start | bytes 196616 | tf_op jit(solution)/shard_map/ppermute | solution.py:197
  26.9 4.1 %collective-permute-start.14 = (bf16[4,64,512]{2,1,0:T(8,128)(2,1)S(1)}, bf16[4,64,512]{2,1,0:T(8,128)(2,1)S(1)}, u32[]{:S(2)}, u32[]{:S(2)}) collective-permute-start(bf16[4,64,512]{2,1,0:T(8,128)(2,1)S(1)} %get-tuple-element.49), channel_id=1, source_target_pairs={{0,128},{64,192},{128,0},{192,64},{1,129},{65,193},{129,1},{193,65... | collective-permute-start | bytes 786440 | tf_op jit(solution)/shard_map/ppermute | solution.py:197
  31.1 10.5 %collective-permute-done = bf16[128,512]{1,0:T(8,128)(2,1)S(1)} collective-permute-done((bf16[128,512]{1,0:T(8,128)(2,1)S(1)}, bf16[128,512]{1,0:T(8,128)(2,1)S(1)}, u32[]{:S(2)}, u32[]{:S(2)}) %collective-permute-start) | collective-permute-done | bytes 131104 | tf_op jit(solution)/shard_map/ppermute | solution.py:197
  49.6 2.9 %collective-permute-done.6 = bf16[4,64,512]{2,1,0:T(8,128)(2,1)S(1)} collective-permute-done((bf16[4,64,512]{2,1,0:T(8,128)(2,1)S(1)}, bf16[4,64,512]{2,1,0:T(8,128)(2,1)S(1)}, u32[]{:S(2)}, u32[]{:S(2)}) %collective-permute-start.6) | collective-permute-done | bytes 262176 | tf_op jit(solution)/shard_map/ppermute | solution.py:197
  52.6 5.0 %collective-permute-done.5 = bf16[4,64,512]{2,1,0:T(8,128)(2,1)S(1)} collective-permute-done((bf16[4,64,512]{2,1,0:T(8,128)(2,1)S(1)}, bf16[4,64,512]{2,1,0:T(8,128)(2,1)S(1)}, u32[]{:S(2)}, u32[]{:S(2)}) %collective-permute-start.5) | collective-permute-done | bytes 262176 | tf_op jit(solution)/shard_map/ppermute | solution.py:197
  58.0 11.0 %collective-permute-done.7 = bf16[4,128,512]{2,1,0:T(8,128)(2,1)S(1)} collective-permute-done((bf16[4,128,512]{2,1,0:T(8,128)(2,1)S(1)}, bf16[4,128,512]{2,1,0:T(8,128)(2,1)S(1)}, u32[]{:S(2)}, u32[]{:S(2)}) %collective-permute-start.7) | collective-permute-done | bytes 524320 | tf_op jit(solution)/shard_map/ppermute | solution.py:197
  69.0 3.3 %collective-permute-done.4 = bf16[4,128,512]{2,1,0:T(8,128)(2,1)S(1)} collective-permute-done((bf16[4,128,512]{2,1,0:T(8,128)(2,1)S(1)}, bf16[4,128,512]{2,1,0:T(8,128)(2,1)S(1)}, u32[]{:S(2)}, u32[]{:S(2)}) %collective-permute-start.4) | collective-permute-done | bytes 524320 | tf_op jit(solution)/shard_map/ppermute | solution.py:197
  75.6 3.8 %all-to-all-start = ((s32[32,1,12]{2,1,0:T(1,128)}), s32[32,1,12]{2,1,0:T(1,128)S(1)}, u32[]{:S(2)}, u32[]{:S(2)}) async-start(s32[32,1,12]{2,1,0:T(1,128)} %broadcast_in_dim.5), calls=%async_computation | async-start | bytes 32768 | tf_op jit(solution)/shard_map/all_to_all | solution.py:219
  79.5 7.2 %all-to-all-done = s32[32,1,12]{2,1,0:T(1,128)S(1)} async-done(((s32[32,1,12]{2,1,0:T(1,128)}), s32[32,1,12]{2,1,0:T(1,128)S(1)}, u32[]{:S(2)}, u32[]{:S(2)}) %all-to-all-start) | async-done | bytes 1568 | tf_op jit(solution)/shard_map/all_to_all | solution.py:219
  88.3 11.1 %project.1 = (bf16[896,512]{1,0:T(8,128)(2,1)}, bf16[7,128,512]{2,1,0:T(8,128)(2,1)}, f32[32,24,128]{2,1,0:T(8,128)}) custom-call(s32[7]{0:T(128)} %bins.3, s32[7]{0:T(128)} %docs.3, s32[32,4]{1,0:T(8,128)} %bitcast.43, bf16[896,4096]{1,0:T(8,128)(2,1)} %e.3, bf16[32,128,512]{2,1,0:T(8,128)(2,1)} %bitcast.34, ...), custom_call_target="tpu_custom_call" | custom-call | tf_op jit(solution)/shard_map/project/pallas_call | solution.py:230
  99.4 14.9 %all_to_all.20.stats = f32[32,24,128]{2,1,0:T(8,128)} all-to-all(f32[32,24,128]{2,1,0:T(8,128)} %get-tuple-element.26), channel_id=1, replica_groups=mesh['y'=4,'x'=4,'c'=2,'mp'=8] {'y','x','c'}, dimensions={0} | all-to-all | bytes 786432 | tf_op jit(solution)/shard_map/all_to_all | solution.py:258
  114.3 6.5 %attend.1 = (bf16[896,512]{1,0:T(8,128)(2,1)}, bf16[512,896]{1,0:T(8,128)(2,1)}, bf16[32,128,512]{2,1,0:T(8,128)(2,1)}) custom-call(s32[7]{0:T(128)} %bins.3, s32[7]{0:T(128)} %docs.3, s32[32,4]{1,0:T(8,128)} %bitcast.44, bf16[896,512]{1,0:T(8,128)(2,1)} %get-tuple-element.24.kv, bf16[7,128,512]{2,1,0:T(8,128)(2,1)} %get-tuple-element.25.qc, ...), custom_call_target="tpu_custom_call" | custom-call | tf_op jit(solution)/shard_map/attend/pallas_call | solution.py:260
  120.8 8.2 %row_terms.1 = bf16[8,896,512]{2,1,0:T(8,128)(2,1)} custom-call(bf16[896,512]{1,0:T(8,128)(2,1)} %get-tuple-element.35.grads, bf16[32,128,512]{2,1,0:T(8,128)(2,1)} %bitcast.35), custom_call_target="tpu_custom_call" | custom-call | flops 3758096384 | bytes 16777216 | tf_op jit(solution)/shard_map/row_terms/pallas_call | solution.py:280
  129.0 4.9 %all-to-all-start.2 = ((bf16[32,128,512]{2,1,0:T(8,128)(2,1)}), bf16[32,128,512]{2,1,0:T(8,128)(2,1)}, u32[]{:S(2)}, u32[]{:S(2)}) async-start(bf16[32,128,512]{2,1,0:T(8,128)(2,1)} %get-tuple-element.28), calls=%async_computation.2 | async-start | bytes 8388608 | tf_op jit(solution)/shard_map/all_to_all | solution.py:278
  133.9 8.6 %weight_terms.1 = (bf16[16,512,128]{2,1,0:T(8,128)(2,1)}, bf16[16,512,128]{2,1,0:T(8,128)(2,1)}) custom-call(bf16[512,896]{1,0:T(8,128)(2,1)} %get-tuple-element.29.grads_t, bf16[896,4096]{1,0:T(8,128)(2,1)} %e.3), custom_call_target="tpu_custom_call" | custom-call | flops 3758096384 | bytes 16777216 | tf_op jit(solution)/shard_map/weight_terms/pallas_call | solution.py:296
  142.6 4.3 %collective-permute-done.17 = bf16[16,512,128]{2,1,0:T(8,128)(2,1)S(1)} collective-permute-done((bf16[16,512,128]{2,1,0:T(8,128)(2,1)}, bf16[16,512,128]{2,1,0:T(8,128)(2,1)S(1)}, u32[]{:S(2)}, u32[]{:S(2)}) %collective-permute-start.17) | collective-permute-done | bytes 2097184 | tf_op jit(solution)/shard_map/ppermute | solution.py:309
  146.8 3.5 %add_convert_fusion = bf16[16,512,128]{2,1,0:T(8,128)(2,1)} fusion(bf16[16,512,128]{2,1,0:T(8,128)(2,1)S(1)} %collective-permute-done.17, bf16[16,512,128]{2,1,0:T(8,128)(2,1)} %get-tuple-element.30), kind=kLoop, calls=%fused_computation.1 | loop fusion | flops 4194304 | bytes 6291456 | tf_op jit(solution)/shard_map/convert_element_type | solution.py:310
  150.3 37.0 %all-to-all-done.2.windows = bf16[32,128,512]{2,1,0:T(8,128)(2,1)} async-done(((bf16[32,128,512]{2,1,0:T(8,128)(2,1)}), bf16[32,128,512]{2,1,0:T(8,128)(2,1)}, u32[]{:S(2)}, u32[]{:S(2)}) %all-to-all-start.2) | async-done | bytes 4194336 | tf_op jit(solution)/shard_map/all_to_all | solution.py:278
  187.4 3.7 %all-to-all-start.3 = ((bf16[16,512,128]{2,1,0:T(8,128)(2,1)}), bf16[16,512,128]{2,1,0:T(8,128)(2,1)S(1)}, u32[]{:S(2)}, u32[]{:S(2)}) async-start(bf16[16,512,128]{2,1,0:T(8,128)(2,1)} %add_convert_fusion), calls=%async_computation.4 | async-start | bytes 4194304 | tf_op jit(solution)/shard_map/all_to_all | solution.py:312
  191.1 6.2 %collect.1 = (bf16[256,256]{1,0:T(8,128)(2,1)}, bf16[256,256]{1,0:T(8,128)(2,1)}) custom-call(s32[32]{0:T(128)} %fusion.2.docs, s32[1,4]{1,0:T(1,128)} %lengths.1, bf16[32,128,512]{2,1,0:T(8,128)(2,1)} %all-to-all-done.2.windows), custom_call_target="tpu_custom_call" | custom-call | tf_op jit(solution)/shard_map/collect/pallas_call | solution.py:314
  197.3 23.9 %all-to-all-done.3 = bf16[16,512,128]{2,1,0:T(8,128)(2,1)S(1)} async-done(((bf16[16,512,128]{2,1,0:T(8,128)(2,1)}), bf16[16,512,128]{2,1,0:T(8,128)(2,1)S(1)}, u32[]{:S(2)}, u32[]{:S(2)}) %all-to-all-start.3) | async-done | bytes 2097184 | tf_op jit(solution)/shard_map/all_to_all | solution.py:312
  (65 shorter events, 23.0 us)
Async XLA Ops:
  7.2 80.4 %all-gather.3.cloned.1.call-start = ((), (), s32[]{:S(2)}) async-start(), calls=%async_computation.6 | async-start | bytes 4325376 | tf_op jit(solution)/shard_map/all_gather | solution.py:207
  10.6 9.5 %collective-permute-start.10 = (bf16[64,512]{1,0:T(8,128)(2,1)S(1)}, bf16[64,512]{1,0:T(8,128)(2,1)S(1)}, u32[]{:S(2)}, u32[]{:S(2)}) collective-permute-start(bf16[64,512]{1,0:T(8,128)(2,1)S(1)} %get-tuple-element.55), channel_id=1, source_target_pairs={{0,32},{16,48},{32,0},{48,16},{1,33},{17,49},{33,1},{49,17},{2,34}... | collective-permute-start | bytes 196616 | tf_op jit(solution)/shard_map/ppermute | solution.py:197
  13.7 7.0 %collective-permute-start.9 = (bf16[64,512]{1,0:T(8,128)(2,1)S(1)}, bf16[64,512]{1,0:T(8,128)(2,1)S(1)}, u32[]{:S(2)}, u32[]{:S(2)}) collective-permute-start(bf16[64,512]{1,0:T(8,128)(2,1)S(1)} %get-tuple-element.56), channel_id=1, source_target_pairs={{0,32},{16,48},{32,0},{48,16},{1,33},{17,49},{33,1},{49,17},{2,34}... | collective-permute-start | bytes 196616 | tf_op jit(solution)/shard_map/ppermute | solution.py:197
  14.3 12.4 %collective-permute-start.11 = (bf16[128,512]{1,0:T(8,128)(2,1)S(1)}, bf16[128,512]{1,0:T(8,128)(2,1)S(1)}, u32[]{:S(2)}, u32[]{:S(2)}) collective-permute-start(bf16[128,512]{1,0:T(8,128)(2,1)S(1)} %get-tuple-element.52), channel_id=1, source_target_pairs={{0,48},{16,0},{32,16},{48,32},{1,49},{17,1},{33,17},{49,33},{2,50}... | collective-permute-start | bytes 393224 | tf_op jit(solution)/shard_map/ppermute | solution.py:197
  17.1 9.6 %collective-permute-start.8 = (bf16[128,512]{1,0:T(8,128)(2,1)S(1)}, bf16[128,512]{1,0:T(8,128)(2,1)S(1)}, u32[]{:S(2)}, u32[]{:S(2)}) collective-permute-start(bf16[128,512]{1,0:T(8,128)(2,1)S(1)} %get-tuple-element.52), channel_id=1, source_target_pairs={{0,16},{16,32},{32,48},{48,0},{1,17},{17,33},{33,49},{49,1},{2,18}... | collective-permute-start | bytes 393224 | tf_op jit(solution)/shard_map/ppermute | solution.py:197
  17.1 13.9 %collective-permute-start.3 = (bf16[128,512]{1,0:T(8,128)(2,1)S(1)}, bf16[128,512]{1,0:T(8,128)(2,1)S(1)}, u32[]{:S(2)}, u32[]{:S(2)}) collective-permute-start(bf16[128,512]{1,0:T(8,128)(2,1)S(1)} %get-tuple-element.53), channel_id=1, source_target_pairs={{0,192},{64,0},{128,64},{192,128},{1,193},{65,1},{129,65},{193,129... | collective-permute-start | bytes 393224 | tf_op jit(solution)/shard_map/ppermute | solution.py:197
  20.2 5.8 %collective-permute-start.2 = (bf16[64,512]{1,0:T(8,128)(2,1)S(1)}, bf16[64,512]{1,0:T(8,128)(2,1)S(1)}, u32[]{:S(2)}, u32[]{:S(2)}) collective-permute-start(bf16[64,512]{1,0:T(8,128)(2,1)S(1)} %get-tuple-element.57), channel_id=1, source_target_pairs={{0,128},{64,192},{128,0},{192,64},{1,129},{65,193},{129,1},{193,65... | collective-permute-start | bytes 196616 | tf_op jit(solution)/shard_map/ppermute | solution.py:197
  20.8 5.9 %collective-permute-start.1 = (bf16[64,512]{1,0:T(8,128)(2,1)S(1)}, bf16[64,512]{1,0:T(8,128)(2,1)S(1)}, u32[]{:S(2)}, u32[]{:S(2)}) collective-permute-start(bf16[64,512]{1,0:T(8,128)(2,1)S(1)} %get-tuple-element.54), channel_id=1, source_target_pairs={{0,128},{64,192},{128,0},{192,64},{1,129},{65,193},{129,1},{193,65... | collective-permute-start | bytes 196616 | tf_op jit(solution)/shard_map/ppermute | solution.py:197
  25.9 15.7 %collective-permute-start = (bf16[128,512]{1,0:T(8,128)(2,1)S(1)}, bf16[128,512]{1,0:T(8,128)(2,1)S(1)}, u32[]{:S(2)}, u32[]{:S(2)}) collective-permute-start(bf16[128,512]{1,0:T(8,128)(2,1)S(1)} %get-tuple-element.53), channel_id=1, source_target_pairs={{0,64},{64,128},{128,192},{192,0},{1,65},{65,129},{129,193},{193,1... | collective-permute-start | bytes 393224 | tf_op jit(solution)/shard_map/ppermute | solution.py:197
  26.9 18.9 %collective-permute-start.14 = (bf16[4,64,512]{2,1,0:T(8,128)(2,1)S(1)}, bf16[4,64,512]{2,1,0:T(8,128)(2,1)S(1)}, u32[]{:S(2)}, u32[]{:S(2)}) collective-permute-start(bf16[4,64,512]{2,1,0:T(8,128)(2,1)S(1)} %get-tuple-element.49), channel_id=1, source_target_pairs={{0,128},{64,192},{128,0},{192,64},{1,129},{65,193},{129,1},{193,65... | collective-permute-start | bytes 786440 | tf_op jit(solution)/shard_map/ppermute | solution.py:197
  31.0 16.4 %collective-permute-start.13 = (bf16[4,64,512]{2,1,0:T(8,128)(2,1)S(1)}, bf16[4,64,512]{2,1,0:T(8,128)(2,1)S(1)}, u32[]{:S(2)}, u32[]{:S(2)}) collective-permute-start(bf16[4,64,512]{2,1,0:T(8,128)(2,1)S(1)} %get-tuple-element.48), channel_id=1, source_target_pairs={{0,128},{64,192},{128,0},{192,64},{1,129},{65,193},{129,1},{193,65... | collective-permute-start | bytes 786440 | tf_op jit(solution)/shard_map/ppermute | solution.py:197
  41.7 10.8 %collective-permute-start.6 = (bf16[4,64,512]{2,1,0:T(8,128)(2,1)S(1)}, bf16[4,64,512]{2,1,0:T(8,128)(2,1)S(1)}, u32[]{:S(2)}, u32[]{:S(2)}) collective-permute-start(bf16[4,64,512]{2,1,0:T(8,128)(2,1)S(1)} %get-tuple-element.45), channel_id=1, source_target_pairs={{0,32},{16,48},{32,0},{48,16},{1,33},{17,49},{33,1},{49,17},{2,34}... | collective-permute-start | bytes 786440 | tf_op jit(solution)/shard_map/ppermute | solution.py:197
  43.7 13.9 %collective-permute-start.15 = (bf16[4,128,512]{2,1,0:T(8,128)(2,1)S(1)}, bf16[4,128,512]{2,1,0:T(8,128)(2,1)S(1)}, u32[]{:S(2)}, u32[]{:S(2)}) collective-permute-start(bf16[4,128,512]{2,1,0:T(8,128)(2,1)S(1)} %get-tuple-element.47), channel_id=1, source_target_pairs={{0,192},{64,0},{128,64},{192,128},{1,193},{65,1},{129,65},{193,129... | collective-permute-start | bytes 1572872 | tf_op jit(solution)/shard_map/ppermute | solution.py:197
  43.7 13.9 %collective-permute-start.12 = (bf16[4,128,512]{2,1,0:T(8,128)(2,1)S(1)}, bf16[4,128,512]{2,1,0:T(8,128)(2,1)S(1)}, u32[]{:S(2)}, u32[]{:S(2)}) collective-permute-start(bf16[4,128,512]{2,1,0:T(8,128)(2,1)S(1)} %get-tuple-element.47), channel_id=1, source_target_pairs={{0,64},{64,128},{128,192},{192,0},{1,65},{65,129},{129,193},{193,1... | collective-permute-start | bytes 1572872 | tf_op jit(solution)/shard_map/ppermute | solution.py:197
  45.8 11.9 %collective-permute-start.5 = (bf16[4,64,512]{2,1,0:T(8,128)(2,1)S(1)}, bf16[4,64,512]{2,1,0:T(8,128)(2,1)S(1)}, u32[]{:S(2)}, u32[]{:S(2)}) collective-permute-start(bf16[4,64,512]{2,1,0:T(8,128)(2,1)S(1)} %get-tuple-element.44), channel_id=1, source_target_pairs={{0,32},{16,48},{32,0},{48,16},{1,33},{17,49},{33,1},{49,17},{2,34}... | collective-permute-start | bytes 786440 | tf_op jit(solution)/shard_map/ppermute | solution.py:197
  47.4 21.6 %collective-permute-start.7 = (bf16[4,128,512]{2,1,0:T(8,128)(2,1)S(1)}, bf16[4,128,512]{2,1,0:T(8,128)(2,1)S(1)}, u32[]{:S(2)}, u32[]{:S(2)}) collective-permute-start(bf16[4,128,512]{2,1,0:T(8,128)(2,1)S(1)} %get-tuple-element.43), channel_id=1, source_target_pairs={{0,48},{16,0},{32,16},{48,32},{1,49},{17,1},{33,17},{49,33},{2,50}... | collective-permute-start | bytes 1572872 | tf_op jit(solution)/shard_map/ppermute | solution.py:197
  52.5 19.7 %collective-permute-start.4 = (bf16[4,128,512]{2,1,0:T(8,128)(2,1)S(1)}, bf16[4,128,512]{2,1,0:T(8,128)(2,1)S(1)}, u32[]{:S(2)}, u32[]{:S(2)}) collective-permute-start(bf16[4,128,512]{2,1,0:T(8,128)(2,1)S(1)} %get-tuple-element.43), channel_id=1, source_target_pairs={{0,16},{16,32},{32,48},{48,0},{1,17},{17,33},{33,49},{49,1},{2,18}... | collective-permute-start | bytes 1572872 | tf_op jit(solution)/shard_map/ppermute | solution.py:197
  72.6 2.4 %copy-start.1 = (s32[7]{0:T(128)S(1)}, s32[7]{0:T(128)}, u32[]{:S(2)}) copy-start(s32[7]{0:T(128)} %docs.3) | copy-start | bytes 88
  74.9 13.4 %collective-permute-start.16 = (bf16[2,4,4,128,512]{4,3,2,1,0:T(8,128)(2,1)}, bf16[2,4,4,128,512]{4,3,2,1,0:T(8,128)(2,1)}, u32[]{:S(2)}, u32[]{:S(2)}) collective-permute-start(bf16[2,4,4,128,512]{4,3,2,1,0:T(8,128)(2,1)} %pad_maximum_fusion.near), channel_id=1, source_target_pairs={{0,8},{8,0},{1,9},{9,1},{2,10},{10,2},{3,11},{11,3},{4,12},{12,4},... | collective-permute-start | bytes 12582920 | tf_op jit(solution)/shard_map/ppermute | solution.py:215
  75.6 11.1 %all-to-all-start = ((s32[32,1,12]{2,1,0:T(1,128)}), s32[32,1,12]{2,1,0:T(1,128)S(1)}, u32[]{:S(2)}, u32[]{:S(2)}) async-start(s32[32,1,12]{2,1,0:T(1,128)} %broadcast_in_dim.5), calls=%async_computation | async-start | bytes 32768 | tf_op jit(solution)/shard_map/all_to_all | solution.py:219
  79.5 143.5 %reduce-scatter.2.cloned.1.call-start = ((), (), s32[]{:S(2)}) async-start(), calls=%async_computation.5 | async-start | bytes 8257536 | tf_op jit(solution)/shard_map/reduce_scatter | solution.py:293
  129.0 58.4 %all-to-all-start.2 = ((bf16[32,128,512]{2,1,0:T(8,128)(2,1)}), bf16[32,128,512]{2,1,0:T(8,128)(2,1)}, u32[]{:S(2)}, u32[]{:S(2)}) async-start(bf16[32,128,512]{2,1,0:T(8,128)(2,1)} %get-tuple-element.28), calls=%async_computation.2 | async-start | bytes 8388608 | tf_op jit(solution)/shard_map/all_to_all | solution.py:278
  142.5 4.4 %collective-permute-start.17 = (bf16[16,512,128]{2,1,0:T(8,128)(2,1)}, bf16[16,512,128]{2,1,0:T(8,128)(2,1)S(1)}, u32[]{:S(2)}, u32[]{:S(2)}) collective-permute-start(bf16[16,512,128]{2,1,0:T(8,128)(2,1)} %get-tuple-element.31), channel_id=1, source_target_pairs={{0,8},{8,0},{1,9},{9,1},{2,10},{10,2},{3,11},{11,3},{4,12},{12,4},... | collective-permute-start | bytes 6291464 | tf_op jit(solution)/shard_map/ppermute | solution.py:309
  187.4 33.8 %all-to-all-start.3 = ((bf16[16,512,128]{2,1,0:T(8,128)(2,1)}), bf16[16,512,128]{2,1,0:T(8,128)(2,1)S(1)}, u32[]{:S(2)}, u32[]{:S(2)}) async-start(bf16[16,512,128]{2,1,0:T(8,128)(2,1)} %add_convert_fusion), calls=%async_computation.4 | async-start | bytes 4194304 | tf_op jit(solution)/shard_map/all_to_all | solution.py:312
  (3 other events, 6.3 us)
Sparse Core Ops, SparseCore 0:
  11.1 61.3 all-gather.2
  129.1 79.2 reduce-scatter.1

commit v7 on v6

--- a/solution.py
+++ b/solution.py
@@ -204,7 +204,15 @@
 def per_device(queries, context_grad, encoder_rows, key_weight, value_weight, document_lengths, block_bin, block_document):
     rows, width = encoder_rows.shape
     tokens = queries.shape[0]
-    gathered = lax.all_gather(jnp.concatenate([key_weight, value_weight], axis=1), DP, axis=0, tiled=False)
+    facts = jnp.concatenate([document_lengths[0], block_bin, block_document]).astype(bf16)
+    packed = jnp.concatenate(
+        [
+            jnp.concatenate([key_weight, value_weight], axis=1),
+            jnp.pad(facts[None, :], ((0, 15), (0, 2 * HD - facts.shape[0]))),
+        ],
+        axis=0,
+    )
+    gathered = lax.all_gather(packed, DP, axis=0, tiled=False)
     own_tokens = jnp.concatenate([queries, context_grad], axis=1)
     near_tokens = jnp.stack(
         [
@@ -214,18 +222,12 @@
     )
     far_tokens = lax.ppermute(near_tokens, "c", [(0, 1), (1, 0)])
 
-    def share(v):
-        spread_out = jnp.broadcast_to(v[None], (BINS, *v.shape))
-        return lax.all_to_all(spread_out, DP, split_axis=0, concat_axis=0, tiled=True)
-
-    facts = jnp.concatenate([document_lengths[0], block_bin * NDOC + block_document, jnp.full((1,), -1, jnp.int32)])
-    facts = share(facts[None, :])[:, 0, :]
-    lengths = facts[:, :NDOC]
-    ids = jnp.broadcast_to(facts[:, NDOC:, None].astype(f32), (BINS, 8, WIN))
-    sent = facts[:, NDOC : NDOC + EBLK]
-    me = lax.axis_index(DP)
-    sent_docs = jnp.sum(jnp.where(sent // NDOC == me, sent % NDOC, 0), axis=1)
-    ids, sent_docs, lengths, gathered = lax.optimization_barrier((ids, sent_docs, lengths, gathered))
+    facts = gathered[:, BLK, : NDOC + 2 * EBLK].astype(jnp.int32)
+    lengths, bins, docs = facts[:, :NDOC], facts[:, NDOC : NDOC + EBLK], facts[:, NDOC + EBLK :]
+    ids = jnp.pad((bins * NDOC + docs).astype(f32), ((0, 0), (0, 1)), constant_values=-1.0)
+    ids = jnp.broadcast_to(ids[:, :, None], (BINS, 8, WIN))
+    sent_docs = jnp.sum(jnp.where(bins == lax.axis_index(DP), docs, 0), axis=1)
+    ids, sent_docs, lengths = lax.optimization_barrier((ids, sent_docs, lengths))
 
     kv, qc, stats = pl.pallas_call(
         project_kernel,

time: 231 us -> 228 us (0.987)
  waiting for transfers between devices: 108 us -> 100 us
    all_to_all x1 -> x0, waiting for transfers between devices: 7.22 us -> none  [share(): lax.all_to_all(spread_out, DP, split_axis=0, concat_axis=0, tiled=True)]
    ppermute x16, starting transfers between devices: 25.3 us -> 31 us  [send(): return lax.ppermute(part, axis, [(i, (i + distance) % 4) for i in range(4)])]
    ppermute x16, waiting for transfers between devices: 35.6 us -> 30.1 us  [send(): return lax.ppermute(part, axis, [(i, (i + distance) % 4) for i in range(4)])]
    ppermute x1, waiting for transfers between devices: 0.01 us -> 5.16 us  [per_device(): far_tokens = lax.ppermute(near_tokens, 'c', [(0, 1), (1, 0)])]
    all_to_all x1 -> x0, starting transfers between devices: 3.83 us -> none  [share(): lax.all_to_all(spread_out, DP, split_axis=0, concat_axis=0, tiled=True)]
  transfers between devices with their start and end apart: 23 -> 22, of which waited for: 11 -> 11; matrix products, arithmetic and copies ran while one was open for 5% -> 6% of each run, Pallas kernels for 6% -> 7%
where the time goes in v7:
time: 228 us; the launch traced here: 226 us
  waiting for transfers between devices  100 us (44%)
  Pallas kernels  40.9 us (18%)
  starting transfers between devices  39.7 us (17%)
  blocking collectives  14.9 us (7%)
  between operations  14.2 us (6%)
  other arithmetic  11.4 us (5%)
  local copies, waits for them, and re-layouts  4.23 us (2%)
    all_to_all x1, waiting for transfers between devices, per_device(): windows = lax.all_to_all(slots, DP, split_axis=0, concat_axis=0, tiled=True)  36.8 us
    ppermute x16, starting transfers between devices, send(): return lax.ppermute(part, axis, [(i, (i + distance) % 4) for i in range(4)])  31 us
    ppermute x16, waiting for transfers between devices, send(): return lax.ppermute(part, axis, [(i, (i + distance) % 4) for i in range(4)])  30.1 us
    all_to_all x1, waiting for transfers between devices, per_device(): lax.all_to_all(pair_sums, PLANE, split_axis=0, concat_axis=0, tiled=True)  23.9 us
    all_to_all x1, blocking collectives, per_device(): lax.all_to_all(stats, DP, split_axis=0, concat_axis=0, tiled=True)  14.9 us
    pallas_call x1, Pallas kernels, per_device(): pl.pallas_call(project_kernel, grid=(4,), in_specs=[SMEM, SMEM, SMEM, pl....  11.1 us
    pallas_call x1, Pallas kernels, per_device(): pl.pallas_call(weights_kernel, grid=(4,), in_specs=[pl.BlockSpec((2 * HD,...  8.84 us
    pallas_call x1, Pallas kernels, per_device(): pl.pallas_call(rows_kernel, grid=(4,), in_specs=[pl.BlockSpec((rows, 2 *...  8.22 us
  transfers between devices with their start and end apart: 22, of which 11 were waited for; matrix products, arithmetic and copies ran while one was open for 6% of the time, Pallas kernels for 7%

profile of v7, /device:TPU:192, one launch (start us, length us, event | category | flops | bytes accessed | tf_op | source)
XLA Modules:
  0.0 225.7 jit_solution(10657757428768781818)
XLA Ops:
  12.1 3.1 %collective-permute-start.10 = (bf16[64,512]{1,0:T(8,128)(2,1)S(1)}, bf16[64,512]{1,0:T(8,128)(2,1)S(1)}, u32[]{:S(2)}, u32[]{:S(2)}) collective-permute-start(bf16[64,512]{1,0:T(8,128)(2,1)S(1)} %get-tuple-element.53), channel_id=1, source_target_pairs={{0,32},{16,48},{32,0},{48,16},{1,33},{17,49},{33,1},{49,17},{2,34}... | collective-permute-start | bytes 196616 | tf_op jit(solution)/shard_map/ppermute | solution.py:197
  15.8 2.8 %collective-permute-start.11 = (bf16[128,512]{1,0:T(8,128)(2,1)S(1)}, bf16[128,512]{1,0:T(8,128)(2,1)S(1)}, u32[]{:S(2)}, u32[]{:S(2)}) collective-permute-start(bf16[128,512]{1,0:T(8,128)(2,1)S(1)} %get-tuple-element.50), channel_id=1, source_target_pairs={{0,48},{16,0},{32,16},{48,32},{1,49},{17,1},{33,17},{49,33},{2,50}... | collective-permute-start | bytes 393224 | tf_op jit(solution)/shard_map/ppermute | solution.py:197
  18.6 3.0 %collective-permute-start.3 = (bf16[128,512]{1,0:T(8,128)(2,1)S(1)}, bf16[128,512]{1,0:T(8,128)(2,1)S(1)}, u32[]{:S(2)}, u32[]{:S(2)}) collective-permute-start(bf16[128,512]{1,0:T(8,128)(2,1)S(1)} %get-tuple-element.51), channel_id=1, source_target_pairs={{0,192},{64,0},{128,64},{192,128},{1,193},{65,1},{129,65},{193,129... | collective-permute-start | bytes 393224 | tf_op jit(solution)/shard_map/ppermute | solution.py:197
  22.3 2.9 %collective-permute-start.1 = (bf16[64,512]{1,0:T(8,128)(2,1)S(1)}, bf16[64,512]{1,0:T(8,128)(2,1)S(1)}, u32[]{:S(2)}, u32[]{:S(2)}) collective-permute-start(bf16[64,512]{1,0:T(8,128)(2,1)S(1)} %get-tuple-element.52), channel_id=1, source_target_pairs={{0,128},{64,192},{128,0},{192,64},{1,129},{65,193},{129,1},{193,65... | collective-permute-start | bytes 196616 | tf_op jit(solution)/shard_map/ppermute | solution.py:197
  28.3 3.6 %collective-permute-start.14 = (bf16[4,64,512]{2,1,0:T(8,128)(2,1)S(1)}, bf16[4,64,512]{2,1,0:T(8,128)(2,1)S(1)}, u32[]{:S(2)}, u32[]{:S(2)}) collective-permute-start(bf16[4,64,512]{2,1,0:T(8,128)(2,1)S(1)} %get-tuple-element.47), channel_id=1, source_target_pairs={{0,128},{64,192},{128,0},{192,64},{1,129},{65,193},{129,1},{193,65... | collective-permute-start | bytes 786440 | tf_op jit(solution)/shard_map/ppermute | solution.py:197
  31.9 5.9 %collective-permute-done = bf16[128,512]{1,0:T(8,128)(2,1)S(1)} collective-permute-done((bf16[128,512]{1,0:T(8,128)(2,1)S(1)}, bf16[128,512]{1,0:T(8,128)(2,1)S(1)}, u32[]{:S(2)}, u32[]{:S(2)}) %collective-permute-start) | collective-permute-done | bytes 131104 | tf_op jit(solution)/shard_map/ppermute | solution.py:197
  38.0 7.3 %collective-permute-start.6 = (bf16[4,64,512]{2,1,0:T(8,128)(2,1)S(1)}, bf16[4,64,512]{2,1,0:T(8,128)(2,1)S(1)}, u32[]{:S(2)}, u32[]{:S(2)}) collective-permute-start(bf16[4,64,512]{2,1,0:T(8,128)(2,1)S(1)} %get-tuple-element.43), channel_id=1, source_target_pairs={{0,32},{16,48},{32,0},{48,16},{1,33},{17,49},{33,1},{49,17},{2,34}... | collective-permute-start | bytes 786440 | tf_op jit(solution)/shard_map/ppermute | solution.py:197
  47.5 2.5 %collective-permute-start.7 = (bf16[4,128,512]{2,1,0:T(8,128)(2,1)S(1)}, bf16[4,128,512]{2,1,0:T(8,128)(2,1)S(1)}, u32[]{:S(2)}, u32[]{:S(2)}) collective-permute-start(bf16[4,128,512]{2,1,0:T(8,128)(2,1)S(1)} %get-tuple-element.41), channel_id=1, source_target_pairs={{0,48},{16,0},{32,16},{48,32},{1,49},{17,1},{33,17},{49,33},{2,50}... | collective-permute-start | bytes 1572872 | tf_op jit(solution)/shard_map/ppermute | solution.py:197
  54.1 6.0 %collective-permute-done.5 = bf16[4,64,512]{2,1,0:T(8,128)(2,1)S(1)} collective-permute-done((bf16[4,64,512]{2,1,0:T(8,128)(2,1)S(1)}, bf16[4,64,512]{2,1,0:T(8,128)(2,1)S(1)}, u32[]{:S(2)}, u32[]{:S(2)}) %collective-permute-start.5) | collective-permute-done | bytes 262176 | tf_op jit(solution)/shard_map/ppermute | solution.py:197
  60.5 10.8 %collective-permute-done.7 = bf16[4,128,512]{2,1,0:T(8,128)(2,1)S(1)} collective-permute-done((bf16[4,128,512]{2,1,0:T(8,128)(2,1)S(1)}, bf16[4,128,512]{2,1,0:T(8,128)(2,1)S(1)}, u32[]{:S(2)}, u32[]{:S(2)}) %collective-permute-start.7) | collective-permute-done | bytes 524320 | tf_op jit(solution)/shard_map/ppermute | solution.py:197
  71.3 2.7 %collective-permute-done.4 = bf16[4,128,512]{2,1,0:T(8,128)(2,1)S(1)} collective-permute-done((bf16[4,128,512]{2,1,0:T(8,128)(2,1)S(1)}, bf16[4,128,512]{2,1,0:T(8,128)(2,1)S(1)}, u32[]{:S(2)}, u32[]{:S(2)}) %collective-permute-start.4) | collective-permute-done | bytes 524320 | tf_op jit(solution)/shard_map/ppermute | solution.py:197
  78.9 5.2 %collective-permute-done.16.far = bf16[2,4,4,128,512]{4,3,2,1,0:T(8,128)(2,1)} collective-permute-done((bf16[2,4,4,128,512]{4,3,2,1,0:T(8,128)(2,1)}, bf16[2,4,4,128,512]{4,3,2,1,0:T(8,128)(2,1)}, u32[]{:S(2)}, u32[]{:S(2)}) %collective-permute-start.16) | collective-permute-done | bytes 4194336 | tf_op jit(solution)/shard_map/ppermute | solution.py:223
  84.1 11.1 %project.1 = (bf16[896,512]{1,0:T(8,128)(2,1)}, bf16[7,128,512]{2,1,0:T(8,128)(2,1)}, f32[32,24,128]{2,1,0:T(8,128)}) custom-call(s32[7]{0:T(128)} %bins.3, s32[7]{0:T(128)} %docs.3, s32[32,4]{1,0:T(8,128)} %bitcast.46, bf16[896,4096]{1,0:T(8,128)(2,1)} %e.3, bf16[32,144,512]{2,1,0:T(8,128)(2,1)} %bitcast.38, ...), custom_call_target="tpu_custom_call" | custom-call | tf_op jit(solution)/shard_map/project/pallas_call | solution.py:232
  95.2 14.9 %all_to_all.15.stats = f32[32,24,128]{2,1,0:T(8,128)} all-to-all(f32[32,24,128]{2,1,0:T(8,128)} %get-tuple-element.24), channel_id=1, replica_groups=mesh['y'=4,'x'=4,'c'=2,'mp'=8] {'y','x','c'}, dimensions={0} | all-to-all | bytes 786432 | tf_op jit(solution)/shard_map/all_to_all | solution.py:260
  110.0 6.6 %attend.1 = (bf16[896,512]{1,0:T(8,128)(2,1)}, bf16[512,896]{1,0:T(8,128)(2,1)}, bf16[32,128,512]{2,1,0:T(8,128)(2,1)}) custom-call(s32[7]{0:T(128)} %bins.3, s32[7]{0:T(128)} %docs.3, s32[32,4]{1,0:T(8,128)} %bitcast.47, bf16[896,512]{1,0:T(8,128)(2,1)} %get-tuple-element.22.kv, bf16[7,128,512]{2,1,0:T(8,128)(2,1)} %get-tuple-element.23.qc, ...), custom_call_target="tpu_custom_call" | custom-call | tf_op jit(solution)/shard_map/attend/pallas_call | solution.py:262
  116.6 8.2 %row_terms.1 = bf16[8,896,512]{2,1,0:T(8,128)(2,1)} custom-call(bf16[896,512]{1,0:T(8,128)(2,1)} %get-tuple-element.33.grads, bf16[32,144,512]{2,1,0:T(8,128)(2,1)} %bitcast.39), custom_call_target="tpu_custom_call" | custom-call | flops 3758096384 | bytes 16777216 | tf_op jit(solution)/shard_map/row_terms/pallas_call | solution.py:282
  124.9 4.9 %all-to-all-start.1 = ((bf16[32,128,512]{2,1,0:T(8,128)(2,1)}), bf16[32,128,512]{2,1,0:T(8,128)(2,1)}, u32[]{:S(2)}, u32[]{:S(2)}) async-start(bf16[32,128,512]{2,1,0:T(8,128)(2,1)} %get-tuple-element.26), calls=%async_computation.1 | async-start | bytes 8388608 | tf_op jit(solution)/shard_map/all_to_all | solution.py:280
  129.8 8.8 %weight_terms.1 = (bf16[16,512,128]{2,1,0:T(8,128)(2,1)}, bf16[16,512,128]{2,1,0:T(8,128)(2,1)}) custom-call(bf16[512,896]{1,0:T(8,128)(2,1)} %get-tuple-element.27.grads_t, bf16[896,4096]{1,0:T(8,128)(2,1)} %e.3), custom_call_target="tpu_custom_call" | custom-call | flops 3758096384 | bytes 16777216 | tf_op jit(solution)/shard_map/weight_terms/pallas_call | solution.py:298
  138.6 4.4 %collective-permute-done.17 = bf16[16,512,128]{2,1,0:T(8,128)(2,1)S(1)} collective-permute-done((bf16[16,512,128]{2,1,0:T(8,128)(2,1)}, bf16[16,512,128]{2,1,0:T(8,128)(2,1)S(1)}, u32[]{:S(2)}, u32[]{:S(2)}) %collective-permute-start.17) | collective-permute-done | bytes 2097184 | tf_op jit(solution)/shard_map/ppermute | solution.py:311
  143.0 3.4 %add_convert_fusion = bf16[16,512,128]{2,1,0:T(8,128)(2,1)} fusion(bf16[16,512,128]{2,1,0:T(8,128)(2,1)S(1)} %collective-permute-done.17, bf16[16,512,128]{2,1,0:T(8,128)(2,1)} %get-tuple-element.28), kind=kLoop, calls=%fused_computation.1 | loop fusion | flops 4194304 | bytes 6291456 | tf_op jit(solution)/shard_map/convert_element_type | solution.py:312
  146.4 36.8 %all-to-all-done.1.windows = bf16[32,128,512]{2,1,0:T(8,128)(2,1)} async-done(((bf16[32,128,512]{2,1,0:T(8,128)(2,1)}), bf16[32,128,512]{2,1,0:T(8,128)(2,1)}, u32[]{:S(2)}, u32[]{:S(2)}) %all-to-all-start.1) | async-done | bytes 4194336 | tf_op jit(solution)/shard_map/all_to_all | solution.py:280
  183.2 3.7 %all-to-all-start.2 = ((bf16[16,512,128]{2,1,0:T(8,128)(2,1)}), bf16[16,512,128]{2,1,0:T(8,128)(2,1)S(1)}, u32[]{:S(2)}, u32[]{:S(2)}) async-start(bf16[16,512,128]{2,1,0:T(8,128)(2,1)} %add_convert_fusion), calls=%async_computation.3 | async-start | bytes 4194304 | tf_op jit(solution)/shard_map/all_to_all | solution.py:314
  187.0 6.2 %collect.1 = (bf16[256,256]{1,0:T(8,128)(2,1)}, bf16[256,256]{1,0:T(8,128)(2,1)}) custom-call(s32[32]{0:T(128)} %get-tuple-element.20.docs, s32[1,4]{1,0:T(1,128)} %lengths.1, bf16[32,128,512]{2,1,0:T(8,128)(2,1)} %all-to-all-done.1.windows), custom_call_target="tpu_custom_call" | custom-call | tf_op jit(solution)/shard_map/collect/pallas_call | solution.py:316
  193.2 23.9 %all-to-all-done.2 = bf16[16,512,128]{2,1,0:T(8,128)(2,1)S(1)} async-done(((bf16[16,512,128]{2,1,0:T(8,128)(2,1)}), bf16[16,512,128]{2,1,0:T(8,128)(2,1)S(1)}, u32[]{:S(2)}, u32[]{:S(2)}) %all-to-all-start.2) | async-done | bytes 2097184 | tf_op jit(solution)/shard_map/all_to_all | solution.py:314
  (58 shorter events, 22.7 us)
Async XLA Ops:
  7.2 69.4 %all-gather.3.cloned.1.call-start = ((), (), s32[]{:S(2)}) async-start(), calls=%async_computation.5 | async-start | bytes 4866048 | tf_op jit(solution)/shard_map/all_gather | solution.py:215
  10.2 208.6 %reduce-scatter.2.cloned.1.call-start = ((), (), s32[]{:S(2)}) async-start(), calls=%async_computation.4 | async-start | bytes 8257536 | tf_op jit(solution)/shard_map/reduce_scatter | solution.py:295
  12.1 9.5 %collective-permute-start.10 = (bf16[64,512]{1,0:T(8,128)(2,1)S(1)}, bf16[64,512]{1,0:T(8,128)(2,1)S(1)}, u32[]{:S(2)}, u32[]{:S(2)}) collective-permute-start(bf16[64,512]{1,0:T(8,128)(2,1)S(1)} %get-tuple-element.53), channel_id=1, source_target_pairs={{0,32},{16,48},{32,0},{48,16},{1,33},{17,49},{33,1},{49,17},{2,34}... | collective-permute-start | bytes 196616 | tf_op jit(solution)/shard_map/ppermute | solution.py:197
  15.2 7.0 %collective-permute-start.9 = (bf16[64,512]{1,0:T(8,128)(2,1)S(1)}, bf16[64,512]{1,0:T(8,128)(2,1)S(1)}, u32[]{:S(2)}, u32[]{:S(2)}) collective-permute-start(bf16[64,512]{1,0:T(8,128)(2,1)S(1)} %get-tuple-element.54), channel_id=1, source_target_pairs={{0,32},{16,48},{32,0},{48,16},{1,33},{17,49},{33,1},{49,17},{2,34}... | collective-permute-start | bytes 196616 | tf_op jit(solution)/shard_map/ppermute | solution.py:197
  15.8 12.3 %collective-permute-start.11 = (bf16[128,512]{1,0:T(8,128)(2,1)S(1)}, bf16[128,512]{1,0:T(8,128)(2,1)S(1)}, u32[]{:S(2)}, u32[]{:S(2)}) collective-permute-start(bf16[128,512]{1,0:T(8,128)(2,1)S(1)} %get-tuple-element.50), channel_id=1, source_target_pairs={{0,48},{16,0},{32,16},{48,32},{1,49},{17,1},{33,17},{49,33},{2,50}... | collective-permute-start | bytes 393224 | tf_op jit(solution)/shard_map/ppermute | solution.py:197
  18.6 9.5 %collective-permute-start.8 = (bf16[128,512]{1,0:T(8,128)(2,1)S(1)}, bf16[128,512]{1,0:T(8,128)(2,1)S(1)}, u32[]{:S(2)}, u32[]{:S(2)}) collective-permute-start(bf16[128,512]{1,0:T(8,128)(2,1)S(1)} %get-tuple-element.50), channel_id=1, source_target_pairs={{0,16},{16,32},{32,48},{48,0},{1,17},{17,33},{33,49},{49,1},{2,18}... | collective-permute-start | bytes 393224 | tf_op jit(solution)/shard_map/ppermute | solution.py:197
  18.6 13.3 %collective-permute-start.3 = (bf16[128,512]{1,0:T(8,128)(2,1)S(1)}, bf16[128,512]{1,0:T(8,128)(2,1)S(1)}, u32[]{:S(2)}, u32[]{:S(2)}) collective-permute-start(bf16[128,512]{1,0:T(8,128)(2,1)S(1)} %get-tuple-element.51), channel_id=1, source_target_pairs={{0,192},{64,0},{128,64},{192,128},{1,193},{65,1},{129,65},{193,129... | collective-permute-start | bytes 393224 | tf_op jit(solution)/shard_map/ppermute | solution.py:197
  21.6 5.8 %collective-permute-start.2 = (bf16[64,512]{1,0:T(8,128)(2,1)S(1)}, bf16[64,512]{1,0:T(8,128)(2,1)S(1)}, u32[]{:S(2)}, u32[]{:S(2)}) collective-permute-start(bf16[64,512]{1,0:T(8,128)(2,1)S(1)} %get-tuple-element.55), channel_id=1, source_target_pairs={{0,128},{64,192},{128,0},{192,64},{1,129},{65,193},{129,1},{193,65... | collective-permute-start | bytes 196616 | tf_op jit(solution)/shard_map/ppermute | solution.py:197
  22.3 5.8 %collective-permute-start.1 = (bf16[64,512]{1,0:T(8,128)(2,1)S(1)}, bf16[64,512]{1,0:T(8,128)(2,1)S(1)}, u32[]{:S(2)}, u32[]{:S(2)}) collective-permute-start(bf16[64,512]{1,0:T(8,128)(2,1)S(1)} %get-tuple-element.52), channel_id=1, source_target_pairs={{0,128},{64,192},{128,0},{192,64},{1,129},{65,193},{129,1},{193,65... | collective-permute-start | bytes 196616 | tf_op jit(solution)/shard_map/ppermute | solution.py:197
  27.4 10.5 %collective-permute-start = (bf16[128,512]{1,0:T(8,128)(2,1)S(1)}, bf16[128,512]{1,0:T(8,128)(2,1)S(1)}, u32[]{:S(2)}, u32[]{:S(2)}) collective-permute-start(bf16[128,512]{1,0:T(8,128)(2,1)S(1)} %get-tuple-element.51), channel_id=1, source_target_pairs={{0,64},{64,128},{128,192},{192,0},{1,65},{65,129},{129,193},{193,1... | collective-permute-start | bytes 393224 | tf_op jit(solution)/shard_map/ppermute | solution.py:197
  28.3 19.1 %collective-permute-start.14 = (bf16[4,64,512]{2,1,0:T(8,128)(2,1)S(1)}, bf16[4,64,512]{2,1,0:T(8,128)(2,1)S(1)}, u32[]{:S(2)}, u32[]{:S(2)}) collective-permute-start(bf16[4,64,512]{2,1,0:T(8,128)(2,1)S(1)} %get-tuple-element.47), channel_id=1, source_target_pairs={{0,128},{64,192},{128,0},{192,64},{1,129},{65,193},{129,1},{193,65... | collective-permute-start | bytes 786440 | tf_op jit(solution)/shard_map/ppermute | solution.py:197
  31.8 15.6 %collective-permute-start.13 = (bf16[4,64,512]{2,1,0:T(8,128)(2,1)S(1)}, bf16[4,64,512]{2,1,0:T(8,128)(2,1)S(1)}, u32[]{:S(2)}, u32[]{:S(2)}) collective-permute-start(bf16[4,64,512]{2,1,0:T(8,128)(2,1)S(1)} %get-tuple-element.46), channel_id=1, source_target_pairs={{0,128},{64,192},{128,0},{192,64},{1,129},{65,193},{129,1},{193,65... | collective-permute-start | bytes 786440 | tf_op jit(solution)/shard_map/ppermute | solution.py:197
  38.0 14.0 %collective-permute-start.6 = (bf16[4,64,512]{2,1,0:T(8,128)(2,1)S(1)}, bf16[4,64,512]{2,1,0:T(8,128)(2,1)S(1)}, u32[]{:S(2)}, u32[]{:S(2)}) collective-permute-start(bf16[4,64,512]{2,1,0:T(8,128)(2,1)S(1)} %get-tuple-element.43), channel_id=1, source_target_pairs={{0,32},{16,48},{32,0},{48,16},{1,33},{17,49},{33,1},{49,17},{2,34}... | collective-permute-start | bytes 786440 | tf_op jit(solution)/shard_map/ppermute | solution.py:197
  45.4 14.8 %collective-permute-start.15 = (bf16[4,128,512]{2,1,0:T(8,128)(2,1)S(1)}, bf16[4,128,512]{2,1,0:T(8,128)(2,1)S(1)}, u32[]{:S(2)}, u32[]{:S(2)}) collective-permute-start(bf16[4,128,512]{2,1,0:T(8,128)(2,1)S(1)} %get-tuple-element.45), channel_id=1, source_target_pairs={{0,192},{64,0},{128,64},{192,128},{1,193},{65,1},{129,65},{193,129... | collective-permute-start | bytes 1572872 | tf_op jit(solution)/shard_map/ppermute | solution.py:197
  45.4 14.8 %collective-permute-start.12 = (bf16[4,128,512]{2,1,0:T(8,128)(2,1)S(1)}, bf16[4,128,512]{2,1,0:T(8,128)(2,1)S(1)}, u32[]{:S(2)}, u32[]{:S(2)}) collective-permute-start(bf16[4,128,512]{2,1,0:T(8,128)(2,1)S(1)} %get-tuple-element.45), channel_id=1, source_target_pairs={{0,64},{64,128},{128,192},{192,0},{1,65},{65,129},{129,193},{193,1... | collective-permute-start | bytes 1572872 | tf_op jit(solution)/shard_map/ppermute | solution.py:197
  47.4 12.8 %collective-permute-start.5 = (bf16[4,64,512]{2,1,0:T(8,128)(2,1)S(1)}, bf16[4,64,512]{2,1,0:T(8,128)(2,1)S(1)}, u32[]{:S(2)}, u32[]{:S(2)}) collective-permute-start(bf16[4,64,512]{2,1,0:T(8,128)(2,1)S(1)} %get-tuple-element.42), channel_id=1, source_target_pairs={{0,32},{16,48},{32,0},{48,16},{1,33},{17,49},{33,1},{49,17},{2,34}... | collective-permute-start | bytes 786440 | tf_op jit(solution)/shard_map/ppermute | solution.py:197
  47.5 23.8 %collective-permute-start.7 = (bf16[4,128,512]{2,1,0:T(8,128)(2,1)S(1)}, bf16[4,128,512]{2,1,0:T(8,128)(2,1)S(1)}, u32[]{:S(2)}, u32[]{:S(2)}) collective-permute-start(bf16[4,128,512]{2,1,0:T(8,128)(2,1)S(1)} %get-tuple-element.41), channel_id=1, source_target_pairs={{0,48},{16,0},{32,16},{48,32},{1,49},{17,1},{33,17},{49,33},{2,50}... | collective-permute-start | bytes 1572872 | tf_op jit(solution)/shard_map/ppermute | solution.py:197
  52.0 22.0 %collective-permute-start.4 = (bf16[4,128,512]{2,1,0:T(8,128)(2,1)S(1)}, bf16[4,128,512]{2,1,0:T(8,128)(2,1)S(1)}, u32[]{:S(2)}, u32[]{:S(2)}) collective-permute-start(bf16[4,128,512]{2,1,0:T(8,128)(2,1)S(1)} %get-tuple-element.41), channel_id=1, source_target_pairs={{0,16},{16,32},{32,48},{48,0},{1,17},{17,33},{33,49},{49,1},{2,18}... | collective-permute-start | bytes 1572872 | tf_op jit(solution)/shard_map/ppermute | solution.py:197
  76.6 7.5 %collective-permute-start.16 = (bf16[2,4,4,128,512]{4,3,2,1,0:T(8,128)(2,1)}, bf16[2,4,4,128,512]{4,3,2,1,0:T(8,128)(2,1)}, u32[]{:S(2)}, u32[]{:S(2)}) collective-permute-start(bf16[2,4,4,128,512]{4,3,2,1,0:T(8,128)(2,1)} %pad_maximum_fusion.near), channel_id=1, source_target_pairs={{0,8},{8,0},{1,9},{9,1},{2,10},{10,2},{3,11},{11,3},{4,12},{12,4},... | collective-permute-start | bytes 12582920 | tf_op jit(solution)/shard_map/ppermute | solution.py:223
  77.4 6.6 %copy-start = (s32[32,1,18]{2,1,0:T(1,128)}, s32[32,1,18]{2,1,0:T(1,128)S(1)}, u32[]{:S(2)}) copy-start(s32[32,1,18]{2,1,0:T(1,128)S(1)} %slice_convert_fusion) | copy-start | bytes 6916
  124.9 58.4 %all-to-all-start.1 = ((bf16[32,128,512]{2,1,0:T(8,128)(2,1)}), bf16[32,128,512]{2,1,0:T(8,128)(2,1)}, u32[]{:S(2)}, u32[]{:S(2)}) async-start(bf16[32,128,512]{2,1,0:T(8,128)(2,1)} %get-tuple-element.26), calls=%async_computation.1 | async-start | bytes 8388608 | tf_op jit(solution)/shard_map/all_to_all | solution.py:280
  138.6 4.4 %collective-permute-start.17 = (bf16[16,512,128]{2,1,0:T(8,128)(2,1)}, bf16[16,512,128]{2,1,0:T(8,128)(2,1)S(1)}, u32[]{:S(2)}, u32[]{:S(2)}) collective-permute-start(bf16[16,512,128]{2,1,0:T(8,128)(2,1)} %get-tuple-element.29), channel_id=1, source_target_pairs={{0,8},{8,0},{1,9},{9,1},{2,10},{10,2},{3,11},{11,3},{4,12},{12,4},... | collective-permute-start | bytes 6291464 | tf_op jit(solution)/shard_map/ppermute | solution.py:311
  183.2 33.8 %all-to-all-start.2 = ((bf16[16,512,128]{2,1,0:T(8,128)(2,1)}), bf16[16,512,128]{2,1,0:T(8,128)(2,1)S(1)}, u32[]{:S(2)}, u32[]{:S(2)}) async-start(bf16[16,512,128]{2,1,0:T(8,128)(2,1)} %add_convert_fusion), calls=%async_computation.3 | async-start | bytes 4194304 | tf_op jit(solution)/shard_map/all_to_all | solution.py:314
Sparse Core Ops, SparseCore 0:
  11.1 63.6 all-gather.2
  125.0 80.8 reduce-scatter.1
